TPU v7x, 512 devices: a whole 4x4x16 slice. The times are simulated.
512 devices in a mesh: member: 16 (over x, y_lo, core), lon: 32 (over y_hi, z).
Axes of the slice: x: 4, y: 4 (y_hi: 2, y_lo: 2; y = y_hi * 2 + y_lo), z: 16, core: 2. Of those that a mesh axis runs over, the one named last changes fastest.
Arguments:
- ensemble: bfloat16 [32, 3, 512, 2048], P('member', None, 'lon'), may hold values from -6 to 6
- copy_list: int32 [32], replicated, may hold values from 0 to 31, as said below
- depth: float32 [512, 2048], P('lon'), may hold values from 0.25 to 4
- land_mask: int32 [512, 2048], P('lon'), may hold values 0 or 1
- friction: float32 [512, 2048], P('lon'), may hold values from 0.05 to 2
- coriolis: float32 [2048], replicated, may hold values from -1 to 1
- spread: float32 [2048, 2048], P('member'), may hold values from -0.125 to 0.125
- observed: float32 [512, 2048], P('lon'), may hold values from -6 to 6
Outputs:
- new_state: float32 [32, 3, 512, 2048], P('member', None, 'lon')
- misfit: float32 [32], P('member')
Inputs may be any that keep to these rules, and one draw needn't show every extreme that they name: `copy_list`: each entry names a particle of the ensemble; the entries name exactly 8 different particles.
All inputs are finite; a program needn't handle non-finite values. No bound on the sum of `land_mask` on one device may be relied on, other than what follows from the above.
Results may differ from a plain program's by a relative error of at most 0.0013.
Values may be sent and summed in bfloat16 or wider, within the bound.
No kernel may reach another device: no remote copies, remote signals or barrier semaphores. Data moves between devices by JAX's collectives and lax.ppermute only.
A program may use at most 64 MiB of HBM per device.

v0:
```python
import jax
import jax.numpy as jnp
from jax import lax
from jax.sharding import PartitionSpec as P

STEPS = 2


time_step = 0.2
gravity = 1.0
nudge_rate = 0.3


def extended(cells, sides, width):
    for axis, dim in sides:
        count = lax.axis_size(axis)
        head = lax.slice_in_dim(cells, 0, width, axis=dim)
        tail = lax.slice_in_dim(cells, cells.shape[dim] - width, cells.shape[dim], axis=dim)
        cells = jnp.concatenate(
            [
                lax.ppermute(tail, axis, [(i, (i + 1) % count) for i in range(count)]),
                cells,
                lax.ppermute(head, axis, [((i + 1) % count, i) for i in range(count)]),
            ],
            axis=dim,
        )
    return cells


def north_diff(field):
    padded = jnp.pad(field, ((0, 0), (0, 0), (1, 1)))
    return 0.5 * (padded[:, :, 2:] - padded[:, :, :-2])


def east_inner(field):
    return 0.5 * (field[..., 2:, :] - field[..., :-2, :])


def nudged(fresh, observed, wet, spread):
    innovation = observed - fresh
    row_parts = jnp.einsum(
        "jk,pxk->pxj",
        spread,
        lax.all_gather(innovation, "member", axis=0, tiled=True),
        precision=lax.Precision.HIGHEST,
    )
    spreaded = lax.all_to_all(row_parts, "member", split_axis=0, concat_axis=2, tiled=True)
    correction = innovation + spreaded
    return fresh + nudge_rate * wet * correction


def per_device(ensemble, copy_list, depth, land_mask, friction, coriolis, spread, observed):
    part_dev = ensemble.shape[0]
    columns = ensemble.shape[2]
    wanted = lax.dynamic_slice_in_dim(copy_list, lax.axis_index("member") * part_dev, part_dev)
    piece = lax.all_gather(ensemble, "member", axis=0, tiled=True)
    owners = jnp.arange(piece.shape[0], dtype=jnp.int32)
    select = (wanted[:, None] == owners[None, :]).astype(jnp.bfloat16)
    picked = jnp.einsum("kn,nfxy->kfxy", select, piece, preferred_element_type=jnp.float32)
    wet = jnp.where(land_mask == 1, 1.0, 0.0).astype(jnp.float32)
    damping = 1.0 / (1.0 + time_step * friction)
    turning = coriolis[None, None, :]
    height, zonal, meridional = (picked[:, 0], picked[:, 1], picked[:, 2])
    for step in range(STEPS):
        flux_east = depth * zonal
        widened = extended(flux_east.astype(jnp.bfloat16), (("lon", 1),), 1).astype(flux_east.dtype)
        divergence = east_inner(widened) + north_diff(depth * meridional)
        fresh = height - time_step * wet * divergence
        fresh_wide = extended(fresh.astype(jnp.bfloat16), (("lon", 1),), 1).astype(fresh.dtype)
        east_slope = east_inner(fresh_wide)
        north_slope = north_diff(fresh)
        zonal_next = (
            wet * (zonal + time_step * (turning * meridional - gravity * east_slope)) * damping
        )
        meridional_next = (
            wet * (meridional - time_step * (turning * zonal + gravity * north_slope)) * damping
        )
        height = nudged(fresh, observed, wet, spread)
        zonal, meridional = (zonal_next, meridional_next)
    new_state = jnp.stack([height, zonal, meridional], axis=1)
    column = (lax.axis_index("lon") * columns + jnp.arange(columns, dtype=jnp.int32)).astype(
        jnp.float32
    )
    total_columns = columns * lax.axis_size("lon")
    weight = 1.0 + 2.0 * column / total_columns
    local_misfit = jnp.sum(
        wet[None] * weight[None, :, None] * (observed[None] - height) ** 2, axis=(1, 2)
    )
    misfit = lax.psum(local_misfit, "lon") / (height.shape[2] * total_columns)
    return (new_state, misfit)


def solution(mesh):
    placed = (
        P("member", None, "lon", None),
        P(),
        P("lon", None),
        P("lon", None),
        P("lon", None),
        P(),
        P("member", None),
        P("lon", None),
    )
    return jax.shard_map(
        per_device,
        mesh=mesh,
        in_specs=placed,
        out_specs=(P("member", None, "lon", None), P("member")),
        check_vma=False,
    )
```

profile of v0, /device:TPU:2, one launch (start us, length us, event | category | flops | bytes accessed | tf_op | source)
XLA Modules:
  0.0 313.6 jit_solution(9015908406566308131)
XLA Ops:
  8.7 55.8 %all-gather.4.cloned.1.call-done = bf16[32,3,16,2048]{3,2,1,0:T(8,128)(2,1)} async-done(((bf16[2,3,16,2048]{3,2,1,0:T(8,128)(2,1)}), bf16[32,3,16,2048]{3,2,1,0:T(8,128)(2,1)}) %all-gather.4.cloned.1.call-update) | async-done | bytes 6291472 | tf_op jit(solution)/shard_map/all_gather | solution.py:56
  64.5 9.6 %fusion = f32[2,3,16,2048]{3,0,2,1:T(2,128)S(1)} fusion(bf16[32,3,16,2048]{3,2,1,0:T(8,128)(2,1)} %all-gather.4.cloned.1.call-done, s32[2]{0:T(128)S(1)} %dynamic_slice.3), kind=kOutput, calls=%fused_computation | convolution fusion | flops 12582976 | bytes 7077896 | tf_op jit(solution)/shard_map/kn,nfxy->kfxy/dot_general | solution.py:59
  74.4 3.5 %collective-permute-start = (bf16[2,1,2048]{2,0,1:T(2,128)(2,1)S(1)}, bf16[2,1,2048]{2,0,1:T(2,128)(2,1)S(1)}, u32[]{:S(2)}, u32[]{:S(2)}) collective-permute-start(bf16[2,1,2048]{2,0,1:T(2,128)(2,1)S(1)} %get-tuple-element.34), channel_id=1, source_target_pairs={{0,1},{1,2},{2,3},{3,4},{4,5},{5,6},{6,7},{7,8},{8,9},{9,10},{10,1... | collective-permute-start | bytes 24584 | tf_op jit(solution)/shard_map/ppermute | solution.py:21
  77.8 6.9 %collective-permute-start.1 = (bf16[2,1,2048]{2,0,1:T(2,128)(2,1)S(1)}, bf16[2,1,2048]{2,0,1:T(2,128)(2,1)S(1)}, u32[]{:S(2)}, u32[]{:S(2)}) collective-permute-start(bf16[2,1,2048]{2,0,1:T(2,128)(2,1)S(1)} %get-tuple-element.35), channel_id=1, source_target_pairs={{1,0},{2,1},{3,2},{4,3},{5,4},{6,5},{7,6},{8,7},{9,8},{10,9},{11,1... | collective-permute-start | bytes 24584 | tf_op jit(solution)/shard_map/ppermute | solution.py:23
  87.9 1.9 collective-permute-start.2
  89.8 8.0 %collective-permute-start.3 = (bf16[2,1,2048]{2,0,1:T(2,128)(2,1)S(1)}, bf16[2,1,2048]{2,0,1:T(2,128)(2,1)S(1)}, u32[]{:S(2)}, u32[]{:S(2)}) collective-permute-start(bf16[2,1,2048]{2,0,1:T(2,128)(2,1)S(1)} %get-tuple-element.33), channel_id=1, source_target_pairs={{1,0},{2,1},{3,2},{4,3},{5,4},{6,5},{7,6},{8,7},{9,8},{10,9},{11,1... | collective-permute-start | bytes 24584 | tf_op jit(solution)/shard_map/ppermute | solution.py:23
  99.2 2.4 multiply_convert_fusion
  101.6 29.8 %all-gather.6.cloned.1.call-done = f32[32,16,2048]{2,1,0:T(8,128)} async-done(((f32[2,16,2048]{2,1,0:T(8,128)}), f32[32,16,2048]{2,1,0:T(8,128)}) %all-gather.6.cloned.1.call-update) | async-done | bytes 4194320 | tf_op jit(solution)/shard_map/all_gather | solution.py:44
  131.4 6.3 %fusion.4 = f32[32,16,128]{2,1,0:T(8,128)} fusion(f32[32,16,2048]{2,1,0:T(8,128)} %all-gather.6.cloned.1.call-done, f32[128,2048]{1,0:T(8,128)S(1)} %copy-done), kind=kOutput, calls=%fused_computation.4 | convolution fusion | flops 1610612736 | bytes 5505024 | tf_op jit(solution)/shard_map/jk,pxk->pxj/dot_general | solution.py:41
  137.7 4.8 %all-to-all-start = ((f32[32,16,128]{2,1,0:T(8,128)}), f32[32,16,128]{2,1,0:T(8,128)S(1)}, u32[]{:S(2)}, u32[]{:S(2)}) async-start(f32[32,16,128]{2,1,0:T(8,128)} %fusion.4), calls=%async_computation | async-start | bytes 524288 | tf_op jit(solution)/shard_map/all_to_all | solution.py:47
  142.5 3.4 %collective-permute-start.4 = (bf16[2,1,2048]{2,0,1:T(2,128)(2,1)S(1)}, bf16[2,1,2048]{2,0,1:T(2,128)(2,1)S(1)}, u32[]{:S(2)}, u32[]{:S(2)}) collective-permute-start(bf16[2,1,2048]{2,0,1:T(2,128)(2,1)S(1)} %get-tuple-element.30), channel_id=1, source_target_pairs={{0,1},{1,2},{2,3},{3,4},{4,5},{5,6},{6,7},{7,8},{8,9},{9,10},{10,1... | collective-permute-start | bytes 24584 | tf_op jit(solution)/shard_map/ppermute | solution.py:21
  146.0 6.4 %collective-permute-start.5 = (bf16[2,1,2048]{2,0,1:T(2,128)(2,1)S(1)}, bf16[2,1,2048]{2,0,1:T(2,128)(2,1)S(1)}, u32[]{:S(2)}, u32[]{:S(2)}) collective-permute-start(bf16[2,1,2048]{2,0,1:T(2,128)(2,1)S(1)} %get-tuple-element.31), channel_id=1, source_target_pairs={{1,0},{2,1},{3,2},{4,3},{5,4},{6,5},{7,6},{8,7},{9,8},{10,9},{11,1... | collective-permute-start | bytes 24584 | tf_op jit(solution)/shard_map/ppermute | solution.py:23
  152.4 1.3 collective-permute-done.5
  154.8 1.8 all_to_all.29
  156.6 1.6 broadcast_subtract_fusion
  159.1 43.8 %all-gather.8.cloned.1.call-done = f32[32,16,2048]{2,1,0:T(8,128)} async-done(((f32[2,16,2048]{2,1,0:T(8,128)}), f32[32,16,2048]{2,1,0:T(8,128)}) %all-gather.8.cloned.1.call-update) | async-done | bytes 4194320 | tf_op jit(solution)/shard_map/all_gather | solution.py:44
  202.9 6.3 %fusion.2 = f32[32,16,128]{2,1,0:T(8,128)} fusion(f32[32,16,2048]{2,1,0:T(8,128)} %all-gather.8.cloned.1.call-done, f32[128,2048]{1,0:T(8,128)S(1)} %copy-done), kind=kOutput, calls=%fused_computation.2 | convolution fusion | flops 1610612736 | bytes 5505024 | tf_op jit(solution)/shard_map/jk,pxk->pxj/dot_general | solution.py:41
  209.2 4.8 %all-to-all-start.1 = ((f32[32,16,128]{2,1,0:T(8,128)}), f32[32,16,128]{2,1,0:T(8,128)S(1)}, u32[]{:S(2)}, u32[]{:S(2)}) async-start(f32[32,16,128]{2,1,0:T(8,128)} %fusion.2), calls=%async_computation.1 | async-start | bytes 524288 | tf_op jit(solution)/shard_map/all_to_all | solution.py:47
  214.0 3.5 %collective-permute-start.6 = (bf16[2,1,2048]{2,0,1:T(2,128)(2,1)S(1)}, bf16[2,1,2048]{2,0,1:T(2,128)(2,1)S(1)}, u32[]{:S(2)}, u32[]{:S(2)}) collective-permute-start(bf16[2,1,2048]{2,0,1:T(2,128)(2,1)S(1)} %get-tuple-element.28), channel_id=1, source_target_pairs={{0,1},{1,2},{2,3},{3,4},{4,5},{5,6},{6,7},{7,8},{8,9},{9,10},{10,1... | collective-permute-start | bytes 24584 | tf_op jit(solution)/shard_map/ppermute | solution.py:21
  217.5 6.6 %collective-permute-start.7 = (bf16[2,1,2048]{2,0,1:T(2,128)(2,1)S(1)}, bf16[2,1,2048]{2,0,1:T(2,128)(2,1)S(1)}, u32[]{:S(2)}, u32[]{:S(2)}) collective-permute-start(bf16[2,1,2048]{2,0,1:T(2,128)(2,1)S(1)} %get-tuple-element.29), channel_id=1, source_target_pairs={{1,0},{2,1},{3,2},{4,3},{5,4},{6,5},{7,6},{8,7},{9,8},{10,9},{11,1... | collective-permute-start | bytes 24584 | tf_op jit(solution)/shard_map/ppermute | solution.py:23
  224.1 1.1 collective-permute-done.7
  225.8 1.1 multiply_bitcast_fusion.1
  227.3 1.3 copy.21
  228.7 77.8 %psum.7 = f32[2]{0:T(128)S(1)} all-reduce(f32[2]{0:T(128)S(1)} %get-tuple-element.23), channel_id=1, replica_groups=mesh['member'=16,'lon'=32] {'lon'}, use_global_device_ids=true, to_apply=%region_1.2 | all-reduce | flops 2 | bytes 16 | tf_op jit(solution)/shard_map/psum | solution.py:89
  (53 shorter events, 9.7 us)
Async XLA Ops:
  7.2 124.2 %copy-start = (f32[128,2048]{1,0:T(8,128)S(1)}, f32[128,2048]{1,0:T(8,128)}, u32[]{:S(2)}) copy-start(f32[128,2048]{1,0:T(8,128)} %param.14) | copy-start | bytes 3145732
  7.2 66.9 %copy-start.4 = (f32[16,2048]{1,0:T(8,128)S(1)}, f32[16,2048]{1,0:T(8,128)}, u32[]{:S(2)}) copy-start(f32[16,2048]{1,0:T(8,128)} %param.10) | copy-start | bytes 393220
  7.2 77.5 %copy-start.6 = (s32[16,2048]{1,0:T(8,128)S(1)}, s32[16,2048]{1,0:T(8,128)}, u32[]{:S(2)}) copy-start(s32[16,2048]{1,0:T(8,128)} %param.11) | copy-start | bytes 393220
  7.2 57.3 %all-gather.4.cloned.1.call-start = ((), (), s32[]{:S(2)}) async-start(), calls=%async_computation.2 | async-start | bytes 6684672 | tf_op jit(solution)/shard_map/all_gather | solution.py:56
  7.9 123.4 %all-gather.6.cloned.1.call-start = ((), (), s32[]{:S(2)}) async-start(), calls=%async_computation.3 | async-start | bytes 4456448 | tf_op jit(solution)/shard_map/all_gather | solution.py:44
  8.7 77.5 %copy-start.1 = (f32[16,2048]{1,0:T(8,128)S(1)}, f32[16,2048]{1,0:T(8,128)}, u32[]{:S(2)}) copy-start(f32[16,2048]{1,0:T(8,128)} %param.15) | copy-start | bytes 393220
  74.1 23.7 %copy-start.5 = (f32[16,2048]{1,0:T(8,128)S(1)}, f32[16,2048]{1,0:T(8,128)}, u32[]{:S(2)}) copy-start(f32[16,2048]{1,0:T(8,128)} %param.12) | copy-start | bytes 393220
  74.1 25.1 %copy-start.7 = (f32[2048]{0:T(1024)S(1)}, f32[2048]{0:T(1024)}, u32[]{:S(2)}) copy-start(f32[2048]{0:T(1024)} %param.13) | copy-start | bytes 24580
  74.4 11.1 %collective-permute-start = (bf16[2,1,2048]{2,0,1:T(2,128)(2,1)S(1)}, bf16[2,1,2048]{2,0,1:T(2,128)(2,1)S(1)}, u32[]{:S(2)}, u32[]{:S(2)}) collective-permute-start(bf16[2,1,2048]{2,0,1:T(2,128)(2,1)S(1)} %get-tuple-element.34), channel_id=1, source_target_pairs={{0,1},{1,2},{2,3},{3,4},{4,5},{5,6},{6,7},{7,8},{8,9},{9,10},{10,1... | collective-permute-start | bytes 24584 | tf_op jit(solution)/shard_map/ppermute | solution.py:21
  77.8 8.2 %collective-permute-start.1 = (bf16[2,1,2048]{2,0,1:T(2,128)(2,1)S(1)}, bf16[2,1,2048]{2,0,1:T(2,128)(2,1)S(1)}, u32[]{:S(2)}, u32[]{:S(2)}) collective-permute-start(bf16[2,1,2048]{2,0,1:T(2,128)(2,1)S(1)} %get-tuple-element.35), channel_id=1, source_target_pairs={{1,0},{2,1},{3,2},{4,3},{5,4},{6,5},{7,6},{8,7},{9,8},{10,9},{11,1... | collective-permute-start | bytes 24584 | tf_op jit(solution)/shard_map/ppermute | solution.py:23
  87.9 10.0 %collective-permute-start.2 = (bf16[2,1,2048]{2,0,1:T(2,128)(2,1)S(1)}, bf16[2,1,2048]{2,0,1:T(2,128)(2,1)S(1)}, u32[]{:S(2)}, u32[]{:S(2)}) collective-permute-start(bf16[2,1,2048]{2,0,1:T(2,128)(2,1)S(1)} %get-tuple-element.32), channel_id=1, source_target_pairs={{0,1},{1,2},{2,3},{3,4},{4,5},{5,6},{6,7},{7,8},{8,9},{9,10},{10,1... | collective-permute-start | bytes 24584 | tf_op jit(solution)/shard_map/ppermute | solution.py:21
  89.8 9.2 %collective-permute-start.3 = (bf16[2,1,2048]{2,0,1:T(2,128)(2,1)S(1)}, bf16[2,1,2048]{2,0,1:T(2,128)(2,1)S(1)}, u32[]{:S(2)}, u32[]{:S(2)}) collective-permute-start(bf16[2,1,2048]{2,0,1:T(2,128)(2,1)S(1)} %get-tuple-element.33), channel_id=1, source_target_pairs={{1,0},{2,1},{3,2},{4,3},{5,4},{6,5},{7,6},{8,7},{9,8},{10,9},{11,1... | collective-permute-start | bytes 24584 | tf_op jit(solution)/shard_map/ppermute | solution.py:23
  101.6 40.9 %copy-start.2 = (bf16[2,16,2048]{2,0,1:T(2,128)(2,1)S(1)}, bf16[2,16,2048]{2,0,1:T(2,128)(2,1)}, u32[]{:S(2)}) copy-start(bf16[2,16,2048]{2,0,1:T(2,128)(2,1)} %get-tuple-element.12) | copy-start | bytes 393220
  137.7 16.3 %all-to-all-start = ((f32[32,16,128]{2,1,0:T(8,128)}), f32[32,16,128]{2,1,0:T(8,128)S(1)}, u32[]{:S(2)}, u32[]{:S(2)}) async-start(f32[32,16,128]{2,1,0:T(8,128)} %fusion.4), calls=%async_computation | async-start | bytes 524288 | tf_op jit(solution)/shard_map/all_to_all | solution.py:47
  142.4 60.4 %all-gather.8.cloned.1.call-start = ((), (), s32[]{:S(2)}) async-start(), calls=%async_computation.4 | async-start | bytes 4456448 | tf_op jit(solution)/shard_map/all_gather | solution.py:44
  142.5 9.9 %collective-permute-start.4 = (bf16[2,1,2048]{2,0,1:T(2,128)(2,1)S(1)}, bf16[2,1,2048]{2,0,1:T(2,128)(2,1)S(1)}, u32[]{:S(2)}, u32[]{:S(2)}) collective-permute-start(bf16[2,1,2048]{2,0,1:T(2,128)(2,1)S(1)} %get-tuple-element.30), channel_id=1, source_target_pairs={{0,1},{1,2},{2,3},{3,4},{4,5},{5,6},{6,7},{7,8},{8,9},{9,10},{10,1... | collective-permute-start | bytes 24584 | tf_op jit(solution)/shard_map/ppermute | solution.py:21
  146.0 7.8 %collective-permute-start.5 = (bf16[2,1,2048]{2,0,1:T(2,128)(2,1)S(1)}, bf16[2,1,2048]{2,0,1:T(2,128)(2,1)S(1)}, u32[]{:S(2)}, u32[]{:S(2)}) collective-permute-start(bf16[2,1,2048]{2,0,1:T(2,128)(2,1)S(1)} %get-tuple-element.31), channel_id=1, source_target_pairs={{1,0},{2,1},{3,2},{4,3},{5,4},{6,5},{7,6},{8,7},{9,8},{10,9},{11,1... | collective-permute-start | bytes 24584 | tf_op jit(solution)/shard_map/ppermute | solution.py:23
  159.0 66.8 %copy-start.3 = (f32[16,2048]{1,0:T(8,128)S(1)}, f32[16,2048]{1,0:T(8,128)}, u32[]{:S(2)}) copy-start(f32[16,2048]{1,0:T(8,128)} %get-tuple-element.24) | copy-start | bytes 393220
  209.2 16.2 %all-to-all-start.1 = ((f32[32,16,128]{2,1,0:T(8,128)}), f32[32,16,128]{2,1,0:T(8,128)S(1)}, u32[]{:S(2)}, u32[]{:S(2)}) async-start(f32[32,16,128]{2,1,0:T(8,128)} %fusion.2), calls=%async_computation.1 | async-start | bytes 524288 | tf_op jit(solution)/shard_map/all_to_all | solution.py:47
  214.0 10.1 %collective-permute-start.6 = (bf16[2,1,2048]{2,0,1:T(2,128)(2,1)S(1)}, bf16[2,1,2048]{2,0,1:T(2,128)(2,1)S(1)}, u32[]{:S(2)}, u32[]{:S(2)}) collective-permute-start(bf16[2,1,2048]{2,0,1:T(2,128)(2,1)S(1)} %get-tuple-element.28), channel_id=1, source_target_pairs={{0,1},{1,2},{2,3},{3,4},{4,5},{5,6},{6,7},{7,8},{8,9},{9,10},{10,1... | collective-permute-start | bytes 24584 | tf_op jit(solution)/shard_map/ppermute | solution.py:21
  217.5 7.7 %collective-permute-start.7 = (bf16[2,1,2048]{2,0,1:T(2,128)(2,1)S(1)}, bf16[2,1,2048]{2,0,1:T(2,128)(2,1)S(1)}, u32[]{:S(2)}, u32[]{:S(2)}) collective-permute-start(bf16[2,1,2048]{2,0,1:T(2,128)(2,1)S(1)} %get-tuple-element.29), channel_id=1, source_target_pairs={{1,0},{2,1},{3,2},{4,3},{5,4},{6,5},{7,6},{8,7},{9,8},{10,9},{11,1... | collective-permute-start | bytes 24584 | tf_op jit(solution)/shard_map/ppermute | solution.py:23
Sparse Core Ops, SparseCore 0:
  10.2 54.2 all-gather.3
  87.9 43.4 all-gather.5
  159.1 43.6 all-gather.7
where the time goes:
time: 314 us
  waiting for transfers between devices  134 us (43%)
  blocking collectives  77.8 us (25%)
  starting transfers between devices  49.9 us (16%)
  matrix products  22.2 us (7%)
  between operations  14 us (4%)
  other arithmetic  8.59 us (3%)
  local copies, waits for them, and re-layouts  6.81 us (2%)
    psum x1, blocking collectives, per_device(): misfit = lax.psum(local_misfit, 'lon') / (height.shape[2] * total_columns)  77.8 us
    all_gather x2, waiting for transfers between devices, nudged(): lax.all_gather(innovation, 'member', axis=0, tiled=True)  73.5 us
    all_gather x1, waiting for transfers between devices, per_device(): piece = lax.all_gather(ensemble, 'member', axis=0, tiled=True)  55.8 us
    ppermute x4, starting transfers between devices, extended(): lax.ppermute(head, axis, [((i + 1) % count, i) for i in range(count)])  27.9 us
    dot_general x2, matrix products, nudged(): jnp.einsum('jk,pxk->pxj', spread, lax.all_gather(innovation, 'member', ax...  12.6 us
    ppermute x4, starting transfers between devices, extended(): lax.ppermute(tail, axis, [(i, (i + 1) % count) for i in range(count)])  12.3 us
    dot_general x1, matrix products, per_device(): jnp.einsum('kn,nfxy->kfxy', select, piece, preferred_element_type=jnp.flo...  9.59 us
    all_to_all x2, starting transfers between devices, nudged(): lax.all_to_all(row_parts, 'member', split_axis=0, concat_axis=2, tiled=True)  9.58 us
  transfers between devices with their start and end apart: 13, of which 7 were waited for; matrix products, arithmetic and copies ran while one was open for 1% of the time, Pallas kernels for 0%

commit v1 on v0

v1 whole, which is shorter than its diff:
```python
import functools

import jax
import jax.numpy as jnp
from jax import lax
from jax.experimental import pallas as pl
from jax.experimental.pallas import tpu as pltpu
from jax.sharding import PartitionSpec as P

DISTINCT = 8
HALO = 3
LANES = 128
time_step = 0.2
nudge_rate = 0.3
f32 = jnp.float32
bf16 = jnp.bfloat16

VMEM = pl.BlockSpec(memory_space=pltpu.VMEM)
SMEM = pl.BlockSpec(memory_space=pltpu.SMEM)


def call(kernel, out_shape, in_specs, out_specs, scratch=(), flops=1e6, bytes_accessed=1e6):
    return pl.pallas_call(
        kernel,
        out_shape=out_shape,
        in_specs=in_specs,
        out_specs=out_specs,
        scratch_shapes=list(scratch),
        compiler_params=pltpu.CompilerParams(vmem_limit_bytes=24 * 1024 * 1024),
        cost_estimate=pl.CostEstimate(
            flops=int(flops), bytes_accessed=int(bytes_accessed), transcendentals=0
        ),
    )


def pieces(x):
    first = x.astype(bf16).astype(f32)
    rest = x - first
    second = rest.astype(bf16).astype(f32)
    return first, second, rest - second


def pack_kernel(copy_ref, ens_ref, depth_ref, mask_ref, fric_ref, head_ref, tail_ref, idx_ref, rows, seen):
    columns = depth_ref.shape[0]
    for p in range(32):
        seen[p] = 0
    for s in range(32):
        seen[copy_ref[s]] = 1
    for i in range(DISTINCT):
        idx_ref[i] = 0
    count = jnp.int32(0)
    for p in range(32):
        used = seen[p]
        place = jnp.minimum(count, DISTINCT - 1)
        idx_ref[place] = jnp.where(used == 1, p, idx_ref[place])
        seen[p] = place
        count = count + used
    for s in range(32):
        idx_ref[DISTINCT + s] = seen[copy_ref[s]]

    depth3 = pieces(depth_ref[...])
    fric3 = pieces(fric_ref[...])
    wet = jnp.where(mask_ref[...] == 1, 1.0, 0.0).astype(f32)
    for out, lo, near2, near1 in (
        (head_ref, 0, 0, 0),
        (tail_ref, columns - HALO, columns - 2, columns - 1),
    ):
        for p in range(2):
            for f in range(3):
                at = (p * 3 + f) * HALO
                rows[at : at + HALO, :] = ens_ref[p, f].astype(f32)[lo : lo + HALO, :]
        for k in range(3):
            rows[18 + 3 * k : 21 + 3 * k, :] = depth3[k][lo : lo + HALO, :]
            rows[29 + k : 30 + k, :] = fric3[k][near1 : near1 + 1, :]
        rows[27:29, :] = wet[near2 : near2 + 2, :]
        out[...] = rows[...].astype(bf16)


def east(x):
    return 0.5 * (pltpu.roll(x, x.shape[0] - 1, 0) - pltpu.roll(x, 1, 0))


def north(x):
    n = x.shape[1]
    lane = lax.broadcasted_iota(jnp.int32, x.shape, 1)
    up = jnp.where(lane == n - 1, 0.0, pltpu.roll(x, n - 1, 1))
    down = jnp.where(lane == 0, 0.0, pltpu.roll(x, 1, 1))
    return 0.5 * (up - down)


def source_kernel(
    ens_ref, left_ref, right_ref, depth_ref, mask_ref, fric_ref, cor_ref, obs_ref,
    innov_ref, rest_ref, ext, lrows, rrows, sdepth, swet, sfric,
):
    columns, lat = depth_ref.shape
    blocks = lat // LANES
    lo, hi = 8, 8 + columns
    lrows[...] = left_ref[...].astype(f32)
    rrows[...] = right_ref[...].astype(f32)

    def three(rows, at, n, step):
        a, b, c = (rows[at + step * k : at + step * k + n, :] for k in range(3))
        return (a + b) + c

    for ref in (sdepth, swet, sfric):
        ref[0:8, :] = jnp.zeros((8, lat), f32)
        ref[hi : hi + 8, :] = jnp.zeros((8, lat), f32)
    sdepth[lo:hi, :] = depth_ref[...]
    sdepth[lo - 3 : lo, :] = three(lrows, 18, 3, 3)
    sdepth[hi : hi + 3, :] = three(rrows, 18, 3, 3)
    swet[lo:hi, :] = jnp.where(mask_ref[...] == 1, 1.0, 0.0).astype(f32)
    swet[lo - 2 : lo, :] = lrows[27:29, :]
    swet[hi : hi + 2, :] = rrows[27:29, :]
    sfric[lo:hi, :] = fric_ref[...]
    sfric[lo - 1 : lo, :] = three(lrows, 29, 1, 1)
    sfric[hi : hi + 1, :] = three(rrows, 29, 1, 1)
    depth = sdepth[...]
    wet = swet[...]
    damped = wet * (1.0 / (1.0 + time_step * sfric[...]))
    turning = cor_ref[...]

    for p in range(2):
        fields = []
        for f in range(3):
            at = (p * 3 + f) * HALO
            ext[f, 0:8, :] = jnp.zeros((8, lat), f32)
            ext[f, hi : hi + 8, :] = jnp.zeros((8, lat), f32)
            ext[f, lo:hi, :] = ens_ref[p, f].astype(f32)
            ext[f, lo - HALO : lo, :] = lrows[at : at + HALO, :]
            ext[f, hi : hi + HALO, :] = rrows[at : at + HALO, :]
            fields.append(ext[f])
        height, zonal, meridional = fields
        fresh = height - time_step * wet * (east(depth * zonal) + north(depth * meridional))
        innov = obs_ref[...] - fresh[lo:hi, :]
        for b in range(blocks):
            innov_ref[b, p] = innov[:, b * LANES : (b + 1) * LANES]
        zonal1 = damped * (zonal + time_step * (turning * meridional - east(fresh)))
        meridional1 = damped * (meridional - time_step * (turning * zonal + north(fresh)))
        change = -time_step * wet * (east(depth * zonal1) + north(depth * meridional1))
        zonal_part = damped * (zonal1 + time_step * (turning * meridional1))
        meridional_part = damped * (meridional1 - time_step * (turning * zonal1))
        for k, value in enumerate((change, zonal_part, meridional_part)):
            for b in range(blocks):
                rest_ref[b, p, k] = value[lo:hi, b * LANES : (b + 1) * LANES]


def split_kernel(spread_ref, out_ref):
    s = spread_ref[...]
    high = s.astype(bf16)
    out_ref[0] = high
    out_ref[1] = (s - high.astype(f32)).astype(bf16)


def select_kernel(idx_ref, all_ref, mine_ref, copies_ref):
    columns = all_ref.shape[1]
    for i in range(DISTINCT):
        v = all_ref[idx_ref[i]]
        mine_ref[i] = v
        b = v.astype(bf16)
        for d in range(copies_ref.shape[0]):
            copies_ref[d, i * columns : (i + 1) * columns, :] = b


def spread_dot(gathered_ref, spread_ref):
    blocks = gathered_ref.shape[0]
    lhs = jnp.concatenate([gathered_ref[b] for b in range(blocks)], axis=1)
    dims = (((1,), (1,)), ((), ()))
    return lax.dot_general(
        lhs, spread_ref[0], dims, preferred_element_type=f32
    ) + lax.dot_general(lhs, spread_ref[1], dims, preferred_element_type=f32)


def block_of(ref, b):
    return ref[:, pl.ds(pl.multiple_of(b * LANES, LANES), LANES)]


def wet_block(mask_ref, b):
    return jnp.where(block_of(mask_ref, b) == 1, 1.0, 0.0).astype(f32)


def update_kernel(
    idx_ref, gathered_ref, spread_ref, mine_ref, rest_ref, mask_ref, obs_ref,
    innov_ref, copies_ref, edge_ref,
):
    columns = mask_ref.shape[0]
    me = lax.axis_index("member")
    wet = wet_block(mask_ref, me)
    obs = block_of(obs_ref, me)
    spreaded = spread_dot(gathered_ref, spread_ref)
    for i in range(DISTINCT):
        innov = mine_ref[i]
        sp = spreaded[i * columns : (i + 1) * columns, :]
        new = innov - nudge_rate * wet * (innov + sp) - rest_ref[idx_ref[i], 0]
        innov_ref[i] = new
        b = new.astype(bf16)
        for d in range(copies_ref.shape[0]):
            copies_ref[d, i * columns : (i + 1) * columns, :] = b
        fresh = obs - new
        edge_ref[0, i : i + 1, :] = fresh[0:1, :]
        edge_ref[1, i : i + 1, :] = fresh[columns - 1 : columns, :]


def height_kernel(
    idx_ref, gathered_ref, spread_ref, innov_ref, mask_ref, obs_ref, out_ref, height
):
    columns = mask_ref.shape[0]
    me = lax.axis_index("member")
    wet = wet_block(mask_ref, me)
    obs = block_of(obs_ref, me)
    spreaded = spread_dot(gathered_ref, spread_ref)
    for i in range(DISTINCT):
        innov = innov_ref[i]
        sp = spreaded[i * columns : (i + 1) * columns, :]
        height[i] = (obs - innov) + nudge_rate * wet * (innov + sp)
    for s in range(32):
        out_ref[s // 2, s % 2] = height[idx_ref[DISTINCT + s]]


def velocity_kernel(
    idx_ref, gathered_ref, innov_ref, left_ref, right_ref, rest_ref, mask_ref, fric_ref, obs_ref,
    out_ref, zonal, meridional,
):
    columns = mask_ref.shape[0]
    blocks = gathered_ref.shape[0]
    me = lax.axis_index("member")
    wet = wet_block(mask_ref, me)
    obs = block_of(obs_ref, me)
    damped = wet * (1.0 / (1.0 + time_step * block_of(fric_ref, me)))
    before = jnp.maximum(me - 1, 0)
    after = jnp.minimum(me + 1, blocks - 1)
    obs_before = block_of(obs_ref, before)
    obs_after = block_of(obs_ref, after)
    has_before = jnp.where(me > 0, 1.0, 0.0).astype(f32)
    has_after = jnp.where(me < blocks - 1, 1.0, 0.0).astype(f32)
    lane = lax.broadcasted_iota(jnp.int32, (columns, LANES), 1)
    row = lax.broadcasted_iota(jnp.int32, (columns, LANES), 0)
    for i in range(DISTINCT):
        fresh = obs - innov_ref[i]
        part = slice(i * columns, (i + 1) * columns)
        fresh_before = has_before * (obs_before - gathered_ref[before, part, :].astype(f32))
        fresh_after = has_after * (obs_after - gathered_ref[after, part, :].astype(f32))
        down = jnp.where(lane == 0, pltpu.roll(fresh_before, 1, 1), pltpu.roll(fresh, 1, 1))
        up = jnp.where(
            lane == LANES - 1,
            pltpu.roll(fresh_after, LANES - 1, 1),
            pltpu.roll(fresh, LANES - 1, 1),
        )
        west = jnp.where(row == 0, left_ref[i : i + 1, :], pltpu.roll(fresh, 1, 0))
        easterly = jnp.where(
            row == columns - 1, right_ref[i : i + 1, :], pltpu.roll(fresh, columns - 1, 0)
        )
        src = idx_ref[i]
        zonal[i] = rest_ref[src, 1] - damped * (time_step * 0.5 * (easterly - west))
        meridional[i] = rest_ref[src, 2] - damped * (time_step * 0.5 * (up - down))
    for s in range(32):
        place = idx_ref[DISTINCT + s]
        out_ref[s // 2, s % 2, 0] = zonal[place]
        out_ref[s // 2, s % 2, 1] = meridional[place]


def misfit_kernel(h_ref, mask_ref, obs_ref, out_ref, *, total):
    columns, lat = mask_ref.shape
    blocks = lat // LANES
    first = (lax.axis_index("lon") * columns).astype(f32)
    column = first + lax.broadcasted_iota(jnp.int32, (columns, LANES), 0).astype(f32)
    weight = 1.0 + 2.0 * column / total
    lane = lax.broadcasted_iota(jnp.int32, (1, LANES), 1)
    sums = jnp.zeros((1, LANES), f32)
    for p in range(2):
        acc = jnp.zeros((columns, LANES), f32)
        for b in range(blocks):
            part = slice(b * LANES, (b + 1) * LANES)
            wet = jnp.where(mask_ref[:, part] == 1, 1.0, 0.0).astype(f32)
            gap = obs_ref[:, part] - h_ref[b, p]
            acc = acc + wet * (gap * gap)
        sums = jnp.where(lane == p, jnp.sum(acc * weight), sums)
    for d in range(out_ref.shape[0]):
        out_ref[d] = sums


def output_kernel(h_ref, zm_ref, out_ref):
    blocks = h_ref.shape[0]
    for p in range(2):
        for b in range(blocks):
            part = slice(b * LANES, (b + 1) * LANES)
            out_ref[p, 0, :, part] = h_ref[b, p]
            out_ref[p, 1, :, part] = zm_ref[b, p, 0]
            out_ref[p, 2, :, part] = zm_ref[b, p, 1]


def per_device(ensemble, copy_list, depth, land_mask, friction, coriolis, spread, observed):
    columns, lat = depth.shape
    members = lax.axis_size("member")
    lons = lax.axis_size("lon")
    blocks = lat // LANES
    rows = DISTINCT * columns
    shape = jax.ShapeDtypeStruct
    eastward = [(i, (i + 1) % lons) for i in range(lons)]
    westward = [((i + 1) % lons, i) for i in range(lons)]

    def swap(x):
        return lax.all_to_all(x, "member", 0, 0, tiled=True)

    head, tail, idx = call(
        pack_kernel,
        (shape((32, lat), bf16), shape((32, lat), bf16), shape((64,), jnp.int32)),
        [SMEM, VMEM, VMEM, VMEM, VMEM],
        (VMEM, VMEM, SMEM),
        [pltpu.VMEM((32, lat), f32), pltpu.SMEM((32,), jnp.int32)],
    )(copy_list, ensemble, depth, land_mask, friction)
    left = lax.ppermute(tail, "lon", eastward)
    right = lax.ppermute(head, "lon", westward)
    parts = call(
        split_kernel, shape((2,) + spread.shape, bf16), [VMEM], VMEM
    )(spread)

    ext_rows = columns + 16
    innov1, rest = call(
        source_kernel,
        (
            shape((blocks, 2, columns, LANES), f32),
            shape((blocks, 2, 3, columns, LANES), f32),
        ),
        [VMEM] * 8,
        (VMEM, VMEM),
        [pltpu.VMEM((3, ext_rows, lat), f32)]
        + [pltpu.VMEM((32, lat), f32)] * 2
        + [pltpu.VMEM((ext_rows, lat), f32)] * 3,
    )(ensemble, left, right, depth, land_mask, friction, coriolis[None, :], observed)

    innov1 = swap(innov1).reshape(2 * members, columns, LANES)
    rest = swap(rest).reshape(2 * members, 3, columns, LANES)
    mine, copies = call(
        select_kernel,
        (shape((DISTINCT, columns, LANES), f32), shape((members, rows, LANES), bf16)),
        [SMEM, VMEM],
        (VMEM, VMEM),
    )(idx, innov1)
    gathered1 = swap(copies)
    innov2, copies, edges = call(
        update_kernel,
        (
            shape((DISTINCT, columns, LANES), f32),
            shape((members, rows, LANES), bf16),
            shape((2, DISTINCT, LANES), f32),
        ),
        [SMEM] + [VMEM] * 6,
        (VMEM, VMEM, VMEM),
        flops=2 * 2 * rows * LANES * lat,
    )(idx, gathered1, parts, mine, rest, land_mask, observed)
    gathered2 = swap(copies)
    left = lax.ppermute(edges[1], "lon", eastward)
    right = lax.ppermute(edges[0], "lon", westward)
    heights = call(
        height_kernel,
        shape((members, 2, columns, LANES), f32),
        [SMEM] + [VMEM] * 5,
        VMEM,
        [pltpu.VMEM((DISTINCT, columns, LANES), f32)],
        flops=2 * 2 * rows * LANES * lat,
    )(idx, gathered2, parts, innov2, land_mask, observed)
    heights = swap(heights)
    velocities = call(
        velocity_kernel,
        shape((members, 2, 2, columns, LANES), f32),
        [SMEM] + [VMEM] * 8,
        VMEM,
        [pltpu.VMEM((DISTINCT, columns, LANES), f32)] * 2,
    )(idx, gathered2, innov2, left, right, rest, land_mask, friction, observed)
    velocities = swap(velocities)
    sums = call(
        functools.partial(misfit_kernel, total=float(columns * lons)),
        shape((lons, 1, LANES), f32),
        [VMEM] * 3,
        VMEM,
    )(heights, land_mask, observed)
    sums = lax.all_to_all(sums, "lon", 0, 0, tiled=True)
    misfit = jnp.sum(sums, axis=(0, 1))[:2] / (lat * columns * lons)
    new_state = call(
        output_kernel,
        shape((2, 3, columns, lat), f32),
        [VMEM, VMEM],
        VMEM,
    )(heights, velocities)
    return new_state, misfit


def solution(mesh):
    placed = (
        P("member", None, "lon", None),
        P(),
        P("lon", None),
        P("lon", None),
        P("lon", None),
        P(),
        P("member", None),
        P("lon", None),
    )
    return jax.shard_map(
        per_device,
        mesh=mesh,
        in_specs=placed,
        out_specs=(P("member", None, "lon", None), P("member")),
        check_vma=False,
    )
```

time: 314 us -> 143 us (0.46)
  the two profiles are of different devices: /device:TPU:2 before, /device:TPU:1 now
where the time goes in v1:
time: 143 us; the launch traced here: 142 us
  starting transfers between devices  49.4 us (35%)
  blocking collectives  37.9 us (27%)
  waiting for transfers between devices  37.1 us (26%)
  Pallas kernels  10.4 us (7%)
  local copies, waits for them, and re-layouts  6.28 us (4%)
    all_to_all x3, blocking collectives, swap(): return lax.all_to_all(x, 'member', 0, 0, tiled=True)  37.9 us
    all_to_all x3, waiting for transfers between devices, swap(): return lax.all_to_all(x, 'member', 0, 0, tiled=True)  28.8 us
    all_to_all x3, starting transfers between devices, swap(): return lax.all_to_all(x, 'member', 0, 0, tiled=True)  13.9 us
    ppermute x1, starting transfers between devices, per_device(): right = lax.ppermute(head, 'lon', westward)  12.1 us
    all_to_all x1, starting transfers between devices, per_device(): sums = lax.all_to_all(sums, 'lon', 0, 0, tiled=True)  10.3 us
    ppermute x1, starting transfers between devices, per_device(): right = lax.ppermute(edges[0], 'lon', westward)  6.84 us
    unnamed x22, local copies, waits for them, and re-layouts  6.28 us
    ppermute x1, waiting for transfers between devices, per_device(): left = lax.ppermute(edges[1], 'lon', eastward)  6.16 us
  transfers between devices with their start and end apart: 8, of which 6 were waited for; matrix products, arithmetic and copies ran while one was open for 0% of the time, Pallas kernels for 2%

profile of v1, /device:TPU:1, one launch (start us, length us, event | category | flops | bytes accessed | tf_op | source)
XLA Modules:
  0.0 142.5 jit_solution(10363965345967467570)
XLA Ops:
  1.5 1.0 copy-done.3
  5.0 1.4 shard_map.95
  6.4 4.4 %collective-permute-start = (bf16[32,2048]{1,0:T(8,128)(2,1)S(1)}, bf16[32,2048]{1,0:T(8,128)(2,1)S(1)}, u32[]{:S(2)}, u32[]{:S(2)}) collective-permute-start(bf16[32,2048]{1,0:T(8,128)(2,1)S(1)} %get-tuple-element.13), channel_id=1, source_target_pairs={{0,1},{1,2},{2,3},{3,4},{4,5},{5,6},{6,7},{7,8},{8,9},{9,10},{10,1... | collective-permute-start | bytes 393224 | tf_op jit(solution)/shard_map/ppermute | solution.py:311
  10.8 12.1 %collective-permute-start.1 = (bf16[32,2048]{1,0:T(8,128)(2,1)S(1)}, bf16[32,2048]{1,0:T(8,128)(2,1)S(1)}, u32[]{:S(2)}, u32[]{:S(2)}) collective-permute-start(bf16[32,2048]{1,0:T(8,128)(2,1)S(1)} %get-tuple-element.14), channel_id=1, source_target_pairs={{1,0},{2,1},{3,2},{4,3},{5,4},{6,5},{7,6},{8,7},{9,8},{10,9},{11,1... | collective-permute-start | bytes 393224 | tf_op jit(solution)/shard_map/ppermute | solution.py:312
  22.9 1.3 collective-permute-done.left_ref
  25.8 2.3 %shard_map.96 = (f32[16,2,16,128]{3,2,1,0:T(8,128)S(1)}, f32[16,2,3,16,128]{4,3,2,1,0:T(8,128)}) custom-call(bf16[2,3,16,2048]{3,2,1,0:T(8,128)(2,1)S(1)} %copy-done.4, bf16[32,2048]{1,0:T(8,128)(2,1)S(1)} %collective-permute-done.left_ref, bf16[32,2048]{1,0:T(8,128)(2,1)S(1)} %collective-permute-done.1.right_ref, f32[16,2048]{1,0:T(8,128)S(1)} %copy-done.8, ...), custom_call_target="tpu_custom_call" | custom-call | flops 1000000 | bytes 1000000 | tf_op jit(solution)/shard_map/pallas_call | solution.py:318
  28.1 13.2 %all_to_all.35 = f32[16,2,16,128]{3,2,1,0:T(8,128)S(1)} all-to-all(f32[16,2,16,128]{3,2,1,0:T(8,128)S(1)} %get-tuple-element.15), channel_id=1, replica_groups=mesh['member'=16,'lon'=32] {'member'}, dimensions={0} | all-to-all | bytes 524288 | tf_op jit(solution)/shard_map/all_to_all | solution.py:302
  41.2 3.8 %all-to-all-start.2 = ((f32[16,2,3,16,128]{4,3,2,1,0:T(8,128)}), f32[16,2,3,16,128]{4,3,2,1,0:T(8,128)S(1)}, u32[]{:S(2)}, u32[]{:S(2)}) async-start(f32[16,2,3,16,128]{4,3,2,1,0:T(8,128)} %get-tuple-element.18), calls=%async_computation.2 | async-start | bytes 1572864 | tf_op jit(solution)/shard_map/all_to_all | solution.py:302
  45.0 1.4 shard_map.97
  46.4 11.4 %all-to-all-done.2 = f32[16,2,3,16,128]{4,3,2,1,0:T(8,128)S(1)} async-done(((f32[16,2,3,16,128]{4,3,2,1,0:T(8,128)}), f32[16,2,3,16,128]{4,3,2,1,0:T(8,128)S(1)}, u32[]{:S(2)}, u32[]{:S(2)}) %all-to-all-start.2) | async-done | bytes 786464 | tf_op jit(solution)/shard_map/all_to_all | solution.py:302
  57.8 4.4 %all-to-all-start.1 = ((bf16[16,128,128]{2,1,0:T(8,128)(2,1)}), bf16[16,128,128]{2,1,0:T(8,128)(2,1)S(1)}, u32[]{:S(2)}, u32[]{:S(2)}) async-start(bf16[16,128,128]{2,1,0:T(8,128)(2,1)} %get-tuple-element.16), calls=%async_computation.1 | async-start | bytes 1048576 | tf_op jit(solution)/shard_map/all_to_all | solution.py:302
  62.2 1.2 copy-done.7
  63.6 8.3 %all-to-all-done.1.gathered_ref = bf16[16,128,128]{2,1,0:T(8,128)(2,1)S(1)} async-done(((bf16[16,128,128]{2,1,0:T(8,128)(2,1)}), bf16[16,128,128]{2,1,0:T(8,128)(2,1)S(1)}, u32[]{:S(2)}, u32[]{:S(2)}) %all-to-all-start.1) | async-done | bytes 524320 | tf_op jit(solution)/shard_map/all_to_all | solution.py:302
  71.9 1.0 shard_map.99
  72.9 13.5 %all_to_all.36.gathered_ref = bf16[16,128,128]{2,1,0:T(8,128)(2,1)S(1)} all-to-all(bf16[16,128,128]{2,1,0:T(8,128)(2,1)S(1)} %get-tuple-element.19), channel_id=1, replica_groups=mesh['member'=16,'lon'=32] {'member'}, dimensions={0} | all-to-all | bytes 1048576 | tf_op jit(solution)/shard_map/all_to_all | solution.py:302
  86.4 1.0 shard_map.100
  87.4 11.2 %all_to_all.37.h_ref = f32[16,2,16,128]{3,2,1,0:T(8,128)S(1)} all-to-all(f32[16,2,16,128]{3,2,1,0:T(8,128)S(1)} %shard_map.100), channel_id=1, replica_groups=mesh['member'=16,'lon'=32] {'member'}, dimensions={0} | all-to-all | bytes 524288 | tf_op jit(solution)/shard_map/all_to_all | solution.py:302
  99.4 10.3 %all-to-all-start.6 = ((f32[32,1,128]{2,1,0:T(1,128)}), f32[32,1,128]{2,1,0:T(1,128)S(1)}, u32[]{:S(2)}, u32[]{:S(2)}) async-start(f32[32,1,128]{2,1,0:T(1,128)} %shard_map.103), calls=%async_computation.6 | async-start | bytes 32768 | tf_op jit(solution)/shard_map/all_to_all | solution.py:377
  109.7 6.8 %collective-permute-start.3 = (f32[8,128]{1,0:T(8,128)S(1)}, f32[8,128]{1,0:T(8,128)S(1)}, u32[]{:S(2)}, u32[]{:S(2)}) collective-permute-start(f32[8,128]{1,0:T(8,128)S(1)} %get-tuple-element.22), channel_id=1, source_target_pairs={{1,0},{2,1},{3,2},{4,3},{5,4},{6,5},{7,6},{8,7},{9,8},{10,9},{11,1... | collective-permute-start | bytes 12296 | tf_op jit(solution)/shard_map/ppermute | solution.py:353
  116.6 1.9 %collective-permute-start.2 = (f32[8,128]{1,0:T(8,128)S(1)}, f32[8,128]{1,0:T(8,128)S(1)}, u32[]{:S(2)}, u32[]{:S(2)}) collective-permute-start(f32[8,128]{1,0:T(8,128)S(1)} %get-tuple-element.23), channel_id=1, source_target_pairs={{0,1},{1,2},{2,3},{3,4},{4,5},{5,6},{6,7},{7,8},{8,9},{9,10},{10,1... | collective-permute-start | bytes 12296 | tf_op jit(solution)/shard_map/ppermute | solution.py:352
  118.5 6.2 %collective-permute-done.2.left_ref = f32[8,128]{1,0:T(8,128)S(1)} collective-permute-done((f32[8,128]{1,0:T(8,128)S(1)}, f32[8,128]{1,0:T(8,128)S(1)}, u32[]{:S(2)}, u32[]{:S(2)}) %collective-permute-start.2) | collective-permute-done | bytes 4128 | tf_op jit(solution)/shard_map/ppermute | solution.py:352
  124.7 1.5 %shard_map.101 = f32[16,2,2,16,128]{4,3,2,1,0:T(8,128)} custom-call(s32[64]{0:T(128)S(1)} %get-tuple-element.12.idx_ref, bf16[16,128,128]{2,1,0:T(8,128)(2,1)S(1)} %all_to_all.36.gathered_ref, f32[8,16,128]{2,1,0:T(8,128)S(1)} %get-tuple-element.20.innov_ref, f32[8,128]{1,0:T(8,128)S(1)} %collective-permute-done.2.left_ref, ...), custom_call_target="tpu_custom_call" | custom-call | flops 1000000 | bytes 1000000 | tf_op jit(solution)/shard_map/pallas_call | solution.py:363
  126.2 5.6 %all-to-all-start.5 = ((f32[16,2,2,16,128]{4,3,2,1,0:T(8,128)}), f32[16,2,2,16,128]{4,3,2,1,0:T(8,128)S(1)}, u32[]{:S(2)}, u32[]{:S(2)}) async-start(f32[16,2,2,16,128]{4,3,2,1,0:T(8,128)} %shard_map.101), calls=%async_computation.5 | async-start | bytes 1048576 | tf_op jit(solution)/shard_map/all_to_all | solution.py:302
  132.4 9.1 %all-to-all-done.5.zm_ref = f32[16,2,2,16,128]{4,3,2,1,0:T(8,128)S(1)} async-done(((f32[16,2,2,16,128]{4,3,2,1,0:T(8,128)}), f32[16,2,2,16,128]{4,3,2,1,0:T(8,128)S(1)}, u32[]{:S(2)}, u32[]{:S(2)}) %all-to-all-start.5) | async-done | bytes 524320 | tf_op jit(solution)/shard_map/all_to_all | solution.py:302
  (29 shorter events, 7.4 us)
Async XLA Ops:
  0.6 0.9 copy-start
  1.5 1.0 copy-start.3
  2.5 0.9 copy-start.5
  3.4 0.9 copy-start.8
  4.3 0.7 copy-start.10
  5.0 20.1 %copy-start.1 = (s32[16,2048]{1,0:T(8,128)S(1)}, s32[16,2048]{1,0:T(8,128)}, u32[]{:S(2)}) copy-start(s32[16,2048]{1,0:T(8,128)} %mask_ref.11) | copy-start | bytes 393220
  5.0 20.1 %copy-start.2 = (f32[16,2048]{1,0:T(8,128)S(1)}, f32[16,2048]{1,0:T(8,128)}, u32[]{:S(2)}) copy-start(f32[16,2048]{1,0:T(8,128)} %obs_ref.9) | copy-start | bytes 393220
  5.0 20.1 %copy-start.4 = (bf16[2,3,16,2048]{3,2,1,0:T(8,128)(2,1)S(1)}, bf16[2,3,16,2048]{3,2,1,0:T(8,128)(2,1)}, u32[]{:S(2)}) copy-start(bf16[2,3,16,2048]{3,2,1,0:T(8,128)(2,1)} %ens_ref.3) | copy-start | bytes 1179652
  5.0 20.1 %copy-start.6 = (f32[16,2048]{1,0:T(8,128)S(1)}, f32[16,2048]{1,0:T(8,128)}, u32[]{:S(2)}) copy-start(f32[16,2048]{1,0:T(8,128)} %fric_ref.5) | copy-start | bytes 393220
  6.4 17.8 %collective-permute-start = (bf16[32,2048]{1,0:T(8,128)(2,1)S(1)}, bf16[32,2048]{1,0:T(8,128)(2,1)S(1)}, u32[]{:S(2)}, u32[]{:S(2)}) collective-permute-start(bf16[32,2048]{1,0:T(8,128)(2,1)S(1)} %get-tuple-element.13), channel_id=1, source_target_pairs={{0,1},{1,2},{2,3},{3,4},{4,5},{5,6},{6,7},{7,8},{8,9},{9,10},{10,1... | collective-permute-start | bytes 393224 | tf_op jit(solution)/shard_map/ppermute | solution.py:311
  10.8 14.3 %collective-permute-start.1 = (bf16[32,2048]{1,0:T(8,128)(2,1)S(1)}, bf16[32,2048]{1,0:T(8,128)(2,1)S(1)}, u32[]{:S(2)}, u32[]{:S(2)}) collective-permute-start(bf16[32,2048]{1,0:T(8,128)(2,1)S(1)} %get-tuple-element.14), channel_id=1, source_target_pairs={{1,0},{2,1},{3,2},{4,3},{5,4},{6,5},{7,6},{8,7},{9,8},{10,9},{11,1... | collective-permute-start | bytes 393224 | tf_op jit(solution)/shard_map/ppermute | solution.py:312
  25.1 0.7 copy-start.9
  41.2 16.6 %all-to-all-start.2 = ((f32[16,2,3,16,128]{4,3,2,1,0:T(8,128)}), f32[16,2,3,16,128]{4,3,2,1,0:T(8,128)S(1)}, u32[]{:S(2)}, u32[]{:S(2)}) async-start(f32[16,2,3,16,128]{4,3,2,1,0:T(8,128)} %get-tuple-element.18), calls=%async_computation.2 | async-start | bytes 1572864 | tf_op jit(solution)/shard_map/all_to_all | solution.py:302
  57.8 14.1 %all-to-all-start.1 = ((bf16[16,128,128]{2,1,0:T(8,128)(2,1)}), bf16[16,128,128]{2,1,0:T(8,128)(2,1)S(1)}, u32[]{:S(2)}, u32[]{:S(2)}) async-start(bf16[16,128,128]{2,1,0:T(8,128)(2,1)} %get-tuple-element.16), calls=%async_computation.1 | async-start | bytes 1048576 | tf_op jit(solution)/shard_map/all_to_all | solution.py:302
  62.2 1.2 copy-start.7
  99.4 26.8 %all-to-all-start.6 = ((f32[32,1,128]{2,1,0:T(1,128)}), f32[32,1,128]{2,1,0:T(1,128)S(1)}, u32[]{:S(2)}, u32[]{:S(2)}) async-start(f32[32,1,128]{2,1,0:T(1,128)} %shard_map.103), calls=%async_computation.6 | async-start | bytes 32768 | tf_op jit(solution)/shard_map/all_to_all | solution.py:377
  109.7 8.8 %collective-permute-start.3 = (f32[8,128]{1,0:T(8,128)S(1)}, f32[8,128]{1,0:T(8,128)S(1)}, u32[]{:S(2)}, u32[]{:S(2)}) collective-permute-start(f32[8,128]{1,0:T(8,128)S(1)} %get-tuple-element.22), channel_id=1, source_target_pairs={{1,0},{2,1},{3,2},{4,3},{5,4},{6,5},{7,6},{8,7},{9,8},{10,9},{11,1... | collective-permute-start | bytes 12296 | tf_op jit(solution)/shard_map/ppermute | solution.py:353
  116.6 8.1 %collective-permute-start.2 = (f32[8,128]{1,0:T(8,128)S(1)}, f32[8,128]{1,0:T(8,128)S(1)}, u32[]{:S(2)}, u32[]{:S(2)}) collective-permute-start(f32[8,128]{1,0:T(8,128)S(1)} %get-tuple-element.23), channel_id=1, source_target_pairs={{0,1},{1,2},{2,3},{3,4},{4,5},{5,6},{6,7},{7,8},{8,9},{9,10},{10,1... | collective-permute-start | bytes 12296 | tf_op jit(solution)/shard_map/ppermute | solution.py:352
  126.2 15.3 %all-to-all-start.5 = ((f32[16,2,2,16,128]{4,3,2,1,0:T(8,128)}), f32[16,2,2,16,128]{4,3,2,1,0:T(8,128)S(1)}, u32[]{:S(2)}, u32[]{:S(2)}) async-start(f32[16,2,2,16,128]{4,3,2,1,0:T(8,128)} %shard_map.101), calls=%async_computation.5 | async-start | bytes 1048576 | tf_op jit(solution)/shard_map/all_to_all | solution.py:302

commit v2 on v1

--- a/solution.py
+++ b/solution.py
@@ -17,16 +17,17 @@
 
 VMEM = pl.BlockSpec(memory_space=pltpu.VMEM)
 SMEM = pl.BlockSpec(memory_space=pltpu.SMEM)
-
-
-def call(kernel, out_shape, in_specs, out_specs, scratch=(), flops=1e6, bytes_accessed=1e6):
+ANY = pl.BlockSpec(memory_space=pl.ANY)
+
+
+def call(kernel, out_shape, in_specs, out_specs, scratch=(), flops=1e6, bytes_accessed=1e6, limit=24):
     return pl.pallas_call(
         kernel,
         out_shape=out_shape,
         in_specs=in_specs,
         out_specs=out_specs,
         scratch_shapes=list(scratch),
-        compiler_params=pltpu.CompilerParams(vmem_limit_bytes=24 * 1024 * 1024),
+        compiler_params=pltpu.CompilerParams(vmem_limit_bytes=limit * 1024 * 1024),
         cost_estimate=pl.CostEstimate(
             flops=int(flops), bytes_accessed=int(bytes_accessed), transcendentals=0
         ),
@@ -40,8 +41,19 @@
     return first, second, rest - second
 
 
-def pack_kernel(copy_ref, ens_ref, depth_ref, mask_ref, fric_ref, head_ref, tail_ref, idx_ref, rows, seen):
+def pack_kernel(
+    copy_ref, ens_hbm, depth_hbm, mask_hbm, fric_hbm, head_ref, tail_ref, idx_ref,
+    ens_ref, depth_ref, mask_ref, fric_ref, rows, seen, sems,
+):
     columns = depth_ref.shape[0]
+    fetches = [
+        pltpu.make_async_copy(src, dst, sems.at[k])
+        for k, (src, dst) in enumerate(
+            ((ens_hbm, ens_ref), (depth_hbm, depth_ref), (mask_hbm, mask_ref), (fric_hbm, fric_ref))
+        )
+    ]
+    for fetch in fetches:
+        fetch.start()
     for p in range(32):
         seen[p] = 0
     for s in range(32):
@@ -58,6 +70,8 @@
     for s in range(32):
         idx_ref[DISTINCT + s] = seen[copy_ref[s]]
 
+    for fetch in fetches:
+        fetch.wait()
     depth3 = pieces(depth_ref[...])
     fric3 = pieces(fric_ref[...])
     wet = jnp.where(mask_ref[...] == 1, 1.0, 0.0).astype(f32)
@@ -90,7 +104,7 @@
 
 def source_kernel(
     ens_ref, left_ref, right_ref, depth_ref, mask_ref, fric_ref, cor_ref, obs_ref,
-    innov_ref, rest_ref, ext, lrows, rrows, sdepth, swet, sfric,
+    out_ref, ext, lrows, rrows, sdepth, swet, sfric,
 ):
     columns, lat = depth_ref.shape
     blocks = lat // LANES
@@ -133,7 +147,7 @@
         fresh = height - time_step * wet * (east(depth * zonal) + north(depth * meridional))
         innov = obs_ref[...] - fresh[lo:hi, :]
         for b in range(blocks):
-            innov_ref[b, p] = innov[:, b * LANES : (b + 1) * LANES]
+            out_ref[b, p, 0] = innov[:, b * LANES : (b + 1) * LANES]
         zonal1 = damped * (zonal + time_step * (turning * meridional - east(fresh)))
         meridional1 = damped * (meridional - time_step * (turning * zonal + north(fresh)))
         change = -time_step * wet * (east(depth * zonal1) + north(depth * meridional1))
@@ -141,7 +155,7 @@
         meridional_part = damped * (meridional1 - time_step * (turning * zonal1))
         for k, value in enumerate((change, zonal_part, meridional_part)):
             for b in range(blocks):
-                rest_ref[b, p, k] = value[lo:hi, b * LANES : (b + 1) * LANES]
+                out_ref[b, p, k + 1] = value[lo:hi, b * LANES : (b + 1) * LANES]
 
 
 def split_kernel(spread_ref, out_ref):
@@ -151,11 +165,10 @@
     out_ref[1] = (s - high.astype(f32)).astype(bf16)
 
 
-def select_kernel(idx_ref, all_ref, mine_ref, copies_ref):
-    columns = all_ref.shape[1]
+def select_kernel(idx_ref, all_ref, copies_ref):
+    columns = all_ref.shape[2]
     for i in range(DISTINCT):
-        v = all_ref[idx_ref[i]]
-        mine_ref[i] = v
+        v = all_ref[idx_ref[i], 0]
         b = v.astype(bf16)
         for d in range(copies_ref.shape[0]):
             copies_ref[d, i * columns : (i + 1) * columns, :] = b
@@ -179,7 +192,7 @@
 
 
 def update_kernel(
-    idx_ref, gathered_ref, spread_ref, mine_ref, rest_ref, mask_ref, obs_ref,
+    idx_ref, gathered_ref, spread_ref, all_ref, mask_ref, obs_ref,
     innov_ref, copies_ref, edge_ref,
 ):
     columns = mask_ref.shape[0]
@@ -188,9 +201,9 @@
     obs = block_of(obs_ref, me)
     spreaded = spread_dot(gathered_ref, spread_ref)
     for i in range(DISTINCT):
-        innov = mine_ref[i]
+        innov = all_ref[idx_ref[i], 0]
         sp = spreaded[i * columns : (i + 1) * columns, :]
-        new = innov - nudge_rate * wet * (innov + sp) - rest_ref[idx_ref[i], 0]
+        new = innov - nudge_rate * wet * (innov + sp) - all_ref[idx_ref[i], 1]
         innov_ref[i] = new
         b = new.astype(bf16)
         for d in range(copies_ref.shape[0]):
@@ -200,25 +213,9 @@
         edge_ref[1, i : i + 1, :] = fresh[columns - 1 : columns, :]
 
 
-def height_kernel(
-    idx_ref, gathered_ref, spread_ref, innov_ref, mask_ref, obs_ref, out_ref, height
-):
-    columns = mask_ref.shape[0]
-    me = lax.axis_index("member")
-    wet = wet_block(mask_ref, me)
-    obs = block_of(obs_ref, me)
-    spreaded = spread_dot(gathered_ref, spread_ref)
-    for i in range(DISTINCT):
-        innov = innov_ref[i]
-        sp = spreaded[i * columns : (i + 1) * columns, :]
-        height[i] = (obs - innov) + nudge_rate * wet * (innov + sp)
-    for s in range(32):
-        out_ref[s // 2, s % 2] = height[idx_ref[DISTINCT + s]]
-
-
-def velocity_kernel(
-    idx_ref, gathered_ref, innov_ref, left_ref, right_ref, rest_ref, mask_ref, fric_ref, obs_ref,
-    out_ref, zonal, meridional,
+def final_kernel(
+    idx_ref, gathered_ref, spread_ref, innov_ref, left_ref, right_ref, all_ref,
+    mask_ref, fric_ref, obs_ref, out_ref, state,
 ):
     columns = mask_ref.shape[0]
     blocks = gathered_ref.shape[0]
@@ -234,9 +231,12 @@
     has_after = jnp.where(me < blocks - 1, 1.0, 0.0).astype(f32)
     lane = lax.broadcasted_iota(jnp.int32, (columns, LANES), 1)
     row = lax.broadcasted_iota(jnp.int32, (columns, LANES), 0)
+    spreaded = spread_dot(gathered_ref, spread_ref)
     for i in range(DISTINCT):
-        fresh = obs - innov_ref[i]
+        innov = innov_ref[i]
+        fresh = obs - innov
         part = slice(i * columns, (i + 1) * columns)
+        state[i, 0] = fresh + nudge_rate * wet * (innov + spreaded[part, :])
         fresh_before = has_before * (obs_before - gathered_ref[before, part, :].astype(f32))
         fresh_after = has_after * (obs_after - gathered_ref[after, part, :].astype(f32))
         down = jnp.where(lane == 0, pltpu.roll(fresh_before, 1, 1), pltpu.roll(fresh, 1, 1))
@@ -250,12 +250,10 @@
             row == columns - 1, right_ref[i : i + 1, :], pltpu.roll(fresh, columns - 1, 0)
         )
         src = idx_ref[i]
-        zonal[i] = rest_ref[src, 1] - damped * (time_step * 0.5 * (easterly - west))
-        meridional[i] = rest_ref[src, 2] - damped * (time_step * 0.5 * (up - down))
+        state[i, 1] = all_ref[src, 2] - damped * (time_step * 0.5 * (easterly - west))
+        state[i, 2] = all_ref[src, 3] - damped * (time_step * 0.5 * (up - down))
     for s in range(32):
-        place = idx_ref[DISTINCT + s]
-        out_ref[s // 2, s % 2, 0] = zonal[place]
-        out_ref[s // 2, s % 2, 1] = meridional[place]
+        out_ref[s // 2, s % 2] = state[idx_ref[DISTINCT + s]]
 
 
 def misfit_kernel(h_ref, mask_ref, obs_ref, out_ref, *, total):
@@ -271,21 +269,16 @@
         for b in range(blocks):
             part = slice(b * LANES, (b + 1) * LANES)
             wet = jnp.where(mask_ref[:, part] == 1, 1.0, 0.0).astype(f32)
-            gap = obs_ref[:, part] - h_ref[b, p]
+            gap = obs_ref[:, part] - h_ref[b, p, 0]
             acc = acc + wet * (gap * gap)
         sums = jnp.where(lane == p, jnp.sum(acc * weight), sums)
     for d in range(out_ref.shape[0]):
         out_ref[d] = sums
 
 
-def output_kernel(h_ref, zm_ref, out_ref):
-    blocks = h_ref.shape[0]
-    for p in range(2):
-        for b in range(blocks):
-            part = slice(b * LANES, (b + 1) * LANES)
-            out_ref[p, 0, :, part] = h_ref[b, p]
-            out_ref[p, 1, :, part] = zm_ref[b, p, 0]
-            out_ref[p, 2, :, part] = zm_ref[b, p, 1]
+def output_kernel(state_ref, out_ref):
+    for b in range(state_ref.shape[0]):
+        out_ref[:, :, :, b * LANES : (b + 1) * LANES] = state_ref[b]
 
 
 def per_device(ensemble, copy_list, depth, land_mask, friction, coriolis, spread, observed):
@@ -304,9 +297,18 @@
     head, tail, idx = call(
         pack_kernel,
         (shape((32, lat), bf16), shape((32, lat), bf16), shape((64,), jnp.int32)),
-        [SMEM, VMEM, VMEM, VMEM, VMEM],
+        [SMEM, ANY, ANY, ANY, ANY],
         (VMEM, VMEM, SMEM),
-        [pltpu.VMEM((32, lat), f32), pltpu.SMEM((32,), jnp.int32)],
+        [
+            pltpu.VMEM(ensemble.shape, bf16),
+            pltpu.VMEM(depth.shape, f32),
+            pltpu.VMEM(depth.shape, jnp.int32),
+            pltpu.VMEM(depth.shape, f32),
+            pltpu.VMEM((32, lat), f32),
+            pltpu.SMEM((32,), jnp.int32),
+            pltpu.SemaphoreType.DMA((4,)),
+        ],
+        limit=60,
     )(copy_list, ensemble, depth, land_mask, friction)
     left = lax.ppermute(tail, "lon", eastward)
     right = lax.ppermute(head, "lon", westward)
@@ -315,27 +317,19 @@
     )(spread)
 
     ext_rows = columns + 16
-    innov1, rest = call(
+    step1 = call(
         source_kernel,
-        (
-            shape((blocks, 2, columns, LANES), f32),
-            shape((blocks, 2, 3, columns, LANES), f32),
-        ),
+        shape((blocks, 2, 4, columns, LANES), f32),
         [VMEM] * 8,
-        (VMEM, VMEM),
+        VMEM,
         [pltpu.VMEM((3, ext_rows, lat), f32)]
         + [pltpu.VMEM((32, lat), f32)] * 2
         + [pltpu.VMEM((ext_rows, lat), f32)] * 3,
     )(ensemble, left, right, depth, land_mask, friction, coriolis[None, :], observed)
-
-    innov1 = swap(innov1).reshape(2 * members, columns, LANES)
-    rest = swap(rest).reshape(2 * members, 3, columns, LANES)
-    mine, copies = call(
-        select_kernel,
-        (shape((DISTINCT, columns, LANES), f32), shape((members, rows, LANES), bf16)),
-        [SMEM, VMEM],
-        (VMEM, VMEM),
-    )(idx, innov1)
+    step1 = swap(step1).reshape(2 * members, 4, columns, LANES)
+    copies = call(
+        select_kernel, shape((members, rows, LANES), bf16), [SMEM, VMEM], VMEM
+    )(idx, step1)
     gathered1 = swap(copies)
     innov2, copies, edges = call(
         update_kernel,
@@ -344,44 +338,31 @@
             shape((members, rows, LANES), bf16),
             shape((2, DISTINCT, LANES), f32),
         ),
-        [SMEM] + [VMEM] * 6,
+        [SMEM] + [VMEM] * 5,
         (VMEM, VMEM, VMEM),
         flops=2 * 2 * rows * LANES * lat,
-    )(idx, gathered1, parts, mine, rest, land_mask, observed)
+    )(idx, gathered1, parts, step1, land_mask, observed)
     gathered2 = swap(copies)
     left = lax.ppermute(edges[1], "lon", eastward)
     right = lax.ppermute(edges[0], "lon", westward)
-    heights = call(
-        height_kernel,
-        shape((members, 2, columns, LANES), f32),
-        [SMEM] + [VMEM] * 5,
+    state = call(
+        final_kernel,
+        shape((members, 2, 3, columns, LANES), f32),
+        [SMEM] + [VMEM] * 9,
         VMEM,
-        [pltpu.VMEM((DISTINCT, columns, LANES), f32)],
+        [pltpu.VMEM((DISTINCT, 3, columns, LANES), f32)],
         flops=2 * 2 * rows * LANES * lat,
-    )(idx, gathered2, parts, innov2, land_mask, observed)
-    heights = swap(heights)
-    velocities = call(
-        velocity_kernel,
-        shape((members, 2, 2, columns, LANES), f32),
-        [SMEM] + [VMEM] * 8,
-        VMEM,
-        [pltpu.VMEM((DISTINCT, columns, LANES), f32)] * 2,
-    )(idx, gathered2, innov2, left, right, rest, land_mask, friction, observed)
-    velocities = swap(velocities)
+    )(idx, gathered2, parts, innov2, left, right, step1, land_mask, friction, observed)
+    state = swap(state)
     sums = call(
         functools.partial(misfit_kernel, total=float(columns * lons)),
         shape((lons, 1, LANES), f32),
         [VMEM] * 3,
         VMEM,
-    )(heights, land_mask, observed)
+    )(state, land_mask, observed)
     sums = lax.all_to_all(sums, "lon", 0, 0, tiled=True)
     misfit = jnp.sum(sums, axis=(0, 1))[:2] / (lat * columns * lons)
-    new_state = call(
-        output_kernel,
-        shape((2, 3, columns, lat), f32),
-        [VMEM, VMEM],
-        VMEM,
-    )(heights, velocities)
+    new_state = call(output_kernel, shape((2, 3, columns, lat), f32), [VMEM], VMEM)(state)
     return new_state, misfit
 
 

time: 143 us -> 126 us (0.88)
  starting transfers between devices: 49.4 us -> 40.5 us
  waiting for transfers between devices: 37.1 us -> 29.5 us
  local copies, waits for them, and re-layouts: 6.28 us -> 3.49 us
  blocking collectives: 37.9 us -> 40.4 us
    all_to_all x3 -> x2, waiting for transfers between devices: 28.8 us -> 8.32 us  [swap(): return lax.all_to_all(x, 'member', 0, 0, tiled=True)]
    all_to_all x1, waiting for transfers between devices: 0.01 us -> 12.7 us  [per_device(): sums = lax.all_to_all(sums, 'lon', 0, 0, tiled=True)]
    all_to_all x1, starting transfers between devices: 10.3 us -> 4.46 us  [per_device(): sums = lax.all_to_all(sums, 'lon', 0, 0, tiled=True)]
    all_to_all x3 -> x2, starting transfers between devices: 13.9 us -> 9.4 us  [swap(): return lax.all_to_all(x, 'member', 0, 0, tiled=True)]
    unnamed x22 -> x16, local copies, waits for them, and re-layouts: 6.28 us -> 3.49 us
    all_to_all x3 -> x2, blocking collectives: 37.9 us -> 40.4 us  [swap(): return lax.all_to_all(x, 'member', 0, 0, tiled=True)]
    pallas_call x5 -> x4, Pallas kernels: 7.16 us -> 4.78 us  [the longest x1 1.41 us: per_device(): call(source_kernel, shape((blocks, 2, 4, columns, LANES), f32), [VMEM] *...]
    pallas_call x1, Pallas kernels: 1.37 us -> 2.85 us  [per_device(): call(pack_kernel, (shape((32, lat), bf16), shape((32, lat), bf16), shape(...]
  transfers between devices with their start and end apart: 8 -> 7, of which waited for: 6 -> 5; matrix products, arithmetic and copies ran while one was open for 0% -> 0% of each run, Pallas kernels for 2% -> 1%
where the time goes in v2:
time: 126 us
  starting transfers between devices  40.5 us (32%)
  blocking collectives  40.4 us (32%)
  waiting for transfers between devices  29.5 us (23%)
  Pallas kernels  10.4 us (8%)
  local copies, waits for them, and re-layouts  3.49 us (3%)
    all_to_all x2, blocking collectives, swap(): return lax.all_to_all(x, 'member', 0, 0, tiled=True)  40.4 us
    all_to_all x1, waiting for transfers between devices, per_device(): sums = lax.all_to_all(sums, 'lon', 0, 0, tiled=True)  12.7 us
    ppermute x1, starting transfers between devices, per_device(): right = lax.ppermute(head, 'lon', westward)  12.1 us
    all_to_all x2, starting transfers between devices, swap(): return lax.all_to_all(x, 'member', 0, 0, tiled=True)  9.4 us
    all_to_all x2, waiting for transfers between devices, swap(): return lax.all_to_all(x, 'member', 0, 0, tiled=True)  8.32 us
    ppermute x1, starting transfers between devices, per_device(): right = lax.ppermute(edges[0], 'lon', westward)  8.23 us
    ppermute x1, waiting for transfers between devices, per_device(): left = lax.ppermute(edges[1], 'lon', eastward)  6.03 us
    all_to_all x1, starting transfers between devices, per_device(): sums = lax.all_to_all(sums, 'lon', 0, 0, tiled=True)  4.46 us
  transfers between devices with their start and end apart: 7, of which 5 were waited for; matrix products, arithmetic and copies ran while one was open for 0% of the time, Pallas kernels for 1%

profile of v2, /device:TPU:1, one launch (start us, length us, event | category | flops | bytes accessed | tf_op | source)
XLA Modules:
  0.0 125.6 jit_solution(14855272827896395751)
XLA Ops:
  0.7 2.8 %shard_map.95 = (bf16[32,2048]{1,0:T(8,128)(2,1)}, bf16[32,2048]{1,0:T(8,128)(2,1)}, s32[64]{0:T(128)}) custom-call(s32[32]{0:T(128)} %copy_ref.1, bf16[2,3,16,2048]{3,2,1,0:T(8,128)(2,1)} %ens_ref.1, f32[16,2048]{1,0:T(8,128)} %depth_ref.1, s32[16,2048]{1,0:T(8,128)} %mask_ref.7, f32[16,2048]{1,0:T(8,128)} %fric_ref.3), custom_call_target="tpu_custom_call" | custom-call | flops 1000000 | bytes 1000000 | tf_op jit(solution)/shard_map/pallas_call | solution.py:297
  3.5 4.4 %collective-permute-start = (bf16[32,2048]{1,0:T(8,128)(2,1)}, bf16[32,2048]{1,0:T(8,128)(2,1)S(1)}, u32[]{:S(2)}, u32[]{:S(2)}) collective-permute-start(bf16[32,2048]{1,0:T(8,128)(2,1)} %get-tuple-element.9), channel_id=1, source_target_pairs={{0,1},{1,2},{2,3},{3,4},{4,5},{5,6},{6,7},{7,8},{8,9},{9,10},{10,1... | collective-permute-start | bytes 393224 | tf_op jit(solution)/shard_map/ppermute | solution.py:313
  7.9 12.1 %collective-permute-start.1 = (bf16[32,2048]{1,0:T(8,128)(2,1)}, bf16[32,2048]{1,0:T(8,128)(2,1)S(1)}, u32[]{:S(2)}, u32[]{:S(2)}) collective-permute-start(bf16[32,2048]{1,0:T(8,128)(2,1)} %get-tuple-element.10), channel_id=1, source_target_pairs={{1,0},{2,1},{3,2},{4,3},{5,4},{6,5},{7,6},{8,7},{9,8},{10,9},{11,1... | collective-permute-start | bytes 393224 | tf_op jit(solution)/shard_map/ppermute | solution.py:314
  20.0 1.5 %collective-permute-done.left_ref = bf16[32,2048]{1,0:T(8,128)(2,1)S(1)} collective-permute-done((bf16[32,2048]{1,0:T(8,128)(2,1)}, bf16[32,2048]{1,0:T(8,128)(2,1)S(1)}, u32[]{:S(2)}, u32[]{:S(2)}) %collective-permute-start) | collective-permute-done | bytes 131104 | tf_op jit(solution)/shard_map/ppermute | solution.py:313
  21.5 1.0 collective-permute-done.1.right_ref
  22.5 0.9 copy-done.5
  23.4 0.7 copy-done.6
  24.1 1.4 %shard_map.96 = f32[16,2,4,16,128]{4,3,2,1,0:T(8,128)S(1)} custom-call(bf16[2,3,16,2048]{3,2,1,0:T(8,128)(2,1)S(1)} %copy-done.2, bf16[32,2048]{1,0:T(8,128)(2,1)S(1)} %collective-permute-done.left_ref, bf16[32,2048]{1,0:T(8,128)(2,1)S(1)} %collective-permute-done.1.right_ref, f32[16,2048]{1,0:T(8,128)S(1)} %copy-done.5, s32[16,2048]{1,0:T(8,128)S(1)} %copy-done, ...), custom_call_target="tpu_custom_call" | custom-call | flops 1000000 | bytes 1000000 | tf_op jit(solution)/shard_map/pallas_call | solution.py:320
  25.5 21.0 %all_to_all.25 = f32[16,2,4,16,128]{4,3,2,1,0:T(8,128)S(1)} all-to-all(f32[16,2,4,16,128]{4,3,2,1,0:T(8,128)S(1)} %shard_map.96), channel_id=1, replica_groups=mesh['member'=16,'lon'=32] {'member'}, dimensions={0} | all-to-all | bytes 2097152 | tf_op jit(solution)/shard_map/all_to_all | solution.py:295
  47.2 1.4 %shard_map.97 = bf16[16,128,128]{2,1,0:T(8,128)(2,1)} custom-call(s32[64]{0:T(128)S(1)} %copy-done.7, f32[32,4,16,128]{3,2,1,0:T(8,128)S(1)} %bitcast.6), custom_call_target="tpu_custom_call" | custom-call | flops 1000000 | bytes 1000000 | tf_op jit(solution)/shard_map/pallas_call | solution.py:330
  48.6 4.7 %all-to-all-start.1 = ((bf16[16,128,128]{2,1,0:T(8,128)(2,1)}), bf16[16,128,128]{2,1,0:T(8,128)(2,1)S(1)}, u32[]{:S(2)}, u32[]{:S(2)}) async-start(bf16[16,128,128]{2,1,0:T(8,128)(2,1)} %shard_map.97), calls=%async_computation.1 | async-start | bytes 1048576 | tf_op jit(solution)/shard_map/all_to_all | solution.py:295
  53.3 1.2 copy-done.4
  54.7 8.3 %all-to-all-done.1.gathered_ref = bf16[16,128,128]{2,1,0:T(8,128)(2,1)S(1)} async-done(((bf16[16,128,128]{2,1,0:T(8,128)(2,1)}), bf16[16,128,128]{2,1,0:T(8,128)(2,1)S(1)}, u32[]{:S(2)}, u32[]{:S(2)}) %all-to-all-start.1) | async-done | bytes 524320 | tf_op jit(solution)/shard_map/all_to_all | solution.py:295
  63.0 1.8 %shard_map.99 = (f32[8,16,128]{2,1,0:T(8,128)S(1)}, bf16[16,128,128]{2,1,0:T(8,128)(2,1)}, f32[2,8,128]{2,1,0:T(8,128)S(1)}) custom-call(s32[64]{0:T(128)S(1)} %copy-done.7, bf16[16,128,128]{2,1,0:T(8,128)(2,1)S(1)} %all-to-all-done.1.gathered_ref, bf16[2,128,2048]{2,1,0:T(8,128)(2,1)S(1)} %shard_map.98.spread_ref, f32[32,4,16,128]{3,2,1,0:T(8,128)S(1)} %bitcast.7, ...), custom_call_target="tpu_custom_call" | custom-call | flops 134217728 | bytes 1000000 | tf_op jit(solution)/shard_map/pallas_call | solution.py:334
  64.8 4.7 %all-to-all-start.2 = ((bf16[16,128,128]{2,1,0:T(8,128)(2,1)}), bf16[16,128,128]{2,1,0:T(8,128)(2,1)S(1)}, u32[]{:S(2)}, u32[]{:S(2)}) async-start(bf16[16,128,128]{2,1,0:T(8,128)(2,1)} %get-tuple-element.11), calls=%async_computation.2 | async-start | bytes 1048576 | tf_op jit(solution)/shard_map/all_to_all | solution.py:295
  69.5 8.2 %collective-permute-start.3 = (f32[8,128]{1,0:T(8,128)S(1)}, f32[8,128]{1,0:T(8,128)S(1)}, u32[]{:S(2)}, u32[]{:S(2)}) collective-permute-start(f32[8,128]{1,0:T(8,128)S(1)} %get-tuple-element.14), channel_id=1, source_target_pairs={{1,0},{2,1},{3,2},{4,3},{5,4},{6,5},{7,6},{8,7},{9,8},{10,9},{11,1... | collective-permute-start | bytes 12296 | tf_op jit(solution)/shard_map/ppermute | solution.py:347
  77.7 1.9 %collective-permute-start.2 = (f32[8,128]{1,0:T(8,128)S(1)}, f32[8,128]{1,0:T(8,128)S(1)}, u32[]{:S(2)}, u32[]{:S(2)}) collective-permute-start(f32[8,128]{1,0:T(8,128)S(1)} %get-tuple-element.15), channel_id=1, source_target_pairs={{0,1},{1,2},{2,3},{3,4},{4,5},{5,6},{6,7},{7,8},{8,9},{9,10},{10,1... | collective-permute-start | bytes 12296 | tf_op jit(solution)/shard_map/ppermute | solution.py:346
  79.7 6.0 %collective-permute-done.2.left_ref = f32[8,128]{1,0:T(8,128)S(1)} collective-permute-done((f32[8,128]{1,0:T(8,128)S(1)}, f32[8,128]{1,0:T(8,128)S(1)}, u32[]{:S(2)}, u32[]{:S(2)}) %collective-permute-start.2) | collective-permute-done | bytes 4128 | tf_op jit(solution)/shard_map/ppermute | solution.py:346
  85.7 1.0 shard_map.100
  86.8 19.4 %all_to_all.26.state_ref.h_ref = f32[16,2,3,16,128]{4,3,2,1,0:T(8,128)S(1)} all-to-all(f32[16,2,3,16,128]{4,3,2,1,0:T(8,128)S(1)} %shard_map.100), channel_id=1, replica_groups=mesh['member'=16,'lon'=32] {'member'}, dimensions={0} | all-to-all | bytes 1572864 | tf_op jit(solution)/shard_map/all_to_all | solution.py:295
  106.2 0.8 shard_map.102
  106.9 4.5 %all-to-all-start.4 = ((f32[32,1,128]{2,1,0:T(1,128)}), f32[32,1,128]{2,1,0:T(1,128)S(1)}, u32[]{:S(2)}, u32[]{:S(2)}) async-start(f32[32,1,128]{2,1,0:T(1,128)} %shard_map.102), calls=%async_computation.4 | async-start | bytes 32768 | tf_op jit(solution)/shard_map/all_to_all | solution.py:363
  111.4 0.9 shard_map.101
  112.4 12.7 %all-to-all-done.4 = f32[32,1,128]{2,1,0:T(1,128)S(1)} async-done(((f32[32,1,128]{2,1,0:T(1,128)}), f32[32,1,128]{2,1,0:T(1,128)S(1)}, u32[]{:S(2)}, u32[]{:S(2)}) %all-to-all-start.4) | async-done | bytes 16416 | tf_op jit(solution)/shard_map/all_to_all | solution.py:363
  (19 shorter events, 1.4 us)
Async XLA Ops:
  0.6 21.9 %copy-start = (s32[16,2048]{1,0:T(8,128)S(1)}, s32[16,2048]{1,0:T(8,128)}, u32[]{:S(2)}) copy-start(s32[16,2048]{1,0:T(8,128)} %mask_ref.7) | copy-start | bytes 393220
  0.6 21.9 %copy-start.3 = (f32[16,2048]{1,0:T(8,128)S(1)}, f32[16,2048]{1,0:T(8,128)}, u32[]{:S(2)}) copy-start(f32[16,2048]{1,0:T(8,128)} %fric_ref.3) | copy-start | bytes 393220
  0.7 21.9 %copy-start.2 = (bf16[2,3,16,2048]{3,2,1,0:T(8,128)(2,1)S(1)}, bf16[2,3,16,2048]{3,2,1,0:T(8,128)(2,1)}, u32[]{:S(2)}) copy-start(bf16[2,3,16,2048]{3,2,1,0:T(8,128)(2,1)} %ens_ref.1) | copy-start | bytes 1179652
  0.7 21.9 %copy-start.1 = (f32[16,2048]{1,0:T(8,128)S(1)}, f32[16,2048]{1,0:T(8,128)}, u32[]{:S(2)}) copy-start(f32[16,2048]{1,0:T(8,128)} %obs_ref.7) | copy-start | bytes 393220
  3.5 18.0 %collective-permute-start = (bf16[32,2048]{1,0:T(8,128)(2,1)}, bf16[32,2048]{1,0:T(8,128)(2,1)S(1)}, u32[]{:S(2)}, u32[]{:S(2)}) collective-permute-start(bf16[32,2048]{1,0:T(8,128)(2,1)} %get-tuple-element.9), channel_id=1, source_target_pairs={{0,1},{1,2},{2,3},{3,4},{4,5},{5,6},{6,7},{7,8},{8,9},{9,10},{10,1... | collective-permute-start | bytes 393224 | tf_op jit(solution)/shard_map/ppermute | solution.py:313
  7.9 14.6 %collective-permute-start.1 = (bf16[32,2048]{1,0:T(8,128)(2,1)}, bf16[32,2048]{1,0:T(8,128)(2,1)S(1)}, u32[]{:S(2)}, u32[]{:S(2)}) collective-permute-start(bf16[32,2048]{1,0:T(8,128)(2,1)} %get-tuple-element.10), channel_id=1, source_target_pairs={{1,0},{2,1},{3,2},{4,3},{5,4},{6,5},{7,6},{8,7},{9,8},{10,9},{11,1... | collective-permute-start | bytes 393224 | tf_op jit(solution)/shard_map/ppermute | solution.py:314
  22.5 0.9 copy-start.5
  23.4 0.7 copy-start.6
  46.6 0.7 copy-start.7
  48.6 14.4 %all-to-all-start.1 = ((bf16[16,128,128]{2,1,0:T(8,128)(2,1)}), bf16[16,128,128]{2,1,0:T(8,128)(2,1)S(1)}, u32[]{:S(2)}, u32[]{:S(2)}) async-start(bf16[16,128,128]{2,1,0:T(8,128)(2,1)} %shard_map.97), calls=%async_computation.1 | async-start | bytes 1048576 | tf_op jit(solution)/shard_map/all_to_all | solution.py:295
  53.3 1.2 copy-start.4
  64.8 20.9 %all-to-all-start.2 = ((bf16[16,128,128]{2,1,0:T(8,128)(2,1)}), bf16[16,128,128]{2,1,0:T(8,128)(2,1)S(1)}, u32[]{:S(2)}, u32[]{:S(2)}) async-start(bf16[16,128,128]{2,1,0:T(8,128)(2,1)} %get-tuple-element.11), calls=%async_computation.2 | async-start | bytes 1048576 | tf_op jit(solution)/shard_map/all_to_all | solution.py:295
  69.5 10.2 %collective-permute-start.3 = (f32[8,128]{1,0:T(8,128)S(1)}, f32[8,128]{1,0:T(8,128)S(1)}, u32[]{:S(2)}, u32[]{:S(2)}) collective-permute-start(f32[8,128]{1,0:T(8,128)S(1)} %get-tuple-element.14), channel_id=1, source_target_pairs={{1,0},{2,1},{3,2},{4,3},{5,4},{6,5},{7,6},{8,7},{9,8},{10,9},{11,1... | collective-permute-start | bytes 12296 | tf_op jit(solution)/shard_map/ppermute | solution.py:347
  77.7 8.0 %collective-permute-start.2 = (f32[8,128]{1,0:T(8,128)S(1)}, f32[8,128]{1,0:T(8,128)S(1)}, u32[]{:S(2)}, u32[]{:S(2)}) collective-permute-start(f32[8,128]{1,0:T(8,128)S(1)} %get-tuple-element.15), channel_id=1, source_target_pairs={{0,1},{1,2},{2,3},{3,4},{4,5},{5,6},{6,7},{7,8},{8,9},{9,10},{10,1... | collective-permute-start | bytes 12296 | tf_op jit(solution)/shard_map/ppermute | solution.py:346
  106.9 18.1 %all-to-all-start.4 = ((f32[32,1,128]{2,1,0:T(1,128)}), f32[32,1,128]{2,1,0:T(1,128)S(1)}, u32[]{:S(2)}, u32[]{:S(2)}) async-start(f32[32,1,128]{2,1,0:T(1,128)} %shard_map.102), calls=%async_computation.4 | async-start | bytes 32768 | tf_op jit(solution)/shard_map/all_to_all | solution.py:363

commit v3 on v2

--- a/solution.py
+++ b/solution.py
@@ -34,26 +34,11 @@
     )
 
 
-def pieces(x):
-    first = x.astype(bf16).astype(f32)
-    rest = x - first
-    second = rest.astype(bf16).astype(f32)
-    return first, second, rest - second
-
-
-def pack_kernel(
-    copy_ref, ens_hbm, depth_hbm, mask_hbm, fric_hbm, head_ref, tail_ref, idx_ref,
-    ens_ref, depth_ref, mask_ref, fric_ref, rows, seen, sems,
-):
-    columns = depth_ref.shape[0]
-    fetches = [
-        pltpu.make_async_copy(src, dst, sems.at[k])
-        for k, (src, dst) in enumerate(
-            ((ens_hbm, ens_ref), (depth_hbm, depth_ref), (mask_hbm, mask_ref), (fric_hbm, fric_ref))
-        )
-    ]
-    for fetch in fetches:
-        fetch.start()
+def pack_kernel(copy_ref, ens_hbm, out_ref, idx_ref, ens_ref, seen, sem):
+    lat = ens_ref.shape[-1]
+    blocks = out_ref.shape[0]
+    fetch = pltpu.make_async_copy(ens_hbm, ens_ref, sem)
+    fetch.start()
     for p in range(32):
         seen[p] = 0
     for s in range(32):
@@ -70,23 +55,55 @@
     for s in range(32):
         idx_ref[DISTINCT + s] = seen[copy_ref[s]]
 
-    for fetch in fetches:
-        fetch.wait()
-    depth3 = pieces(depth_ref[...])
-    fric3 = pieces(fric_ref[...])
+    row = lax.broadcasted_iota(jnp.int32, (16 * blocks, lat), 0)
+    lane = lax.broadcasted_iota(jnp.int32, (16 * blocks, lat), 1)
+    beside = row % 16
+    source = (row // 16) * LANES + jnp.where(beside < HALO, beside - HALO, beside - HALO + LANES)
+    pick = jnp.where((source == lane) & (beside < 2 * HALO), 1.0, 0.0).astype(bf16)
+    fetch.wait()
+    x = jnp.concatenate([ens_ref[p, f] for p in range(2) for f in range(3)], axis=0)
+    halos = lax.dot_general(pick, x, (((1,), (1,)), ((), ())), preferred_element_type=f32)
+    n = x.shape[0]
+    halos = jnp.concatenate([halos, jnp.zeros((16 * blocks, LANES - n), f32)], axis=1).astype(bf16)
+    for b in range(blocks):
+        out_ref[b, 0:n, :] = x[:, b * LANES : (b + 1) * LANES]
+        out_ref[b, n : n + 16, :] = halos[16 * b : 16 * b + 16, :]
+
+
+def static_kernel(depth_ref, mask_ref, fric_ref, head_ref, tail_ref):
+    columns = depth_ref.shape[0]
     wet = jnp.where(mask_ref[...] == 1, 1.0, 0.0).astype(f32)
     for out, lo, near2, near1 in (
         (head_ref, 0, 0, 0),
         (tail_ref, columns - HALO, columns - 2, columns - 1),
     ):
-        for p in range(2):
+        out[0:3, :] = depth_ref[lo : lo + HALO, :]
+        out[3:5, :] = wet[near2 : near2 + 2, :]
+        out[5:6, :] = fric_ref[near1 : near1 + 1, :]
+        out[6:8, :] = jnp.zeros((2, wet.shape[1]), f32)
+
+
+def select_kernel(idx_ref, all_ref, fields_ref, head_ref, tail_ref, rows):
+    columns = fields_ref.shape[1] // 3
+    part = 3 * columns
+    h = lax.broadcasted_iota(jnp.int32, (16, LANES), 0)
+    lane = lax.broadcasted_iota(jnp.int32, (16, LANES), 1)
+    target = jnp.where(h < HALO, h + LANES - HALO, h - HALO)
+    place = jnp.where((target == lane) & (h < 2 * HALO), 1.0, 0.0).astype(bf16)
+    for i in range(DISTINCT):
+        particle = idx_ref[i]
+        src, p = particle // 2, particle % 2
+        main = all_ref[src, pl.ds(pl.multiple_of(p * part, 16), part), :]
+        halos = all_ref[src, 2 * part : 2 * part + 16, :]
+        tile = lax.dot_general(halos, place, (((0,), (0,)), ((), ())), preferred_element_type=f32)
+        fields_ref[i, :, :LANES] = main.astype(f32)
+        fields_ref[i, :, LANES:] = jnp.where(p == 0, tile[:part], tile[part : 2 * part])
+    for out, lo in ((head_ref, 0), (tail_ref, columns - HALO)):
+        rows[...] = jnp.zeros(rows.shape, f32)
+        for i in range(DISTINCT):
             for f in range(3):
-                at = (p * 3 + f) * HALO
-                rows[at : at + HALO, :] = ens_ref[p, f].astype(f32)[lo : lo + HALO, :]
-        for k in range(3):
-            rows[18 + 3 * k : 21 + 3 * k, :] = depth3[k][lo : lo + HALO, :]
-            rows[29 + k : 30 + k, :] = fric3[k][near1 : near1 + 1, :]
-        rows[27:29, :] = wet[near2 : near2 + 2, :]
+                at = (i * 3 + f) * HALO
+                rows[at : at + HALO, :] = fields_ref[i, f * columns + lo : f * columns + lo + HALO, :]
         out[...] = rows[...].astype(bf16)
 
 
@@ -95,67 +112,71 @@
 
 
 def north(x):
-    n = x.shape[1]
-    lane = lax.broadcasted_iota(jnp.int32, x.shape, 1)
-    up = jnp.where(lane == n - 1, 0.0, pltpu.roll(x, n - 1, 1))
-    down = jnp.where(lane == 0, 0.0, pltpu.roll(x, 1, 1))
-    return 0.5 * (up - down)
-
-
-def source_kernel(
-    ens_ref, left_ref, right_ref, depth_ref, mask_ref, fric_ref, cor_ref, obs_ref,
-    out_ref, ext, lrows, rrows, sdepth, swet, sfric,
+    return 0.5 * (pltpu.roll(x, x.shape[1] - 1, 1) - pltpu.roll(x, 1, 1))
+
+
+def widened(ref, b, blocks):
+    main = block_of(ref, b)
+    after = block_of(ref, jnp.minimum(b + 1, blocks - 1))
+    before = block_of(ref, jnp.maximum(b - 1, 0))
+    lane = lax.broadcasted_iota(jnp.int32, main.shape, 1)
+    zero = jnp.zeros_like(main)
+    after = jnp.where(b < blocks - 1, after, zero)
+    before = jnp.where(b > 0, before, zero)
+    return jnp.concatenate([main, jnp.where(lane < LANES // 2, after, before)], axis=1)
+
+
+def step_kernel(
+    fields_ref, left_ref, right_ref, depth_ref, mask_ref, fric_ref, cor_ref, obs_ref,
+    sleft_ref, sright_ref, out_ref, copies_ref, ext, lrows, rrows, statics,
 ):
     columns, lat = depth_ref.shape
     blocks = lat // LANES
     lo, hi = 8, 8 + columns
+    me = lax.axis_index("member")
     lrows[...] = left_ref[...].astype(f32)
     rrows[...] = right_ref[...].astype(f32)
-
-    def three(rows, at, n, step):
-        a, b, c = (rows[at + step * k : at + step * k + n, :] for k in range(3))
-        return (a + b) + c
-
-    for ref in (sdepth, swet, sfric):
-        ref[0:8, :] = jnp.zeros((8, lat), f32)
-        ref[hi : hi + 8, :] = jnp.zeros((8, lat), f32)
-    sdepth[lo:hi, :] = depth_ref[...]
-    sdepth[lo - 3 : lo, :] = three(lrows, 18, 3, 3)
-    sdepth[hi : hi + 3, :] = three(rrows, 18, 3, 3)
-    swet[lo:hi, :] = jnp.where(mask_ref[...] == 1, 1.0, 0.0).astype(f32)
-    swet[lo - 2 : lo, :] = lrows[27:29, :]
-    swet[hi : hi + 2, :] = rrows[27:29, :]
-    sfric[lo:hi, :] = fric_ref[...]
-    sfric[lo - 1 : lo, :] = three(lrows, 29, 1, 1)
-    sfric[hi : hi + 1, :] = three(rrows, 29, 1, 1)
-    depth = sdepth[...]
-    wet = swet[...]
-    damped = wet * (1.0 / (1.0 + time_step * sfric[...]))
-    turning = cor_ref[...]
-
-    for p in range(2):
+    ext[...] = jnp.zeros(ext.shape, f32)
+    statics[...] = jnp.zeros(statics.shape, f32)
+    sleft = widened(sleft_ref, me, blocks)
+    sright = widened(sright_ref, me, blocks)
+    statics[0, lo:hi, :] = widened(depth_ref, me, blocks)
+    statics[0, lo - 3 : lo, :] = sleft[0:3, :]
+    statics[0, hi : hi + 3, :] = sright[0:3, :]
+    statics[1, lo:hi, :] = jnp.where(widened(mask_ref, me, blocks) == 1, 1.0, 0.0).astype(f32)
+    statics[1, lo - 2 : lo, :] = sleft[3:5, :]
+    statics[1, hi : hi + 2, :] = sright[3:5, :]
+    statics[2, lo:hi, :] = widened(fric_ref, me, blocks)
+    statics[2, lo - 1 : lo, :] = sleft[5:6, :]
+    statics[2, hi : hi + 1, :] = sright[5:6, :]
+    depth = statics[0]
+    wet = statics[1]
+    damped = wet * (1.0 / (1.0 + time_step * statics[2]))
+    turning = widened(cor_ref, me, blocks)
+    obs = block_of(obs_ref, me)
+
+    for i in range(DISTINCT):
         fields = []
         for f in range(3):
-            at = (p * 3 + f) * HALO
-            ext[f, 0:8, :] = jnp.zeros((8, lat), f32)
-            ext[f, hi : hi + 8, :] = jnp.zeros((8, lat), f32)
-            ext[f, lo:hi, :] = ens_ref[p, f].astype(f32)
+            at = (i * 3 + f) * HALO
+            ext[f, lo:hi, :] = fields_ref[i, f * columns : (f + 1) * columns, :]
             ext[f, lo - HALO : lo, :] = lrows[at : at + HALO, :]
             ext[f, hi : hi + HALO, :] = rrows[at : at + HALO, :]
             fields.append(ext[f])
         height, zonal, meridional = fields
         fresh = height - time_step * wet * (east(depth * zonal) + north(depth * meridional))
-        innov = obs_ref[...] - fresh[lo:hi, :]
-        for b in range(blocks):
-            out_ref[b, p, 0] = innov[:, b * LANES : (b + 1) * LANES]
+        innov = obs - fresh[lo:hi, :LANES]
+        out_ref[i, 0] = innov
+        b = innov.astype(bf16)
+        for d in range(copies_ref.shape[0]):
+            copies_ref[d, i * columns : (i + 1) * columns, :] = b
         zonal1 = damped * (zonal + time_step * (turning * meridional - east(fresh)))
         meridional1 = damped * (meridional - time_step * (turning * zonal + north(fresh)))
         change = -time_step * wet * (east(depth * zonal1) + north(depth * meridional1))
         zonal_part = damped * (zonal1 + time_step * (turning * meridional1))
         meridional_part = damped * (meridional1 - time_step * (turning * zonal1))
         for k, value in enumerate((change, zonal_part, meridional_part)):
-            for b in range(blocks):
-                out_ref[b, p, k + 1] = value[lo:hi, b * LANES : (b + 1) * LANES]
+            out_ref[i, k + 1] = value[lo:hi, :LANES]
 
 
 def split_kernel(spread_ref, out_ref):
@@ -163,15 +184,6 @@
     high = s.astype(bf16)
     out_ref[0] = high
     out_ref[1] = (s - high.astype(f32)).astype(bf16)
-
-
-def select_kernel(idx_ref, all_ref, copies_ref):
-    columns = all_ref.shape[2]
-    for i in range(DISTINCT):
-        v = all_ref[idx_ref[i], 0]
-        b = v.astype(bf16)
-        for d in range(copies_ref.shape[0]):
-            copies_ref[d, i * columns : (i + 1) * columns, :] = b
 
 
 def spread_dot(gathered_ref, spread_ref):
@@ -192,7 +204,7 @@
 
 
 def update_kernel(
-    idx_ref, gathered_ref, spread_ref, all_ref, mask_ref, obs_ref,
+    gathered_ref, spread_ref, all_ref, mask_ref, obs_ref,
     innov_ref, copies_ref, edge_ref,
 ):
     columns = mask_ref.shape[0]
@@ -201,9 +213,9 @@
     obs = block_of(obs_ref, me)
     spreaded = spread_dot(gathered_ref, spread_ref)
     for i in range(DISTINCT):
-        innov = all_ref[idx_ref[i], 0]
+        innov = all_ref[i, 0]
         sp = spreaded[i * columns : (i + 1) * columns, :]
-        new = innov - nudge_rate * wet * (innov + sp) - all_ref[idx_ref[i], 1]
+        new = innov - nudge_rate * wet * (innov + sp) - all_ref[i, 1]
         innov_ref[i] = new
         b = new.astype(bf16)
         for d in range(copies_ref.shape[0]):
@@ -249,9 +261,8 @@
         easterly = jnp.where(
             row == columns - 1, right_ref[i : i + 1, :], pltpu.roll(fresh, columns - 1, 0)
         )
-        src = idx_ref[i]
-        state[i, 1] = all_ref[src, 2] - damped * (time_step * 0.5 * (easterly - west))
-        state[i, 2] = all_ref[src, 3] - damped * (time_step * 0.5 * (up - down))
+        state[i, 1] = all_ref[i, 2] - damped * (time_step * 0.5 * (easterly - west))
+        state[i, 2] = all_ref[i, 3] - damped * (time_step * 0.5 * (up - down))
     for s in range(32):
         out_ref[s // 2, s % 2] = state[idx_ref[DISTINCT + s]]
 
@@ -294,42 +305,60 @@
     def swap(x):
         return lax.all_to_all(x, "member", 0, 0, tiled=True)
 
-    head, tail, idx = call(
+    packed, idx = call(
         pack_kernel,
-        (shape((32, lat), bf16), shape((32, lat), bf16), shape((64,), jnp.int32)),
-        [SMEM, ANY, ANY, ANY, ANY],
-        (VMEM, VMEM, SMEM),
+        (shape((blocks, 6 * columns + 16, LANES), bf16), shape((64,), jnp.int32)),
+        [SMEM, ANY],
+        (VMEM, SMEM),
         [
             pltpu.VMEM(ensemble.shape, bf16),
-            pltpu.VMEM(depth.shape, f32),
-            pltpu.VMEM(depth.shape, jnp.int32),
-            pltpu.VMEM(depth.shape, f32),
-            pltpu.VMEM((32, lat), f32),
             pltpu.SMEM((32,), jnp.int32),
-            pltpu.SemaphoreType.DMA((4,)),
+            pltpu.SemaphoreType.DMA(()),
         ],
         limit=60,
-    )(copy_list, ensemble, depth, land_mask, friction)
-    left = lax.ppermute(tail, "lon", eastward)
-    right = lax.ppermute(head, "lon", westward)
+    )(copy_list, ensemble)
+    packed = swap(packed)
+    shead, stail = call(
+        static_kernel, (shape((8, lat), f32),) * 2, [VMEM] * 3, (VMEM, VMEM)
+    )(depth, land_mask, friction)
+    sleft = lax.ppermute(stail, "lon", eastward)
+    sright = lax.ppermute(shead, "lon", westward)
     parts = call(
         split_kernel, shape((2,) + spread.shape, bf16), [VMEM], VMEM
     )(spread)
-
+    halo_rows = -(-DISTINCT * 3 * HALO // 16) * 16
+    fields, head, tail = call(
+        select_kernel,
+        (
+            shape((DISTINCT, 3 * columns, 2 * LANES), f32),
+            shape((halo_rows, 2 * LANES), bf16),
+            shape((halo_rows, 2 * LANES), bf16),
+        ),
+        [SMEM, VMEM],
+        (VMEM, VMEM, VMEM),
+        [pltpu.VMEM((halo_rows, 2 * LANES), f32)],
+    )(idx, packed)
+    left = lax.ppermute(tail, "lon", eastward)
+    right = lax.ppermute(head, "lon", westward)
     ext_rows = columns + 16
-    step1 = call(
-        source_kernel,
-        shape((blocks, 2, 4, columns, LANES), f32),
-        [VMEM] * 8,
-        VMEM,
-        [pltpu.VMEM((3, ext_rows, lat), f32)]
-        + [pltpu.VMEM((32, lat), f32)] * 2
-        + [pltpu.VMEM((ext_rows, lat), f32)] * 3,
-    )(ensemble, left, right, depth, land_mask, friction, coriolis[None, :], observed)
-    step1 = swap(step1).reshape(2 * members, 4, columns, LANES)
-    copies = call(
-        select_kernel, shape((members, rows, LANES), bf16), [SMEM, VMEM], VMEM
-    )(idx, step1)
+    step1, copies = call(
+        step_kernel,
+        (
+            shape((DISTINCT, 4, columns, LANES), f32),
+            shape((members, rows, LANES), bf16),
+        ),
+        [VMEM] * 10,
+        (VMEM, VMEM),
+        [
+            pltpu.VMEM((3, ext_rows, 2 * LANES), f32),
+            pltpu.VMEM((halo_rows, 2 * LANES), f32),
+            pltpu.VMEM((halo_rows, 2 * LANES), f32),
+            pltpu.VMEM((3, ext_rows, 2 * LANES), f32),
+        ],
+    )(
+        fields, left, right, depth, land_mask, friction, coriolis[None, :], observed,
+        sleft, sright,
+    )
     gathered1 = swap(copies)
     innov2, copies, edges = call(
         update_kernel,
@@ -338,10 +367,10 @@
             shape((members, rows, LANES), bf16),
             shape((2, DISTINCT, LANES), f32),
         ),
-        [SMEM] + [VMEM] * 5,
+        [VMEM] * 5,
         (VMEM, VMEM, VMEM),
         flops=2 * 2 * rows * LANES * lat,
-    )(idx, gathered1, parts, step1, land_mask, observed)
+    )(gathered1, parts, step1, land_mask, observed)
     gathered2 = swap(copies)
     left = lax.ppermute(edges[1], "lon", eastward)
     right = lax.ppermute(edges[0], "lon", westward)

time: 126 us -> 116 us (0.921)
  blocking collectives: 40.4 us -> 19.4 us
  starting transfers between devices: 40.5 us -> 56.3 us
  local copies, waits for them, and re-layouts: 3.49 us -> 0.04 us
    all_to_all x2 -> x1, blocking collectives: 40.4 us -> 19.4 us  [swap(): return lax.all_to_all(x, 'member', 0, 0, tiled=True)]
    all_to_all x2 -> x3, starting transfers between devices: 9.4 us -> 21.5 us  [swap(): return lax.all_to_all(x, 'member', 0, 0, tiled=True)]
    ppermute x0 -> x2, starting transfers between devices: none -> 12 us  [the longest x1 10.1 us: per_device(): sright = lax.ppermute(shead, 'lon', westward)]
    ppermute x1, starting transfers between devices: 12.1 us -> 7.02 us  [per_device(): right = lax.ppermute(head, 'lon', westward)]
    unnamed x16 -> x14, local copies, waits for them, and re-layouts: 3.49 us -> 0.04 us
    ppermute x1, starting transfers between devices: 4.37 us -> 1.92 us  [per_device(): left = lax.ppermute(tail, 'lon', eastward)]
    ppermute x1, waiting for transfers between devices: 1.49 us -> 0.01 us  [per_device(): left = lax.ppermute(tail, 'lon', eastward)]
    all_to_all x2 -> x3, waiting for transfers between devices: 8.32 us -> 9.47 us  [swap(): return lax.all_to_all(x, 'member', 0, 0, tiled=True)]
  transfers between devices with their start and end apart: 7 -> 10, of which waited for: 5 -> 4; matrix products, arithmetic and copies ran while one was open for 0% -> 0% of each run, Pallas kernels for 1% -> 2%
where the time goes in v3:
time: 116 us
  starting transfers between devices  56.3 us (49%)
  waiting for transfers between devices  29.1 us (25%)
  blocking collectives  19.4 us (17%)
  Pallas kernels  9.26 us (8%)
    all_to_all x3, starting transfers between devices, swap(): return lax.all_to_all(x, 'member', 0, 0, tiled=True)  21.5 us
    all_to_all x1, blocking collectives, swap(): return lax.all_to_all(x, 'member', 0, 0, tiled=True)  19.4 us
    all_to_all x1, waiting for transfers between devices, per_device(): sums = lax.all_to_all(sums, 'lon', 0, 0, tiled=True)  12.6 us
    ppermute x1, starting transfers between devices, per_device(): sright = lax.ppermute(shead, 'lon', westward)  10.1 us
    all_to_all x3, waiting for transfers between devices, swap(): return lax.all_to_all(x, 'member', 0, 0, tiled=True)  9.47 us
    ppermute x1, starting transfers between devices, per_device(): right = lax.ppermute(edges[0], 'lon', westward)  8.18 us
    ppermute x1, starting transfers between devices, per_device(): right = lax.ppermute(head, 'lon', westward)  7.02 us
    ppermute x1, waiting for transfers between devices, per_device(): left = lax.ppermute(edges[1], 'lon', eastward)  6.03 us
  transfers between devices with their start and end apart: 10, of which 4 were waited for; matrix products, arithmetic and copies ran while one was open for 0% of the time, Pallas kernels for 2%

profile of v3, /device:TPU:1, one launch (start us, length us, event | category | flops | bytes accessed | tf_op | source)
XLA Modules:
  0.0 115.6 jit_solution(13889586386995060780)
XLA Ops:
  0.6 2.9 %shard_map.95 = (bf16[16,112,128]{2,1,0:T(8,128)(2,1)}, s32[64]{0:T(128)}) custom-call(s32[32]{0:T(128)} %copy_ref.1, bf16[2,3,16,2048]{3,2,1,0:T(8,128)(2,1)} %ens_hbm.1), custom_call_target="tpu_custom_call" | custom-call | flops 1000000 | bytes 1000000 | tf_op jit(solution)/shard_map/pallas_call | solution.py:308
  3.6 10.4 %all-to-all-start = ((bf16[16,112,128]{2,1,0:T(8,128)(2,1)}), bf16[16,112,128]{2,1,0:T(8,128)(2,1)S(1)}, u32[]{:S(2)}, u32[]{:S(2)}) async-start(bf16[16,112,128]{2,1,0:T(8,128)(2,1)} %get-tuple-element.15), calls=%async_computation | async-start | bytes 917504 | tf_op jit(solution)/shard_map/all_to_all | solution.py:306
  14.0 1.9 %collective-permute-start.2 = (f32[8,2048]{1,0:T(8,128)S(1)}, f32[8,2048]{1,0:T(8,128)S(1)}, u32[]{:S(2)}, u32[]{:S(2)}) collective-permute-start(f32[8,2048]{1,0:T(8,128)S(1)} %get-tuple-element.19), channel_id=1, source_target_pairs={{0,1},{1,2},{2,3},{3,4},{4,5},{5,6},{6,7},{7,8},{8,9},{9,10},{10,1... | collective-permute-start | bytes 196616 | tf_op jit(solution)/shard_map/ppermute | solution.py:324
  15.9 10.1 %collective-permute-start.3 = (f32[8,2048]{1,0:T(8,128)S(1)}, f32[8,2048]{1,0:T(8,128)S(1)}, u32[]{:S(2)}, u32[]{:S(2)}) collective-permute-start(f32[8,2048]{1,0:T(8,128)S(1)} %get-tuple-element.20), channel_id=1, source_target_pairs={{1,0},{2,1},{3,2},{4,3},{5,4},{6,5},{7,6},{8,7},{9,8},{10,9},{11,1... | collective-permute-start | bytes 196616 | tf_op jit(solution)/shard_map/ppermute | solution.py:325
  26.1 0.9 shard_map.96
  26.9 1.9 %collective-permute-start = (bf16[80,256]{1,0:T(8,128)(2,1)S(1)}, bf16[80,256]{1,0:T(8,128)(2,1)S(1)}, u32[]{:S(2)}, u32[]{:S(2)}) collective-permute-start(bf16[80,256]{1,0:T(8,128)(2,1)S(1)} %get-tuple-element.17), channel_id=1, source_target_pairs={{0,1},{1,2},{2,3},{3,4},{4,5},{5,6},{6,7},{7,8},{8,9},{9,10},{10,1... | collective-permute-start | bytes 122888 | tf_op jit(solution)/shard_map/ppermute | solution.py:341
  28.9 7.0 %collective-permute-start.1 = (bf16[80,256]{1,0:T(8,128)(2,1)S(1)}, bf16[80,256]{1,0:T(8,128)(2,1)S(1)}, u32[]{:S(2)}, u32[]{:S(2)}) collective-permute-start(bf16[80,256]{1,0:T(8,128)(2,1)S(1)} %get-tuple-element.18), channel_id=1, source_target_pairs={{1,0},{2,1},{3,2},{4,3},{5,4},{6,5},{7,6},{8,7},{9,8},{10,9},{11,1... | collective-permute-start | bytes 122888 | tf_op jit(solution)/shard_map/ppermute | solution.py:342
  35.9 1.0 collective-permute-done.1.right_ref
  37.0 1.3 %shard_map.98 = (f32[8,4,16,128]{3,2,1,0:T(8,128)S(1)}, bf16[16,128,128]{2,1,0:T(8,128)(2,1)}) custom-call(f32[8,48,256]{2,1,0:T(8,128)S(1)} %get-tuple-element.16.fields_ref, bf16[80,256]{1,0:T(8,128)(2,1)S(1)} %collective-permute-done.left_ref, bf16[80,256]{1,0:T(8,128)(2,1)S(1)} %collective-permute-done.1.right_ref, f32[16,2048]{1,0:T(8,128)S(1)} %copy-done.4, ...), custom_call_target="tpu_custom_call" | custom-call | flops 1000000 | bytes 1000000 | tf_op jit(solution)/shard_map/pallas_call | solution.py:344
  38.3 6.5 %all-to-all-start.1 = ((bf16[16,128,128]{2,1,0:T(8,128)(2,1)}), bf16[16,128,128]{2,1,0:T(8,128)(2,1)S(1)}, u32[]{:S(2)}, u32[]{:S(2)}) async-start(bf16[16,128,128]{2,1,0:T(8,128)(2,1)} %get-tuple-element.21), calls=%async_computation.1 | async-start | bytes 1048576 | tf_op jit(solution)/shard_map/all_to_all | solution.py:306
  44.7 0.2 shard_map.99.spread_ref
  44.9 9.5 %all-to-all-done.1.gathered_ref = bf16[16,128,128]{2,1,0:T(8,128)(2,1)S(1)} async-done(((bf16[16,128,128]{2,1,0:T(8,128)(2,1)}), bf16[16,128,128]{2,1,0:T(8,128)(2,1)S(1)}, u32[]{:S(2)}, u32[]{:S(2)}) %all-to-all-start.1) | async-done | bytes 524320 | tf_op jit(solution)/shard_map/all_to_all | solution.py:306
  54.4 1.3 %shard_map.100 = (f32[8,16,128]{2,1,0:T(8,128)S(1)}, bf16[16,128,128]{2,1,0:T(8,128)(2,1)}, f32[2,8,128]{2,1,0:T(8,128)S(1)}) custom-call(bf16[16,128,128]{2,1,0:T(8,128)(2,1)S(1)} %all-to-all-done.1.gathered_ref, bf16[2,128,2048]{2,1,0:T(8,128)(2,1)S(1)} %shard_map.99.spread_ref, f32[8,4,16,128]{3,2,1,0:T(8,128)S(1)} %get-tuple-element.22.all_ref, ...), custom_call_target="tpu_custom_call" | custom-call | flops 134217728 | bytes 1000000 | tf_op jit(solution)/shard_map/pallas_call | solution.py:363
  55.6 4.7 %all-to-all-start.2 = ((bf16[16,128,128]{2,1,0:T(8,128)(2,1)}), bf16[16,128,128]{2,1,0:T(8,128)(2,1)S(1)}, u32[]{:S(2)}, u32[]{:S(2)}) async-start(bf16[16,128,128]{2,1,0:T(8,128)(2,1)} %get-tuple-element.23), calls=%async_computation.2 | async-start | bytes 1048576 | tf_op jit(solution)/shard_map/all_to_all | solution.py:306
  60.3 8.2 %collective-permute-start.5 = (f32[8,128]{1,0:T(8,128)S(1)}, f32[8,128]{1,0:T(8,128)S(1)}, u32[]{:S(2)}, u32[]{:S(2)}) collective-permute-start(f32[8,128]{1,0:T(8,128)S(1)} %get-tuple-element.26), channel_id=1, source_target_pairs={{1,0},{2,1},{3,2},{4,3},{5,4},{6,5},{7,6},{8,7},{9,8},{10,9},{11,1... | collective-permute-start | bytes 12296 | tf_op jit(solution)/shard_map/ppermute | solution.py:376
  68.5 1.9 %collective-permute-start.4 = (f32[8,128]{1,0:T(8,128)S(1)}, f32[8,128]{1,0:T(8,128)S(1)}, u32[]{:S(2)}, u32[]{:S(2)}) collective-permute-start(f32[8,128]{1,0:T(8,128)S(1)} %get-tuple-element.27), channel_id=1, source_target_pairs={{0,1},{1,2},{2,3},{3,4},{4,5},{5,6},{6,7},{7,8},{8,9},{9,10},{10,1... | collective-permute-start | bytes 12296 | tf_op jit(solution)/shard_map/ppermute | solution.py:375
  70.5 6.0 %collective-permute-done.4.left_ref = f32[8,128]{1,0:T(8,128)S(1)} collective-permute-done((f32[8,128]{1,0:T(8,128)S(1)}, f32[8,128]{1,0:T(8,128)S(1)}, u32[]{:S(2)}, u32[]{:S(2)}) %collective-permute-start.4) | collective-permute-done | bytes 4128 | tf_op jit(solution)/shard_map/ppermute | solution.py:375
  76.5 1.0 shard_map.101
  77.5 19.4 %all_to_all.25.state_ref.h_ref = f32[16,2,3,16,128]{4,3,2,1,0:T(8,128)S(1)} all-to-all(f32[16,2,3,16,128]{4,3,2,1,0:T(8,128)S(1)} %shard_map.101), channel_id=1, replica_groups=mesh['member'=16,'lon'=32] {'member'}, dimensions={0} | all-to-all | bytes 1572864 | tf_op jit(solution)/shard_map/all_to_all | solution.py:306
  96.9 0.8 shard_map.103
  97.7 3.8 %all-to-all-start.4 = ((f32[32,1,128]{2,1,0:T(1,128)}), f32[32,1,128]{2,1,0:T(1,128)S(1)}, u32[]{:S(2)}, u32[]{:S(2)}) async-start(f32[32,1,128]{2,1,0:T(1,128)} %shard_map.103), calls=%async_computation.4 | async-start | bytes 32768 | tf_op jit(solution)/shard_map/all_to_all | solution.py:392
  101.5 0.9 shard_map.102
  102.5 12.6 %all-to-all-done.4 = f32[32,1,128]{2,1,0:T(1,128)S(1)} async-done(((f32[32,1,128]{2,1,0:T(1,128)}), f32[32,1,128]{2,1,0:T(1,128)S(1)}, u32[]{:S(2)}, u32[]{:S(2)}) %all-to-all-start.4) | async-done | bytes 16416 | tf_op jit(solution)/shard_map/all_to_all | solution.py:392
  115.1 0.5 slice_multiply_fusion
  (23 shorter events, 0.2 us)
Async XLA Ops:
  3.5 10.4 %copy-start = (s32[16,2048]{1,0:T(8,128)S(1)}, s32[16,2048]{1,0:T(8,128)}, u32[]{:S(2)}) copy-start(s32[16,2048]{1,0:T(8,128)} %mask_ref.9) | copy-start | bytes 393220
  3.5 10.4 %copy-start.2 = (f32[16,2048]{1,0:T(8,128)S(1)}, f32[16,2048]{1,0:T(8,128)}, u32[]{:S(2)}) copy-start(f32[16,2048]{1,0:T(8,128)} %fric_ref.5) | copy-start | bytes 393220
  3.5 10.4 %copy-start.4 = (f32[16,2048]{1,0:T(8,128)S(1)}, f32[16,2048]{1,0:T(8,128)}, u32[]{:S(2)}) copy-start(f32[16,2048]{1,0:T(8,128)} %depth_ref.3) | copy-start | bytes 393220
  3.6 22.5 %all-to-all-start = ((bf16[16,112,128]{2,1,0:T(8,128)(2,1)}), bf16[16,112,128]{2,1,0:T(8,128)(2,1)S(1)}, u32[]{:S(2)}, u32[]{:S(2)}) async-start(bf16[16,112,128]{2,1,0:T(8,128)(2,1)} %get-tuple-element.15), calls=%async_computation | async-start | bytes 917504 | tf_op jit(solution)/shard_map/all_to_all | solution.py:306
  14.0 21.9 %collective-permute-start.2 = (f32[8,2048]{1,0:T(8,128)S(1)}, f32[8,2048]{1,0:T(8,128)S(1)}, u32[]{:S(2)}, u32[]{:S(2)}) collective-permute-start(f32[8,2048]{1,0:T(8,128)S(1)} %get-tuple-element.19), channel_id=1, source_target_pairs={{0,1},{1,2},{2,3},{3,4},{4,5},{5,6},{6,7},{7,8},{8,9},{9,10},{10,1... | collective-permute-start | bytes 196616 | tf_op jit(solution)/shard_map/ppermute | solution.py:324
  15.9 10.1 %copy-start.6 = (s32[64]{0:T(128)S(1)}, s32[64]{0:T(128)}, u32[]{:S(2)}) copy-start(s32[64]{0:T(128)} %get-tuple-element.14.idx_ref) | copy-start | bytes 772
  15.9 20.0 %collective-permute-start.3 = (f32[8,2048]{1,0:T(8,128)S(1)}, f32[8,2048]{1,0:T(8,128)S(1)}, u32[]{:S(2)}, u32[]{:S(2)}) collective-permute-start(f32[8,2048]{1,0:T(8,128)S(1)} %get-tuple-element.20), channel_id=1, source_target_pairs={{1,0},{2,1},{3,2},{4,3},{5,4},{6,5},{7,6},{8,7},{9,8},{10,9},{11,1... | collective-permute-start | bytes 196616 | tf_op jit(solution)/shard_map/ppermute | solution.py:325
  26.1 10.9 %copy-start.1 = (f32[16,2048]{1,0:T(8,128)S(1)}, f32[16,2048]{1,0:T(8,128)}, u32[]{:S(2)}) copy-start(f32[16,2048]{1,0:T(8,128)} %obs_ref.7) | copy-start | bytes 393220
  26.1 10.9 %copy-start.5 = (f32[2048]{0:T(1024)S(1)}, f32[2048]{0:T(1024)}, u32[]{:S(2)}) copy-start(f32[2048]{0:T(1024)} %param.13) | copy-start | bytes 24580
  26.9 9.0 %collective-permute-start = (bf16[80,256]{1,0:T(8,128)(2,1)S(1)}, bf16[80,256]{1,0:T(8,128)(2,1)S(1)}, u32[]{:S(2)}, u32[]{:S(2)}) collective-permute-start(bf16[80,256]{1,0:T(8,128)(2,1)S(1)} %get-tuple-element.17), channel_id=1, source_target_pairs={{0,1},{1,2},{2,3},{3,4},{4,5},{5,6},{6,7},{7,8},{8,9},{9,10},{10,1... | collective-permute-start | bytes 122888 | tf_op jit(solution)/shard_map/ppermute | solution.py:341
  28.9 8.1 %collective-permute-start.1 = (bf16[80,256]{1,0:T(8,128)(2,1)S(1)}, bf16[80,256]{1,0:T(8,128)(2,1)S(1)}, u32[]{:S(2)}, u32[]{:S(2)}) collective-permute-start(bf16[80,256]{1,0:T(8,128)(2,1)S(1)} %get-tuple-element.18), channel_id=1, source_target_pairs={{1,0},{2,1},{3,2},{4,3},{5,4},{6,5},{7,6},{8,7},{9,8},{10,9},{11,1... | collective-permute-start | bytes 122888 | tf_op jit(solution)/shard_map/ppermute | solution.py:342
  37.0 7.8 %copy-start.3 = (f32[128,2048]{1,0:T(8,128)S(1)}, f32[128,2048]{1,0:T(8,128)}, u32[]{:S(2)}) copy-start(f32[128,2048]{1,0:T(8,128)} %spread_ref.1) | copy-start | bytes 3145732
  38.3 16.1 %all-to-all-start.1 = ((bf16[16,128,128]{2,1,0:T(8,128)(2,1)}), bf16[16,128,128]{2,1,0:T(8,128)(2,1)S(1)}, u32[]{:S(2)}, u32[]{:S(2)}) async-start(bf16[16,128,128]{2,1,0:T(8,128)(2,1)} %get-tuple-element.21), calls=%async_computation.1 | async-start | bytes 1048576 | tf_op jit(solution)/shard_map/all_to_all | solution.py:306
  55.6 20.8 %all-to-all-start.2 = ((bf16[16,128,128]{2,1,0:T(8,128)(2,1)}), bf16[16,128,128]{2,1,0:T(8,128)(2,1)S(1)}, u32[]{:S(2)}, u32[]{:S(2)}) async-start(bf16[16,128,128]{2,1,0:T(8,128)(2,1)} %get-tuple-element.23), calls=%async_computation.2 | async-start | bytes 1048576 | tf_op jit(solution)/shard_map/all_to_all | solution.py:306
  60.3 10.1 %collective-permute-start.5 = (f32[8,128]{1,0:T(8,128)S(1)}, f32[8,128]{1,0:T(8,128)S(1)}, u32[]{:S(2)}, u32[]{:S(2)}) collective-permute-start(f32[8,128]{1,0:T(8,128)S(1)} %get-tuple-element.26), channel_id=1, source_target_pairs={{1,0},{2,1},{3,2},{4,3},{5,4},{6,5},{7,6},{8,7},{9,8},{10,9},{11,1... | collective-permute-start | bytes 12296 | tf_op jit(solution)/shard_map/ppermute | solution.py:376
  68.5 8.0 %collective-permute-start.4 = (f32[8,128]{1,0:T(8,128)S(1)}, f32[8,128]{1,0:T(8,128)S(1)}, u32[]{:S(2)}, u32[]{:S(2)}) collective-permute-start(f32[8,128]{1,0:T(8,128)S(1)} %get-tuple-element.27), channel_id=1, source_target_pairs={{0,1},{1,2},{2,3},{3,4},{4,5},{5,6},{6,7},{7,8},{8,9},{9,10},{10,1... | collective-permute-start | bytes 12296 | tf_op jit(solution)/shard_map/ppermute | solution.py:375
  97.7 17.3 %all-to-all-start.4 = ((f32[32,1,128]{2,1,0:T(1,128)}), f32[32,1,128]{2,1,0:T(1,128)S(1)}, u32[]{:S(2)}, u32[]{:S(2)}) async-start(f32[32,1,128]{2,1,0:T(1,128)} %shard_map.103), calls=%async_computation.4 | async-start | bytes 32768 | tf_op jit(solution)/shard_map/all_to_all | solution.py:392

commit v4 on v0

v4 whole, which is shorter than its diff:
```python
import functools

import jax
import jax.numpy as jnp
from jax import lax
from jax.experimental import pallas as pl
from jax.experimental.pallas import tpu as pltpu
from jax.sharding import PartitionSpec as P

DISTINCT = 8
HALO = 3
EXTRA = 8
SHIFT = 4
LANES = 128
time_step = 0.2
nudge_rate = 0.3
f32 = jnp.float32
bf16 = jnp.bfloat16

VMEM = pl.BlockSpec(memory_space=pltpu.VMEM)
SMEM = pl.BlockSpec(memory_space=pltpu.SMEM)
ANY = pl.BlockSpec(memory_space=pl.ANY)


def call(kernel, out_shape, in_specs, out_specs, scratch=(), flops=1e6, bytes_accessed=1e6, limit=24):
    return pl.pallas_call(
        kernel,
        out_shape=out_shape,
        in_specs=in_specs,
        out_specs=out_specs,
        scratch_shapes=list(scratch),
        compiler_params=pltpu.CompilerParams(vmem_limit_bytes=limit * 1024 * 1024),
        cost_estimate=pl.CostEstimate(
            flops=int(flops), bytes_accessed=int(bytes_accessed), transcendentals=0
        ),
    )


def pack_kernel(ens_hbm, out_ref, ens_ref, sem):
    lat = ens_ref.shape[-1]
    blocks = out_ref.shape[0]
    fetch = pltpu.make_async_copy(ens_hbm, ens_ref, sem)
    fetch.start()
    row = lax.broadcasted_iota(jnp.int32, (16 * blocks, lat), 0)
    lane = lax.broadcasted_iota(jnp.int32, (16 * blocks, lat), 1)
    beside = row % 16
    source = (row // 16) * LANES + jnp.where(beside < HALO, beside - HALO, beside - HALO + LANES)
    pick = jnp.where((source == lane) & (beside < 2 * HALO), 1.0, 0.0).astype(bf16)
    fetch.wait()
    x = jnp.concatenate([ens_ref[p, f] for p in range(2) for f in range(3)], axis=0)
    halos = lax.dot_general(pick, x, (((1,), (1,)), ((), ())), preferred_element_type=f32)
    n = x.shape[0]
    halos = jnp.concatenate([halos, jnp.zeros((16 * blocks, LANES - n), f32)], axis=1).astype(bf16)
    for b in range(blocks):
        out_ref[b, 0:n, :] = x[:, b * LANES : (b + 1) * LANES]
        out_ref[b, n : n + 16, :] = halos[16 * b : 16 * b + 16, :]


def block_of(ref, b):
    return ref[:, pl.ds(pl.multiple_of(b * LANES, LANES), LANES)]


def widened(ref, b, blocks):
    main = block_of(ref, b)
    after = block_of(ref, jnp.minimum(b + 1, blocks - 1))
    before = block_of(ref, jnp.maximum(b - 1, 0))
    lane = lax.broadcasted_iota(jnp.int32, main.shape, 1)
    zero = jnp.zeros_like(main)
    after = jnp.where(b < blocks - 1, after, zero)
    before = jnp.where(b > 0, before, zero)
    return jnp.concatenate([main, jnp.where(lane < LANES // 2, after, before)], axis=1)


def static_kernel(
    copy_ref, depth_ref, mask_ref, fric_ref, obs_ref, cor_ref, spread_ref,
    own_ref, head_ref, turn_ref, split_ref, idx_ref, seen,
):
    for p in range(32):
        seen[p] = 0
    for s in range(32):
        seen[copy_ref[s]] = 1
    for i in range(DISTINCT):
        idx_ref[i] = 0
    count = jnp.int32(0)
    for p in range(32):
        used = seen[p]
        place = jnp.minimum(count, DISTINCT - 1)
        idx_ref[place] = jnp.where(used == 1, p, idx_ref[place])
        seen[p] = place
        count = count + used
    for s in range(32):
        idx_ref[DISTINCT + s] = seen[copy_ref[s]]

    blocks = depth_ref.shape[1] // LANES
    me = lax.axis_index("member")
    wet = jnp.where(widened(mask_ref, me, blocks) == 1, 1.0, 0.0).astype(f32)
    for k, value in enumerate(
        (
            widened(depth_ref, me, blocks),
            wet,
            widened(fric_ref, me, blocks),
            widened(obs_ref, me, blocks),
        )
    ):
        own_ref[k] = value
        head_ref[EXTRA * k : EXTRA * (k + 1), :] = value[:EXTRA, :]
    turn_ref[...] = widened(cor_ref, me, blocks)
    spread = spread_ref[...]
    high = spread.astype(bf16)
    split_ref[0] = high
    split_ref[1] = (spread - high.astype(f32)).astype(bf16)


def select_kernel(idx_ref, all_ref, fields_ref, head_ref, rows):
    columns = fields_ref.shape[1] // 3
    part = 3 * columns
    h = lax.broadcasted_iota(jnp.int32, (16, LANES), 0)
    lane = lax.broadcasted_iota(jnp.int32, (16, LANES), 1)
    target = jnp.where(h < HALO, h + LANES - HALO, h - HALO)
    place = jnp.where((target == lane) & (h < 2 * HALO), 1.0, 0.0).astype(bf16)
    for i in range(DISTINCT):
        particle = idx_ref[i]
        src, p = particle // 2, particle % 2
        main = all_ref[src, pl.ds(pl.multiple_of(p * part, 16), part), :]
        halos = all_ref[src, 2 * part : 2 * part + 16, :]
        tile = lax.dot_general(halos, place, (((0,), (0,)), ((), ())), preferred_element_type=f32)
        fields_ref[i, :, :LANES] = main.astype(f32)
        fields_ref[i, :, LANES:] = jnp.where(p == 0, tile[:part], tile[part : 2 * part])
        for f in range(3):
            at = (i * 3 + f) * EXTRA
            rows[at : at + EXTRA, :] = fields_ref[i, f * columns : f * columns + EXTRA, :]
    head_ref[...] = rows[...].astype(bf16)


def east(x):
    return 0.5 * (pltpu.roll(x, x.shape[0] - 1, 0) - pltpu.roll(x, 1, 0))


def north(x):
    return 0.5 * (pltpu.roll(x, x.shape[1] - 1, 1) - pltpu.roll(x, 1, 1))


def step_kernel(
    fields_ref, right_ref, own_ref, sright_ref, turn_ref,
    out_ref, work_ref, copies_ref, rrows, compact,
):
    columns = own_ref.shape[1]
    width = columns + 2
    keep = slice(SHIFT - 1, SHIFT - 1 + width)
    rrows[...] = right_ref[...].astype(f32)

    def static(k):
        return jnp.concatenate([own_ref[k], sright_ref[EXTRA * k : EXTRA * (k + 1), :]], axis=0)

    depth, wet, friction, obs = (static(k) for k in range(4))
    damped = wet * (1.0 / (1.0 + time_step * friction))
    turning = turn_ref[...]
    for k, value in enumerate((wet, damped, obs)):
        work_ref[k] = value[keep, :]
    for i in range(DISTINCT):
        fields = []
        for f in range(3):
            at = (i * 3 + f) * EXTRA
            fields.append(
                jnp.concatenate(
                    [fields_ref[i, f * columns : (f + 1) * columns, :], rrows[at : at + EXTRA, :]],
                    axis=0,
                )
            )
        height, zonal, meridional = fields
        fresh = height - time_step * wet * (east(depth * zonal) + north(depth * meridional))
        zonal1 = damped * (zonal + time_step * (turning * meridional - east(fresh)))
        meridional1 = damped * (meridional - time_step * (turning * zonal + north(fresh)))
        change = -time_step * wet * (east(depth * zonal1) + north(depth * meridional1))
        zonal_part = damped * (zonal1 + time_step * (turning * meridional1))
        meridional_part = damped * (meridional1 - time_step * (turning * zonal1))
        innov = obs - fresh
        compact[i * width : (i + 1) * width, :] = innov[keep, :LANES]
        for k, value in enumerate((innov, change, zonal_part, meridional_part)):
            out_ref[i, k] = value[keep, :LANES]
    sent = compact[...].astype(bf16)
    for d in range(copies_ref.shape[0]):
        copies_ref[d] = sent


def spread_dot(gathered_ref, spread_ref):
    blocks = gathered_ref.shape[0]
    lhs = jnp.concatenate([gathered_ref[b] for b in range(blocks)], axis=1)
    dims = (((1,), (1,)), ((), ()))
    return lax.dot_general(
        lhs, spread_ref[0], dims, preferred_element_type=f32
    ) + lax.dot_general(lhs, spread_ref[1], dims, preferred_element_type=f32)


def update_kernel(
    gathered_ref, spread_ref, all_ref, work_ref, innov_ref, copies_ref, spreaded, compact
):
    width = work_ref.shape[1]
    wet = work_ref[0, :, :LANES]
    spreaded[...] = spread_dot(gathered_ref, spread_ref)
    for i in range(DISTINCT):
        innov = all_ref[i, 0]
        sp = spreaded[i * width : (i + 1) * width, :]
        new = innov - nudge_rate * wet * (innov + sp) - all_ref[i, 1]
        innov_ref[i] = new
        compact[i * width : (i + 1) * width, :] = new
    sent = compact[...].astype(bf16)
    for d in range(copies_ref.shape[0]):
        copies_ref[d] = sent


def final_kernel(
    idx_ref, gathered_ref, spread_ref, innov_ref, all_ref, work_ref,
    out_ref, state, sums, spreaded, sides, *, total,
):
    width = work_ref.shape[1]
    columns = width - 2
    blocks = gathered_ref.shape[0]
    me = lax.axis_index("member")
    inner = slice(1, 1 + columns)
    wet = work_ref[0, inner, :LANES]
    damped = work_ref[1, inner, :LANES]
    obs_tile = work_ref[2, inner, LANES:]
    obs = work_ref[2, inner, :LANES]
    before = jnp.maximum(me - 1, 0)
    after = jnp.minimum(me + 1, blocks - 1)
    has_before = jnp.where(me > 0, 1.0, 0.0).astype(f32)
    has_after = jnp.where(me < blocks - 1, 1.0, 0.0).astype(f32)
    lane = lax.broadcasted_iota(jnp.int32, (columns, LANES), 1)
    first = lax.axis_index("lon") * columns + SHIFT
    column = first + lax.broadcasted_iota(jnp.int32, (columns, LANES), 0)
    column = jnp.where(column >= total, column - total, column).astype(f32)
    weight = wet * (1.0 + 2.0 * column / total)
    spreaded[...] = spread_dot(gathered_ref, spread_ref)
    sides[0] = gathered_ref[before].astype(f32)
    sides[1] = gathered_ref[after].astype(f32)
    for i in range(DISTINCT):
        part = slice(i * width + 1, i * width + 1 + columns)
        innov = innov_ref[i, inner, :]
        fresh = obs - innov
        height = fresh + nudge_rate * wet * (innov + spreaded[part, :])
        state[i, 0:columns, :] = height
        gap = obs - height
        sums[i : i + 1, :] = jnp.sum(weight * (gap * gap), axis=0, keepdims=True)
        fresh_before = has_before * (obs_tile - sides[0, part, :])
        fresh_after = has_after * (obs_tile - sides[1, part, :])
        down = jnp.where(lane == 0, pltpu.roll(fresh_before, 1, 1), pltpu.roll(fresh, 1, 1))
        up = jnp.where(
            lane == LANES - 1,
            pltpu.roll(fresh_after, LANES - 1, 1),
            pltpu.roll(fresh, LANES - 1, 1),
        )
        west = work_ref[2, 0:columns, :LANES] - innov_ref[i, 0:columns, :]
        easterly = work_ref[2, 2:width, :LANES] - innov_ref[i, 2:width, :]
        state[i, columns : 2 * columns, :] = all_ref[i, 2, inner, :] - damped * (
            time_step * 0.5 * (easterly - west)
        )
        state[i, 2 * columns : 3 * columns, :] = all_ref[i, 3, inner, :] - damped * (
            time_step * 0.5 * (up - down)
        )
    n = 3 * columns
    for d in range(out_ref.shape[0]):
        out_ref[d, 2 * n : 2 * n + 8, :] = jnp.zeros((8, LANES), f32)
        for p in range(2):
            place = idx_ref[DISTINCT + 2 * d + p]
            out_ref[d, p * n : (p + 1) * n, :] = state[place]
            out_ref[d, 2 * n + p : 2 * n + p + 1, :] = sums[pl.ds(place, 1), :]


def tail_kernel(state_ref, sums_ref, tail_ref, *, columns):
    blocks = state_ref.shape[0]
    n = 6 * columns
    acc = state_ref[0, n : n + 8, :]
    for b in range(1, blocks):
        acc = acc + state_ref[b, n : n + 8, :]
    acc = jnp.sum(acc, axis=1, keepdims=True)
    lane = lax.broadcasted_iota(jnp.int32, (1, LANES), 1)
    row = jnp.where(lane == 0, acc[0:1], jnp.where(lane == 1, acc[1:2], 0.0))
    for d in range(sums_ref.shape[0]):
        sums_ref[d] = row
    for b in range(blocks):
        for k in range(6):
            at = (k + 1) * columns - SHIFT
            tail_ref[k * SHIFT : (k + 1) * SHIFT, b * LANES : (b + 1) * LANES] = state_ref[
                b, at : at + SHIFT, :
            ]


def output_kernel(state_ref, tail_ref, out_ref):
    columns = out_ref.shape[2]
    for b in range(state_ref.shape[0]):
        part = slice(b * LANES, (b + 1) * LANES)
        for p in range(2):
            for f in range(3):
                k = p * 3 + f
                out_ref[p, f, 0:SHIFT, part] = tail_ref[k * SHIFT : (k + 1) * SHIFT, part]
                out_ref[p, f, SHIFT:columns, part] = state_ref[
                    b, k * columns : (k + 1) * columns - SHIFT, :
                ]


def per_device(ensemble, copy_list, depth, land_mask, friction, coriolis, spread, observed):
    columns, lat = depth.shape
    members = lax.axis_size("member")
    lons = lax.axis_size("lon")
    blocks = lat // LANES
    width = columns + 2
    rows = DISTINCT * width
    wide = 2 * LANES
    shape = jax.ShapeDtypeStruct
    eastward = [(i, (i + 1) % lons) for i in range(lons)]
    westward = [((i + 1) % lons, i) for i in range(lons)]

    def swap(x):
        return lax.all_to_all(x, "member", 0, 0, tiled=True)

    packed = call(
        pack_kernel,
        shape((blocks, 6 * columns + 16, LANES), bf16),
        [ANY],
        VMEM,
        [pltpu.VMEM(ensemble.shape, bf16), pltpu.SemaphoreType.DMA(())],
        limit=60,
    )(ensemble)
    packed = swap(packed)
    own, shead, turning, parts, idx = call(
        static_kernel,
        (
            shape((4, columns, wide), f32),
            shape((4 * EXTRA, wide), f32),
            shape((1, wide), f32),
            shape((2,) + spread.shape, bf16),
            shape((64,), jnp.int32),
        ),
        [SMEM] + [VMEM] * 6,
        (VMEM, VMEM, VMEM, VMEM, SMEM),
        [pltpu.SMEM((32,), jnp.int32)],
    )(copy_list, depth, land_mask, friction, observed, coriolis[None, :], spread)
    sright = lax.ppermute(shead, "lon", westward)
    fields, head = call(
        select_kernel,
        (
            shape((DISTINCT, 3 * columns, wide), f32),
            shape((DISTINCT * 3 * EXTRA, wide), bf16),
        ),
        [SMEM, VMEM],
        (VMEM, VMEM),
        [pltpu.VMEM((DISTINCT * 3 * EXTRA, wide), f32)],
    )(idx, packed)
    right = lax.ppermute(head, "lon", westward)
    step1, work, copies = call(
        step_kernel,
        (
            shape((DISTINCT, 4, width, LANES), f32),
            shape((3, width, wide), f32),
            shape((members, rows, LANES), bf16),
        ),
        [VMEM] * 5,
        (VMEM, VMEM, VMEM),
        [
            pltpu.VMEM((DISTINCT * 3 * EXTRA, wide), f32),
            pltpu.VMEM((rows, LANES), f32),
        ],
    )(fields, right, own, sright, turning)
    gathered1 = swap(copies)
    innov2, copies = call(
        update_kernel,
        (
            shape((DISTINCT, width, LANES), f32),
            shape((members, rows, LANES), bf16),
        ),
        [VMEM] * 4,
        (VMEM, VMEM),
        [pltpu.VMEM((rows, LANES), f32)] * 2,
        flops=2 * 2 * rows * LANES * lat,
    )(gathered1, parts, step1, work)
    gathered2 = swap(copies)
    state = call(
        functools.partial(final_kernel, total=columns * lons),
        shape((members, 6 * columns + 8, LANES), f32),
        [SMEM] + [VMEM] * 5,
        VMEM,
        [
            pltpu.VMEM((DISTINCT, 3 * columns, LANES), f32),
            pltpu.VMEM((DISTINCT, LANES), f32),
            pltpu.VMEM((rows, LANES), f32),
            pltpu.VMEM((2, rows, LANES), f32),
        ],
        flops=2 * 2 * rows * LANES * lat,
    )(idx, gathered2, parts, innov2, step1, work)
    state = swap(state)
    sums, tail = call(
        functools.partial(tail_kernel, columns=columns),
        (shape((lons, 1, LANES), f32), shape((6 * SHIFT, lat), f32)),
        [VMEM],
        (VMEM, VMEM),
    )(state)
    sums = lax.all_to_all(sums, "lon", 0, 0, tiled=True)
    tail = lax.ppermute(tail, "lon", eastward)
    misfit = jnp.sum(sums, axis=(0, 1))[:2] / (lat * columns * lons)
    new_state = call(output_kernel, shape((2, 3, columns, lat), f32), [VMEM, VMEM], VMEM)(
        state, tail
    )
    return new_state, misfit


def solution(mesh):
    placed = (
        P("member", None, "lon", None),
        P(),
        P("lon", None),
        P("lon", None),
        P("lon", None),
        P(),
        P("member", None),
        P("lon", None),
    )
    return jax.shard_map(
        per_device,
        mesh=mesh,
        in_specs=placed,
        out_specs=(P("member", None, "lon", None), P("member")),
        check_vma=False,
    )
```

time: 314 us -> 110 us (0.35)
  the two profiles are of different devices: /device:TPU:2 before, /device:TPU:1 now
where the time goes in v4:
time: 110 us
  blocking collectives  47 us (43%)
  starting transfers between devices  32.8 us (30%)
  waiting for transfers between devices  19.6 us (18%)
  Pallas kernels  8.65 us (8%)
    all_to_all x3, blocking collectives, swap(): return lax.all_to_all(x, 'member', 0, 0, tiled=True)  47 us
    all_to_all x1, waiting for transfers between devices, per_device(): sums = lax.all_to_all(sums, 'lon', 0, 0, tiled=True)  10.5 us
    all_to_all x1, starting transfers between devices, swap(): return lax.all_to_all(x, 'member', 0, 0, tiled=True)  10.4 us
    ppermute x1, starting transfers between devices, per_device(): right = lax.ppermute(head, 'lon', westward)  10 us
    all_to_all x1, waiting for transfers between devices, swap(): return lax.all_to_all(x, 'member', 0, 0, tiled=True)  7.11 us
    all_to_all x1, starting transfers between devices, per_device(): sums = lax.all_to_all(sums, 'lon', 0, 0, tiled=True)  6.59 us
    ppermute x1, starting transfers between devices, per_device(): tail = lax.ppermute(tail, 'lon', eastward)  3.14 us
    ppermute x1, starting transfers between devices, per_device(): sright = lax.ppermute(shead, 'lon', westward)  2.66 us
  transfers between devices with their start and end apart: 5, of which 3 were waited for; matrix products, arithmetic and copies ran while one was open for 1% of the time, Pallas kernels for 1%

profile of v4, /device:TPU:1, one launch (start us, length us, event | category | flops | bytes accessed | tf_op | source)
XLA Modules:
  0.0 110.0 jit_solution(4452190053419652848)
XLA Ops:
  0.6 2.3 %shard_map.96 = bf16[16,112,128]{2,1,0:T(8,128)(2,1)} custom-call(bf16[2,3,16,2048]{3,2,1,0:T(8,128)(2,1)} %ens_hbm.1), custom_call_target="tpu_custom_call" | custom-call | flops 1000000 | bytes 1000000 | tf_op jit(solution)/shard_map/pallas_call | solution.py:317
  2.9 0.0 copy-start.1
  3.0 0.0 copy-start.4
  3.0 10.4 %all-to-all-start = ((bf16[16,112,128]{2,1,0:T(8,128)(2,1)}), bf16[16,112,128]{2,1,0:T(8,128)(2,1)S(1)}, u32[]{:S(2)}, u32[]{:S(2)}) async-start(bf16[16,112,128]{2,1,0:T(8,128)(2,1)} %shard_map.96), calls=%async_computation | async-start | bytes 917504 | tf_op jit(solution)/shard_map/all_to_all | solution.py:315
  13.4 0.6 copy-done.6
  14.0 1.4 %shard_map.95 = (f32[4,16,256]{2,1,0:T(8,128)S(1)}, f32[32,256]{1,0:T(8,128)S(1)}, f32[1,256]{1,0:T(1,128)S(1)}, bf16[2,128,2048]{2,1,0:T(8,128)(2,1)S(1)}, s32[64]{0:T(128)S(1)}) custom-call(s32[32]{0:T(128)S(1)} %copy-done.6, f32[16,2048]{1,0:T(8,128)S(1)} %copy-done.1, s32[16,2048]{1,0:T(8,128)S(1)} %copy-done.2, f32[16,2048]{1,0:T(8,128)S(1)} %copy-done.3, ...), custom_call_target="tpu_custom_call" | custom-call | flops 1000000 | bytes 1000000 | tf_op jit(solution)/shard_map/pallas_call | solution.py:326
  15.4 7.1 %all-to-all-done.all_ref = bf16[16,112,128]{2,1,0:T(8,128)(2,1)S(1)} async-done(((bf16[16,112,128]{2,1,0:T(8,128)(2,1)}), bf16[16,112,128]{2,1,0:T(8,128)(2,1)S(1)}, u32[]{:S(2)}, u32[]{:S(2)}) %all-to-all-start) | async-done | bytes 458784 | tf_op jit(solution)/shard_map/all_to_all | solution.py:315
  22.5 0.8 shard_map.97
  23.4 10.0 %collective-permute-start = (bf16[192,256]{1,0:T(8,128)(2,1)S(1)}, bf16[192,256]{1,0:T(8,128)(2,1)S(1)}, u32[]{:S(2)}, u32[]{:S(2)}) collective-permute-start(bf16[192,256]{1,0:T(8,128)(2,1)S(1)} %get-tuple-element.18), channel_id=1, source_target_pairs={{1,0},{2,1},{3,2},{4,3},{5,4},{6,5},{7,6},{8,7},{9,8},{10,9},{11,1... | collective-permute-start | bytes 294920 | tf_op jit(solution)/shard_map/ppermute | solution.py:350
  33.4 2.7 %collective-permute-start.1 = (f32[32,256]{1,0:T(8,128)S(1)}, f32[32,256]{1,0:T(8,128)S(1)}, u32[]{:S(2)}, u32[]{:S(2)}) collective-permute-start(f32[32,256]{1,0:T(8,128)S(1)} %get-tuple-element.20), channel_id=1, source_target_pairs={{1,0},{2,1},{3,2},{4,3},{5,4},{6,5},{7,6},{8,7},{9,8},{10,9},{11,1... | collective-permute-start | bytes 98312 | tf_op jit(solution)/shard_map/ppermute | solution.py:339
  36.0 2.0 %collective-permute-done.1.sright_ref = f32[32,256]{1,0:T(8,128)S(1)} collective-permute-done((f32[32,256]{1,0:T(8,128)S(1)}, f32[32,256]{1,0:T(8,128)S(1)}, u32[]{:S(2)}, u32[]{:S(2)}) %collective-permute-start.1) | collective-permute-done | bytes 32800 | tf_op jit(solution)/shard_map/ppermute | solution.py:339
  38.0 0.8 shard_map.98
  38.8 16.3 %all_to_all.25.gathered_ref = bf16[16,144,128]{2,1,0:T(8,128)(2,1)S(1)} all-to-all(bf16[16,144,128]{2,1,0:T(8,128)(2,1)S(1)} %get-tuple-element.22), channel_id=1, replica_groups=mesh['member'=16,'lon'=32] {'member'}, dimensions={0} | all-to-all | bytes 1179648 | tf_op jit(solution)/shard_map/all_to_all | solution.py:315
  55.2 0.5 shard_map.99
  55.7 14.2 %all_to_all.26.gathered_ref = bf16[16,144,128]{2,1,0:T(8,128)(2,1)S(1)} all-to-all(bf16[16,144,128]{2,1,0:T(8,128)(2,1)S(1)} %get-tuple-element.26), channel_id=1, replica_groups=mesh['member'=16,'lon'=32] {'member'}, dimensions={0} | all-to-all | bytes 1179648 | tf_op jit(solution)/shard_map/all_to_all | solution.py:315
  69.9 1.1 %shard_map.100 = f32[16,104,128]{2,1,0:T(8,128)S(1)} custom-call(s32[64]{0:T(128)S(1)} %get-tuple-element.16.idx_ref, bf16[16,144,128]{2,1,0:T(8,128)(2,1)S(1)} %all_to_all.26.gathered_ref, bf16[2,128,2048]{2,1,0:T(8,128)(2,1)S(1)} %get-tuple-element.23.spread_ref, f32[8,18,128]{2,1,0:T(8,128)S(1)} %get-tuple-element.27.innov_ref, ...), custom_call_target="tpu_custom_call" | custom-call | flops 150994944 | bytes 1000000 | tf_op jit(solution)/shard_map/pallas_call | solution.py:378
  71.0 16.5 %all_to_all.27.state_ref = f32[16,104,128]{2,1,0:T(8,128)S(1)} all-to-all(f32[16,104,128]{2,1,0:T(8,128)S(1)} %shard_map.100), channel_id=1, replica_groups=mesh['member'=16,'lon'=32] {'member'}, dimensions={0} | all-to-all | bytes 1703936 | tf_op jit(solution)/shard_map/all_to_all | solution.py:315
  87.5 0.7 shard_map.101
  88.2 6.6 %all-to-all-start.4 = ((f32[32,1,128]{2,1,0:T(1,128)}), f32[32,1,128]{2,1,0:T(1,128)S(1)}, u32[]{:S(2)}, u32[]{:S(2)}) async-start(f32[32,1,128]{2,1,0:T(1,128)} %get-tuple-element.29), calls=%async_computation.4 | async-start | bytes 32768 | tf_op jit(solution)/shard_map/all_to_all | solution.py:398
  94.8 3.1 %collective-permute-start.2 = (f32[24,2048]{1,0:T(8,128)S(1)}, f32[24,2048]{1,0:T(8,128)S(1)}, u32[]{:S(2)}, u32[]{:S(2)}) collective-permute-start(f32[24,2048]{1,0:T(8,128)S(1)} %get-tuple-element.28), channel_id=1, source_target_pairs={{0,1},{1,2},{2,3},{3,4},{4,5},{5,6},{6,7},{7,8},{8,9},{9,10},{10,1... | collective-permute-start | bytes 589832 | tf_op jit(solution)/shard_map/ppermute | solution.py:399
  97.9 10.5 %all-to-all-done.4 = f32[32,1,128]{2,1,0:T(1,128)S(1)} async-done(((f32[32,1,128]{2,1,0:T(1,128)}), f32[32,1,128]{2,1,0:T(1,128)S(1)}, u32[]{:S(2)}, u32[]{:S(2)}) %all-to-all-start.4) | async-done | bytes 16416 | tf_op jit(solution)/shard_map/all_to_all | solution.py:398
  108.4 0.1 reduce_sum.9
  108.5 0.5 slice_multiply_fusion
  109.0 1.0 shard_map.102
  (13 shorter events, 0.0 us)
Async XLA Ops:
  0.6 12.8 %copy-start = (f32[128,2048]{1,0:T(8,128)S(1)}, f32[128,2048]{1,0:T(8,128)}, u32[]{:S(2)}) copy-start(f32[128,2048]{1,0:T(8,128)} %spread_ref.1) | copy-start | bytes 3145732
  2.9 10.5 %copy-start.1 = (f32[16,2048]{1,0:T(8,128)S(1)}, f32[16,2048]{1,0:T(8,128)}, u32[]{:S(2)}) copy-start(f32[16,2048]{1,0:T(8,128)} %depth_ref.1) | copy-start | bytes 393220
  3.0 10.5 %copy-start.2 = (s32[16,2048]{1,0:T(8,128)S(1)}, s32[16,2048]{1,0:T(8,128)}, u32[]{:S(2)}) copy-start(s32[16,2048]{1,0:T(8,128)} %mask_ref.1) | copy-start | bytes 393220
  3.0 10.5 %copy-start.3 = (f32[16,2048]{1,0:T(8,128)S(1)}, f32[16,2048]{1,0:T(8,128)}, u32[]{:S(2)}) copy-start(f32[16,2048]{1,0:T(8,128)} %fric_ref.1) | copy-start | bytes 393220
  3.0 10.4 %copy-start.4 = (f32[16,2048]{1,0:T(8,128)S(1)}, f32[16,2048]{1,0:T(8,128)}, u32[]{:S(2)}) copy-start(f32[16,2048]{1,0:T(8,128)} %obs_ref.1) | copy-start | bytes 393220
  3.0 10.4 %copy-start.5 = (f32[2048]{0:T(1024)S(1)}, f32[2048]{0:T(1024)}, u32[]{:S(2)}) copy-start(f32[2048]{0:T(1024)} %param.13) | copy-start | bytes 24580
  3.0 19.5 %all-to-all-start = ((bf16[16,112,128]{2,1,0:T(8,128)(2,1)}), bf16[16,112,128]{2,1,0:T(8,128)(2,1)S(1)}, u32[]{:S(2)}, u32[]{:S(2)}) async-start(bf16[16,112,128]{2,1,0:T(8,128)(2,1)} %shard_map.96), calls=%async_computation | async-start | bytes 917504 | tf_op jit(solution)/shard_map/all_to_all | solution.py:315
  13.4 0.7 copy-start.6
  23.4 14.7 %collective-permute-start = (bf16[192,256]{1,0:T(8,128)(2,1)S(1)}, bf16[192,256]{1,0:T(8,128)(2,1)S(1)}, u32[]{:S(2)}, u32[]{:S(2)}) collective-permute-start(bf16[192,256]{1,0:T(8,128)(2,1)S(1)} %get-tuple-element.18), channel_id=1, source_target_pairs={{1,0},{2,1},{3,2},{4,3},{5,4},{6,5},{7,6},{8,7},{9,8},{10,9},{11,1... | collective-permute-start | bytes 294920 | tf_op jit(solution)/shard_map/ppermute | solution.py:350
  33.4 4.7 %collective-permute-start.1 = (f32[32,256]{1,0:T(8,128)S(1)}, f32[32,256]{1,0:T(8,128)S(1)}, u32[]{:S(2)}, u32[]{:S(2)}) collective-permute-start(f32[32,256]{1,0:T(8,128)S(1)} %get-tuple-element.20), channel_id=1, source_target_pairs={{1,0},{2,1},{3,2},{4,3},{5,4},{6,5},{7,6},{8,7},{9,8},{10,9},{11,1... | collective-permute-start | bytes 98312 | tf_op jit(solution)/shard_map/ppermute | solution.py:339
  88.2 20.2 %all-to-all-start.4 = ((f32[32,1,128]{2,1,0:T(1,128)}), f32[32,1,128]{2,1,0:T(1,128)S(1)}, u32[]{:S(2)}, u32[]{:S(2)}) async-start(f32[32,1,128]{2,1,0:T(1,128)} %get-tuple-element.29), calls=%async_computation.4 | async-start | bytes 32768 | tf_op jit(solution)/shard_map/all_to_all | solution.py:398
  94.8 14.2 %collective-permute-start.2 = (f32[24,2048]{1,0:T(8,128)S(1)}, f32[24,2048]{1,0:T(8,128)S(1)}, u32[]{:S(2)}, u32[]{:S(2)}) collective-permute-start(f32[24,2048]{1,0:T(8,128)S(1)} %get-tuple-element.28), channel_id=1, source_target_pairs={{0,1},{1,2},{2,3},{3,4},{4,5},{5,6},{6,7},{7,8},{8,9},{9,10},{10,1... | collective-permute-start | bytes 589832 | tf_op jit(solution)/shard_map/ppermute | solution.py:399

commit v5 on v4

v5 whole, which is shorter than its diff:
```python
import functools

import jax
import jax.numpy as jnp
from jax import lax
from jax.experimental import pallas as pl
from jax.experimental.pallas import tpu as pltpu
from jax.sharding import PartitionSpec as P

DISTINCT = 8
HALO = 3
EXTRA = 8
SHIFT = 4
LANES = 128
time_step = 0.2
nudge_rate = 0.3
f32 = jnp.float32
bf16 = jnp.bfloat16

VMEM = pl.BlockSpec(memory_space=pltpu.VMEM)
SMEM = pl.BlockSpec(memory_space=pltpu.SMEM)
ANY = pl.BlockSpec(memory_space=pl.ANY)


def call(kernel, out_shape, in_specs, out_specs, scratch=(), flops=1e6, bytes_accessed=1e6, limit=24):
    return pl.pallas_call(
        kernel,
        out_shape=out_shape,
        in_specs=in_specs,
        out_specs=out_specs,
        scratch_shapes=list(scratch),
        compiler_params=pltpu.CompilerParams(vmem_limit_bytes=limit * 1024 * 1024),
        cost_estimate=pl.CostEstimate(
            flops=int(flops), bytes_accessed=int(bytes_accessed), transcendentals=0
        ),
    )


def halo_lanes(shape):
    lane = lax.broadcasted_iota(jnp.int32, shape, 1)
    return (lane < HALO) | (lane >= LANES - HALO)


def fold(acc, tile, group):
    lane = lax.broadcasted_iota(jnp.int32, tile.shape, 1)
    at = 2 * HALO * group
    moved = pltpu.roll(tile, at + HALO, 1)
    return jnp.where((lane >= at) & (lane < at + 2 * HALO), moved, acc)


def unfold(acc, group):
    moved = pltpu.roll(acc, LANES - (2 * HALO * group + HALO), 1)
    return jnp.where(halo_lanes(acc.shape), moved, 0.0)


def pack_kernel(ens_hbm, out_ref, ens_ref, sem):
    blocks = out_ref.shape[0]
    columns = ens_ref.shape[2]
    fetch = pltpu.make_async_copy(ens_hbm, ens_ref, sem)
    fetch.start()
    fetch.wait()
    low = lax.broadcasted_iota(jnp.int32, (columns, LANES), 1) < LANES // 2
    zero = jnp.zeros((columns, LANES), f32)
    halos = [zero] * blocks
    for p in range(2):
        for f in range(3):
            k = p * 3 + f
            tiles = [ens_ref[p, f, :, b * LANES : (b + 1) * LANES] for b in range(blocks)]
            wide = [zero] + [t.astype(f32) for t in tiles] + [zero]
            for b in range(blocks):
                out_ref[b, k * columns : (k + 1) * columns, :] = tiles[b]
                halos[b] = fold(halos[b], jnp.where(low, wide[b + 2], wide[b]), k)
    for b in range(blocks):
        out_ref[b, 6 * columns : 7 * columns, :] = halos[b].astype(bf16)


def block_of(ref, b):
    return ref[:, pl.ds(pl.multiple_of(b * LANES, LANES), LANES)]


def widened(ref, b, blocks):
    main = block_of(ref, b)
    after = block_of(ref, jnp.minimum(b + 1, blocks - 1))
    before = block_of(ref, jnp.maximum(b - 1, 0))
    lane = lax.broadcasted_iota(jnp.int32, main.shape, 1)
    zero = jnp.zeros_like(main)
    after = jnp.where(b < blocks - 1, after, zero)
    before = jnp.where(b > 0, before, zero)
    return jnp.concatenate([main, jnp.where(lane < LANES // 2, after, before)], axis=1)


def pieces(x):
    first = x.astype(bf16).astype(f32)
    rest = x - first
    second = rest.astype(bf16).astype(f32)
    return first, second, rest - second


def static_kernel(depth_ref, mask_ref, fric_ref, obs_ref, cor_ref, own_ref, head_ref, turn_ref):
    blocks = depth_ref.shape[1] // LANES
    me = lax.axis_index("member")
    depth = widened(depth_ref, me, blocks)
    wet = jnp.where(widened(mask_ref, me, blocks) == 1, 1.0, 0.0).astype(f32)
    friction = widened(fric_ref, me, blocks)
    observed = widened(obs_ref, me, blocks)
    for k, value in enumerate((depth, wet, friction, observed)):
        own_ref[k] = value
    parts = [
        part for value in (depth, friction, observed) for part in pieces(value[:EXTRA, :])
    ]
    for k, part in enumerate(parts + [wet[:EXTRA, :]]):
        head_ref[EXTRA * k : EXTRA * (k + 1), :] = part
    turn_ref[...] = widened(cor_ref, me, blocks)


def index_kernel(copy_ref, spread_ref, split_ref, idx_ref, seen):
    for p in range(32):
        seen[p] = 0
    for s in range(32):
        seen[copy_ref[s]] = 1
    for i in range(DISTINCT):
        idx_ref[i] = 0
    count = jnp.int32(0)
    for p in range(32):
        used = seen[p]
        place = jnp.minimum(count, DISTINCT - 1)
        idx_ref[place] = jnp.where(used == 1, p, idx_ref[place])
        seen[p] = place
        count = count + used
    for s in range(32):
        idx_ref[DISTINCT + s] = seen[copy_ref[s]]
    spread = spread_ref[...]
    high = spread.astype(bf16)
    split_ref[0] = high
    split_ref[1] = (spread - high.astype(f32)).astype(bf16)


def select_kernel(idx_ref, all_ref, shead_ref, fields_ref, head_ref, rows):
    columns = fields_ref.shape[1] // 3
    part = 3 * columns
    for i in range(DISTINCT):
        particle = idx_ref[i]
        src, p = particle // 2, particle % 2
        main = all_ref[src, pl.ds(pl.multiple_of(p * part, 16), part), :]
        folded = all_ref[src, 2 * part : 2 * part + columns, :].astype(f32)
        fields_ref[i, :, :LANES] = main.astype(f32)
        for f in range(3):
            fields_ref[i, f * columns : (f + 1) * columns, LANES:] = jnp.where(
                p == 0, unfold(folded, f), unfold(folded, 3 + f)
            )
            at = (i * 3 + f) * EXTRA
            rows[at : at + EXTRA, :] = fields_ref[i, f * columns : f * columns + EXTRA, :]
    n = rows.shape[0]
    rows[DISTINCT * 3 * EXTRA : n, :] = shead_ref[...]
    head_ref[0:n, :] = rows[:, :LANES].astype(bf16)
    halos = jnp.zeros((16, LANES), f32)
    for g in range(n // 16):
        halos = fold(halos, rows[16 * g : 16 * g + 16, LANES:], g)
    head_ref[n : n + 16, :] = halos.astype(bf16)


def east(x):
    return 0.5 * (pltpu.roll(x, x.shape[0] - 1, 0) - pltpu.roll(x, 1, 0))


def north(x):
    return 0.5 * (pltpu.roll(x, x.shape[1] - 1, 1) - pltpu.roll(x, 1, 1))


def step_kernel(
    fields_ref, right_ref, own_ref, turn_ref, out_ref, work_ref, copies_ref, rrows,
):
    columns = own_ref.shape[1]
    keep = slice(SHIFT, SHIFT + columns)
    n = rrows.shape[0]
    rrows[:, :LANES] = right_ref[0:n, :].astype(f32)
    folded = right_ref[n : n + 16, :].astype(f32)
    for g in range(n // 16):
        rrows[16 * g : 16 * g + 16, LANES:] = unfold(folded, g)
    base = DISTINCT * 3 * EXTRA

    def beside(k):
        return rrows[base + EXTRA * k : base + EXTRA * (k + 1), :]

    def static(k, at):
        extra = (beside(at) + beside(at + 1)) + beside(at + 2)
        return jnp.concatenate([own_ref[k], extra], axis=0)

    depth = static(0, 0)
    friction = static(2, 3)
    obs = static(3, 6)
    wet = jnp.concatenate([own_ref[1], beside(9)], axis=0)
    damped = wet * (1.0 / (1.0 + time_step * friction))
    turning = turn_ref[...]
    for k, value in enumerate((wet, damped, obs)):
        work_ref[k] = value[keep, :]
    for i in range(DISTINCT):
        fields = []
        for f in range(3):
            at = (i * 3 + f) * EXTRA
            fields.append(
                jnp.concatenate(
                    [fields_ref[i, f * columns : (f + 1) * columns, :], rrows[at : at + EXTRA, :]],
                    axis=0,
                )
            )
        height, zonal, meridional = fields
        fresh = height - time_step * wet * (east(depth * zonal) + north(depth * meridional))
        zonal1 = damped * (zonal + time_step * (turning * meridional - east(fresh)))
        meridional1 = damped * (meridional - time_step * (turning * zonal + north(fresh)))
        change = -time_step * wet * (east(depth * zonal1) + north(depth * meridional1))
        zonal_part = damped * (zonal1 + time_step * (turning * meridional1))
        meridional_part = damped * (meridional1 - time_step * (turning * zonal1))
        innov = (obs - fresh)[keep, :LANES]
        sent = innov.astype(bf16)
        for d in range(copies_ref.shape[0]):
            copies_ref[d, i * columns : (i + 1) * columns, :] = sent
        out_ref[i, 0] = innov
        for k, value in enumerate((change, zonal_part, meridional_part)):
            out_ref[i, k + 1] = value[keep, :LANES]


def spread_dot(gathered_ref, spread_ref):
    blocks = gathered_ref.shape[0]
    lhs = jnp.concatenate([gathered_ref[b] for b in range(blocks)], axis=1)
    dims = (((1,), (1,)), ((), ()))
    return lax.dot_general(
        lhs, spread_ref[0], dims, preferred_element_type=f32
    ) + lax.dot_general(lhs, spread_ref[1], dims, preferred_element_type=f32)


def update_kernel(gathered_ref, spread_ref, all_ref, work_ref, innov_ref, copies_ref):
    columns = work_ref.shape[1]
    wet = work_ref[0, :, :LANES]
    spreaded = spread_dot(gathered_ref, spread_ref)
    for i in range(DISTINCT):
        innov = all_ref[i, 0]
        sp = spreaded[i * columns : (i + 1) * columns, :]
        new = innov - nudge_rate * wet * (innov + sp) - all_ref[i, 1]
        innov_ref[i] = new
        sent = new.astype(bf16)
        for d in range(copies_ref.shape[0]):
            copies_ref[d, i * columns : (i + 1) * columns, :] = sent


def final_kernel(
    gathered_ref, spread_ref, innov_ref, all_ref, work_ref,
    state_ref, tail_ref, edge_ref, sums_ref, *, total,
):
    columns = work_ref.shape[1]
    blocks = gathered_ref.shape[0]
    me = lax.axis_index("member")
    wet = work_ref[0, :, :LANES]
    damped = work_ref[1, :, :LANES]
    obs_tile = work_ref[2, :, LANES:]
    obs = work_ref[2, :, :LANES]
    before = jnp.maximum(me - 1, 0)
    after = jnp.minimum(me + 1, blocks - 1)
    has_before = jnp.where(me > 0, 1.0, 0.0).astype(f32)
    has_after = jnp.where(me < blocks - 1, 1.0, 0.0).astype(f32)
    lane = lax.broadcasted_iota(jnp.int32, (columns, LANES), 1)
    line = lax.broadcasted_iota(jnp.int32, (columns, LANES), 0)
    first = lax.axis_index("lon") * columns + SHIFT
    column = first + line
    column = jnp.where(column >= total, column - total, column).astype(f32)
    weight = wet * (1.0 + 2.0 * column / total)
    spreaded = spread_dot(gathered_ref, spread_ref)
    row = jnp.zeros((1, LANES), f32)
    for i in range(DISTINCT):
        part = slice(i * columns, (i + 1) * columns)
        innov = innov_ref[i]
        fresh = obs - innov
        height = fresh + nudge_rate * wet * (innov + spreaded[part, :])
        gap = obs - height
        row = jnp.where(lane[0:1] == i, jnp.sum(weight * (gap * gap)), row)
        near = gathered_ref[before, part, :].astype(f32)
        far = gathered_ref[after, part, :].astype(f32)
        fresh_before = has_before * (obs_tile - near)
        fresh_after = has_after * (obs_tile - far)
        down = jnp.where(lane == 0, pltpu.roll(fresh_before, 1, 1), pltpu.roll(fresh, 1, 1))
        up = jnp.where(
            lane == LANES - 1,
            pltpu.roll(fresh_after, LANES - 1, 1),
            pltpu.roll(fresh, LANES - 1, 1),
        )
        west = jnp.where(line == 0, 0.0, pltpu.roll(fresh, 1, 0))
        easterly = jnp.where(line == columns - 1, 0.0, pltpu.roll(fresh, columns - 1, 0))
        zonal = all_ref[i, 2] - damped * (time_step * 0.5 * (easterly - west))
        meridional = all_ref[i, 3] - damped * (time_step * 0.5 * (up - down))
        for f, value in enumerate((height, zonal, meridional)):
            state_ref[i, f * columns : (f + 1) * columns, :] = value
            at = (i * 3 + f) * SHIFT
            tail_ref[at : at + SHIFT, :] = value[columns - SHIFT :, :]
        at = DISTINCT * 3 * SHIFT + i
        tail_ref[at : at + 1, :] = fresh[columns - 1 :, :]
        edge_ref[i : i + 1, :] = fresh[0:1, :]
    for d in range(sums_ref.shape[0]):
        sums_ref[d] = row


def slots_kernel(idx_ref, state_ref, tail_ref, edge_ref, own_ref, sums_ref, out_ref, moved):
    columns = state_ref.shape[1] // 3
    at = slice(SHIFT - 1, SHIFT + 1)
    damped = own_ref[1, at, :LANES] * (1.0 / (1.0 + time_step * own_ref[2, at, :LANES]))
    side = damped * (time_step * 0.5)
    last = DISTINCT * 3 * SHIFT
    for i in range(DISTINCT):
        for f in range(3):
            k = i * 3 + f
            moved[i, f * columns : (f + 1) * columns, :] = jnp.concatenate(
                [
                    tail_ref[k * SHIFT : (k + 1) * SHIFT, :],
                    state_ref[i, f * columns : (f + 1) * columns - SHIFT, :],
                ],
                axis=0,
            )
        row = columns + SHIFT - 1
        moved[i, row : row + 1, :] = moved[i, row : row + 1, :] - side[0:1] * edge_ref[i : i + 1, :]
        moved[i, row + 1 : row + 2, :] = (
            moved[i, row + 1 : row + 2, :] + side[1:2] * tail_ref[last + i : last + i + 1, :]
        )
    row = jnp.broadcast_to(jnp.sum(sums_ref[...], axis=0), (8, LANES))
    n = 3 * columns
    for d in range(out_ref.shape[0]):
        for p in range(2):
            out_ref[d, p * n : (p + 1) * n, :] = moved[idx_ref[DISTINCT + 2 * d + p]]
        out_ref[d, 2 * n : 2 * n + 8, :] = row


def output_kernel(idx_ref, state_ref, out_ref, misfit_ref, *, cells):
    columns = out_ref.shape[2]
    blocks = state_ref.shape[0]
    n = 6 * columns
    me = lax.axis_index("member")
    row = jnp.zeros((1, LANES), f32)
    for b in range(blocks):
        row = row + state_ref[b, n : n + 1, :]
        for p in range(2):
            for f in range(3):
                k = p * 3 + f
                out_ref[p, f, :, b * LANES : (b + 1) * LANES] = state_ref[
                    b, k * columns : (k + 1) * columns, :
                ]
    lane = lax.broadcasted_iota(jnp.int32, (1, LANES), 1)
    for p in range(2):
        place = idx_ref[DISTINCT + 2 * me + p]
        misfit_ref[p] = jnp.sum(jnp.where(lane == place, row, 0.0)) / cells


def per_device(ensemble, copy_list, depth, land_mask, friction, coriolis, spread, observed):
    columns, lat = depth.shape
    members = lax.axis_size("member")
    lons = lax.axis_size("lon")
    blocks = lat // LANES
    rows = DISTINCT * columns
    wide = 2 * LANES
    statics = 10 * EXTRA
    halo_rows = DISTINCT * 3 * EXTRA + statics
    shape = jax.ShapeDtypeStruct
    eastward = [(i, (i + 1) % lons) for i in range(lons)]
    westward = [((i + 1) % lons, i) for i in range(lons)]

    def swap(x):
        return lax.all_to_all(x, "member", 0, 0, tiled=True)

    packed = call(
        pack_kernel,
        shape((blocks, 7 * columns, LANES), bf16),
        [ANY],
        VMEM,
        [pltpu.VMEM(ensemble.shape, bf16), pltpu.SemaphoreType.DMA(())],
        limit=60,
    )(ensemble)
    packed = swap(packed)
    own, shead, turning = call(
        static_kernel,
        (shape((4, columns, wide), f32), shape((statics, wide), f32), shape((1, wide), f32)),
        [VMEM] * 5,
        (VMEM, VMEM, VMEM),
    )(depth, land_mask, friction, observed, coriolis[None, :])
    parts, idx = call(
        index_kernel,
        (shape((2,) + spread.shape, bf16), shape((64,), jnp.int32)),
        [SMEM, VMEM],
        (VMEM, SMEM),
        [pltpu.SMEM((32,), jnp.int32)],
    )(copy_list, spread)
    packed, own, turning, parts = lax.optimization_barrier((packed, own, turning, parts))
    fields, head = call(
        select_kernel,
        (
            shape((DISTINCT, 3 * columns, wide), f32),
            shape((halo_rows + 16, LANES), bf16),
        ),
        [SMEM, VMEM, VMEM],
        (VMEM, VMEM),
        [pltpu.VMEM((halo_rows, wide), f32)],
    )(idx, packed, shead)
    right = lax.ppermute(head, "lon", westward)
    step1, work, copies = call(
        step_kernel,
        (
            shape((DISTINCT, 4, columns, LANES), f32),
            shape((3, columns, wide), f32),
            shape((members, rows, LANES), bf16),
        ),
        [VMEM] * 4,
        (VMEM, VMEM, VMEM),
        [pltpu.VMEM((halo_rows, wide), f32)],
    )(fields, right, own, turning)
    gathered1 = swap(copies)
    innov2, copies = call(
        update_kernel,
        (
            shape((DISTINCT, columns, LANES), f32),
            shape((members, rows, LANES), bf16),
        ),
        [VMEM] * 4,
        (VMEM, VMEM),
        flops=2 * 2 * rows * LANES * lat,
    )(gathered1, parts, step1, work)
    gathered2 = swap(copies)
    state, tail, edge, sums = call(
        functools.partial(final_kernel, total=columns * lons),
        (
            shape((DISTINCT, 3 * columns, LANES), f32),
            shape((DISTINCT * (3 * SHIFT + 1), LANES), f32),
            shape((DISTINCT, LANES), f32),
            shape((lons, 1, LANES), f32),
        ),
        [VMEM] * 5,
        (VMEM,) * 4,
        flops=2 * 2 * rows * LANES * lat,
    )(gathered2, parts, innov2, step1, work)
    sums = lax.all_to_all(sums, "lon", 0, 0, tiled=True)
    tail = lax.ppermute(tail, "lon", eastward)
    state = call(
        slots_kernel,
        shape((members, 6 * columns + 8, LANES), f32),
        [SMEM] + [VMEM] * 5,
        VMEM,
        [pltpu.VMEM((DISTINCT, 3 * columns, LANES), f32)],
    )(idx, state, tail, edge, own, sums)
    state = swap(state)
    return call(
        functools.partial(output_kernel, cells=float(lat * columns * lons)),
        (shape((2, 3, columns, lat), f32), shape((2,), f32)),
        [SMEM, VMEM],
        (VMEM, SMEM),
    )(idx, state)


def solution(mesh):
    placed = (
        P("member", None, "lon", None),
        P(),
        P("lon", None),
        P("lon", None),
        P("lon", None),
        P(),
        P("member", None),
        P("lon", None),
    )
    return jax.shard_map(
        per_device,
        mesh=mesh,
        in_specs=placed,
        out_specs=(P("member", None, "lon", None), P("member")),
        check_vma=False,
    )
```

time: 110 us -> 108 us (0.982)
  starting transfers between devices: 32.8 us -> 31.5 us
    all_to_all x1, waiting for transfers between devices: 10.5 us -> 4.73 us  [per_device(): sums = lax.all_to_all(sums, 'lon', 0, 0, tiled=True)]
    ppermute x1, waiting for transfers between devices: 0.01 us -> 5.73 us  [per_device(): tail = lax.ppermute(tail, 'lon', eastward)]
    ppermute x1 -> x0, starting transfers between devices: 2.66 us -> none  [per_device(): sright = lax.ppermute(shead, 'lon', westward)]
    ppermute x1 -> x0, waiting for transfers between devices: 2 us -> none  [per_device(): sright = lax.ppermute(shead, 'lon', westward)]
    all_to_all x1, starting transfers between devices: 6.59 us -> 8.08 us  [per_device(): sums = lax.all_to_all(sums, 'lon', 0, 0, tiled=True)]
    ppermute x1, waiting for transfers between devices: 0.01 us -> 1.39 us  [per_device(): right = lax.ppermute(head, 'lon', westward)]
    pallas_call x8 -> x9, Pallas kernels: 8.65 us -> 8.82 us  [the longest x1 2.07 us: per_device(): call(pack_kernel, shape((blocks, 7 * columns, LANES), bf16), [ANY], VMEM,...]
  transfers between devices with their start and end apart: 5 -> 4, of which waited for: 3 -> 4; matrix products, arithmetic and copies ran while one was open for 1% -> 0% of each run, Pallas kernels for 1% -> 1%
where the time goes in v5:
time: 108 us; the launch traced here: 107 us
  blocking collectives  46.6 us (43%)
  starting transfers between devices  31.5 us (29%)
  waiting for transfers between devices  19.5 us (18%)
  Pallas kernels  8.82 us (8%)
    all_to_all x3, blocking collectives, swap(): return lax.all_to_all(x, 'member', 0, 0, tiled=True)  46.6 us
    all_to_all x1, starting transfers between devices, swap(): return lax.all_to_all(x, 'member', 0, 0, tiled=True)  10.2 us
    ppermute x1, starting transfers between devices, per_device(): right = lax.ppermute(head, 'lon', westward)  10 us
    all_to_all x1, starting transfers between devices, per_device(): sums = lax.all_to_all(sums, 'lon', 0, 0, tiled=True)  8.08 us
    all_to_all x1, waiting for transfers between devices, swap(): return lax.all_to_all(x, 'member', 0, 0, tiled=True)  7.63 us
    ppermute x1, waiting for transfers between devices, per_device(): tail = lax.ppermute(tail, 'lon', eastward)  5.73 us
    all_to_all x1, waiting for transfers between devices, per_device(): sums = lax.all_to_all(sums, 'lon', 0, 0, tiled=True)  4.73 us
    ppermute x1, starting transfers between devices, per_device(): tail = lax.ppermute(tail, 'lon', eastward)  3.14 us
  transfers between devices with their start and end apart: 4, of which 4 were waited for; matrix products, arithmetic and copies ran while one was open for 0% of the time, Pallas kernels for 1%

profile of v5, /device:TPU:1, one launch (start us, length us, event | category | flops | bytes accessed | tf_op | source)
XLA Modules:
  0.0 107.2 jit_solution(636751096518878357)
XLA Ops:
  0.6 2.1 %shard_map.96 = bf16[16,112,128]{2,1,0:T(8,128)(2,1)} custom-call(bf16[2,3,16,2048]{3,2,1,0:T(8,128)(2,1)} %ens_hbm.1), custom_call_target="tpu_custom_call" | custom-call | flops 1000000 | bytes 1000000 | tf_op jit(solution)/shard_map/pallas_call | solution.py:366
  2.7 0.0 copy-start.6
  2.7 10.2 %all-to-all-start = ((bf16[16,112,128]{2,1,0:T(8,128)(2,1)}), bf16[16,112,128]{2,1,0:T(8,128)(2,1)S(1)}, u32[]{:S(2)}, u32[]{:S(2)}) async-start(bf16[16,112,128]{2,1,0:T(8,128)(2,1)} %shard_map.96), calls=%async_computation | async-start | bytes 917504 | tf_op jit(solution)/shard_map/all_to_all | solution.py:364
  13.0 0.0 copy-start.1
  13.0 0.0 copy-start.2
  13.0 0.0 copy-start.3
  13.0 0.0 copy-start.5
  13.1 1.4 %shard_map.95 = (bf16[2,128,2048]{2,1,0:T(8,128)(2,1)S(1)}, s32[64]{0:T(128)S(1)}) custom-call(s32[32]{0:T(128)S(1)} %copy-done.6, f32[128,2048]{1,0:T(8,128)S(1)} %copy-done), custom_call_target="tpu_custom_call" | custom-call | flops 1000000 | bytes 1000000 | tf_op jit(solution)/shard_map/pallas_call | solution.py:381
  14.5 7.6 %all-to-all-done.all_ref = bf16[16,112,128]{2,1,0:T(8,128)(2,1)S(1)} async-done(((bf16[16,112,128]{2,1,0:T(8,128)(2,1)}), bf16[16,112,128]{2,1,0:T(8,128)(2,1)S(1)}, u32[]{:S(2)}, u32[]{:S(2)}) %all-to-all-start) | async-done | bytes 458784 | tf_op jit(solution)/shard_map/all_to_all | solution.py:364
  22.1 0.7 shard_map.98
  22.9 10.0 %collective-permute-start = (bf16[288,128]{1,0:T(8,128)(2,1)S(1)}, bf16[288,128]{1,0:T(8,128)(2,1)S(1)}, u32[]{:S(2)}, u32[]{:S(2)}) collective-permute-start(bf16[288,128]{1,0:T(8,128)(2,1)S(1)} %get-tuple-element.29), channel_id=1, source_target_pairs={{1,0},{2,1},{3,2},{4,3},{5,4},{6,5},{7,6},{8,7},{9,8},{10,9},{11,1... | collective-permute-start | bytes 221192 | tf_op jit(solution)/shard_map/ppermute | solution.py:399
  32.9 1.4 %collective-permute-done.right_ref = bf16[288,128]{1,0:T(8,128)(2,1)S(1)} collective-permute-done((bf16[288,128]{1,0:T(8,128)(2,1)S(1)}, bf16[288,128]{1,0:T(8,128)(2,1)S(1)}, u32[]{:S(2)}, u32[]{:S(2)}) %collective-permute-start) | collective-permute-done | bytes 73760 | tf_op jit(solution)/shard_map/ppermute | solution.py:399
  34.3 0.8 shard_map.99
  35.1 14.1 %all_to_all.25.gathered_ref = bf16[16,128,128]{2,1,0:T(8,128)(2,1)S(1)} all-to-all(bf16[16,128,128]{2,1,0:T(8,128)(2,1)S(1)} %get-tuple-element.32), channel_id=1, replica_groups=mesh['member'=16,'lon'=32] {'member'}, dimensions={0} | all-to-all | bytes 1048576 | tf_op jit(solution)/shard_map/all_to_all | solution.py:364
  49.2 0.5 shard_map.100
  49.7 13.5 %all_to_all.26.gathered_ref = bf16[16,128,128]{2,1,0:T(8,128)(2,1)S(1)} all-to-all(bf16[16,128,128]{2,1,0:T(8,128)(2,1)S(1)} %get-tuple-element.36), channel_id=1, replica_groups=mesh['member'=16,'lon'=32] {'member'}, dimensions={0} | all-to-all | bytes 1048576 | tf_op jit(solution)/shard_map/all_to_all | solution.py:364
  63.2 1.2 %shard_map.101 = (f32[8,48,128]{2,1,0:T(8,128)S(1)}, f32[104,128]{1,0:T(8,128)S(1)}, f32[8,128]{1,0:T(8,128)S(1)}, f32[32,1,128]{2,1,0:T(1,128)}) custom-call(bf16[16,128,128]{2,1,0:T(8,128)(2,1)S(1)} %all_to_all.26.gathered_ref, bf16[2,128,2048]{2,1,0:T(8,128)(2,1)S(1)} %get-tuple-element.33.spread_ref, f32[8,16,128]{2,1,0:T(8,128)S(1)} %get-tuple-element.37.innov_ref, ...), custom_call_target="tpu_custom_call" | custom-call | flops 134217728 | bytes 1000000 | tf_op jit(solution)/shard_map/pallas_call | solution.py:423
  64.4 8.1 %all-to-all-start.3 = ((f32[32,1,128]{2,1,0:T(1,128)}), f32[32,1,128]{2,1,0:T(1,128)S(1)}, u32[]{:S(2)}, u32[]{:S(2)}) async-start(f32[32,1,128]{2,1,0:T(1,128)} %get-tuple-element.41), calls=%async_computation.3 | async-start | bytes 32768 | tf_op jit(solution)/shard_map/all_to_all | solution.py:435
  72.5 3.1 %collective-permute-start.1 = (f32[104,128]{1,0:T(8,128)S(1)}, f32[104,128]{1,0:T(8,128)S(1)}, u32[]{:S(2)}, u32[]{:S(2)}) collective-permute-start(f32[104,128]{1,0:T(8,128)S(1)} %get-tuple-element.39), channel_id=1, source_target_pairs={{0,1},{1,2},{2,3},{3,4},{4,5},{5,6},{6,7},{7,8},{8,9},{9,10},{10,1... | collective-permute-start | bytes 159752 | tf_op jit(solution)/shard_map/ppermute | solution.py:436
  75.6 5.7 %collective-permute-done.1.tail_ref = f32[104,128]{1,0:T(8,128)S(1)} collective-permute-done((f32[104,128]{1,0:T(8,128)S(1)}, f32[104,128]{1,0:T(8,128)S(1)}, u32[]{:S(2)}, u32[]{:S(2)}) %collective-permute-start.1) | collective-permute-done | bytes 53280 | tf_op jit(solution)/shard_map/ppermute | solution.py:436
  81.3 4.7 %all-to-all-done.3.sums_ref = f32[32,1,128]{2,1,0:T(1,128)S(1)} async-done(((f32[32,1,128]{2,1,0:T(1,128)}), f32[32,1,128]{2,1,0:T(1,128)S(1)}, u32[]{:S(2)}, u32[]{:S(2)}) %all-to-all-start.3) | async-done | bytes 16416 | tf_op jit(solution)/shard_map/all_to_all | solution.py:435
  86.1 0.6 shard_map.102
  86.7 19.0 %all_to_all.27.state_ref = f32[16,104,128]{2,1,0:T(8,128)S(1)} all-to-all(f32[16,104,128]{2,1,0:T(8,128)S(1)} %shard_map.102), channel_id=1, replica_groups=mesh['member'=16,'lon'=32] {'member'}, dimensions={0} | all-to-all | bytes 1703936 | tf_op jit(solution)/shard_map/all_to_all | solution.py:364
  105.7 1.5 %shard_map.103 = (f32[2,3,16,2048]{3,2,1,0:T(8,128)}, f32[2]{0:T(128)}) custom-call(s32[64]{0:T(128)S(1)} %get-tuple-element.22.idx_ref, f32[16,104,128]{2,1,0:T(8,128)S(1)} %all_to_all.27.state_ref), custom_call_target="tpu_custom_call" | custom-call | flops 1000000 | bytes 1000000 | tf_op jit(solution)/shard_map/pallas_call | solution.py:445
  (10 shorter events, 0.1 us)
Async XLA Ops:
  0.6 12.3 %copy-start = (f32[128,2048]{1,0:T(8,128)S(1)}, f32[128,2048]{1,0:T(8,128)}, u32[]{:S(2)}) copy-start(f32[128,2048]{1,0:T(8,128)} %spread_ref.1) | copy-start | bytes 3145732
  2.7 10.3 %copy-start.6 = (s32[32]{0:T(128)S(1)}, s32[32]{0:T(128)}, u32[]{:S(2)}) copy-start(s32[32]{0:T(128)} %copy_ref.1) | copy-start | bytes 388
  2.7 19.4 %all-to-all-start = ((bf16[16,112,128]{2,1,0:T(8,128)(2,1)}), bf16[16,112,128]{2,1,0:T(8,128)(2,1)S(1)}, u32[]{:S(2)}, u32[]{:S(2)}) async-start(bf16[16,112,128]{2,1,0:T(8,128)(2,1)} %shard_map.96), calls=%async_computation | async-start | bytes 917504 | tf_op jit(solution)/shard_map/all_to_all | solution.py:364
  13.0 1.4 %copy-start.1 = (f32[16,2048]{1,0:T(8,128)S(1)}, f32[16,2048]{1,0:T(8,128)}, u32[]{:S(2)}) copy-start(f32[16,2048]{1,0:T(8,128)} %depth_ref.1) | copy-start | bytes 393220
  13.0 1.4 %copy-start.2 = (s32[16,2048]{1,0:T(8,128)S(1)}, s32[16,2048]{1,0:T(8,128)}, u32[]{:S(2)}) copy-start(s32[16,2048]{1,0:T(8,128)} %mask_ref.1) | copy-start | bytes 393220
  13.0 1.4 %copy-start.3 = (f32[16,2048]{1,0:T(8,128)S(1)}, f32[16,2048]{1,0:T(8,128)}, u32[]{:S(2)}) copy-start(f32[16,2048]{1,0:T(8,128)} %fric_ref.1) | copy-start | bytes 393220
  13.0 1.4 %copy-start.4 = (f32[16,2048]{1,0:T(8,128)S(1)}, f32[16,2048]{1,0:T(8,128)}, u32[]{:S(2)}) copy-start(f32[16,2048]{1,0:T(8,128)} %obs_ref.1) | copy-start | bytes 393220
  13.0 1.4 %copy-start.5 = (f32[2048]{0:T(1024)S(1)}, f32[2048]{0:T(1024)}, u32[]{:S(2)}) copy-start(f32[2048]{0:T(1024)} %param.13) | copy-start | bytes 24580
  22.9 11.4 %collective-permute-start = (bf16[288,128]{1,0:T(8,128)(2,1)S(1)}, bf16[288,128]{1,0:T(8,128)(2,1)S(1)}, u32[]{:S(2)}, u32[]{:S(2)}) collective-permute-start(bf16[288,128]{1,0:T(8,128)(2,1)S(1)} %get-tuple-element.29), channel_id=1, source_target_pairs={{1,0},{2,1},{3,2},{4,3},{5,4},{6,5},{7,6},{8,7},{9,8},{10,9},{11,1... | collective-permute-start | bytes 221192 | tf_op jit(solution)/shard_map/ppermute | solution.py:399
  64.4 21.7 %all-to-all-start.3 = ((f32[32,1,128]{2,1,0:T(1,128)}), f32[32,1,128]{2,1,0:T(1,128)S(1)}, u32[]{:S(2)}, u32[]{:S(2)}) async-start(f32[32,1,128]{2,1,0:T(1,128)} %get-tuple-element.41), calls=%async_computation.3 | async-start | bytes 32768 | tf_op jit(solution)/shard_map/all_to_all | solution.py:435
  72.5 8.9 %collective-permute-start.1 = (f32[104,128]{1,0:T(8,128)S(1)}, f32[104,128]{1,0:T(8,128)S(1)}, u32[]{:S(2)}, u32[]{:S(2)}) collective-permute-start(f32[104,128]{1,0:T(8,128)S(1)} %get-tuple-element.39), channel_id=1, source_target_pairs={{0,1},{1,2},{2,3},{3,4},{4,5},{5,6},{6,7},{7,8},{8,9},{9,10},{10,1... | collective-permute-start | bytes 159752 | tf_op jit(solution)/shard_map/ppermute | solution.py:436

commit v6 on v5

--- a/solution.py
+++ b/solution.py
@@ -298,7 +298,21 @@
         sums_ref[d] = row
 
 
-def slots_kernel(idx_ref, state_ref, tail_ref, edge_ref, own_ref, sums_ref, out_ref, moved):
+LEVELS = (9, 5, 5)
+
+
+def residue_level(value, rounded, levels):
+    size = jnp.maximum(jnp.abs(rounded), 1e-30)
+    at = (value - rounded) * 256.0 / size + 1.0
+    return jnp.clip(jnp.floor(at * (0.5 * levels)), 0.0, levels - 1.0)
+
+
+def restored(rounded, level, levels):
+    step = 2.0 / (256.0 * levels)
+    return rounded + jnp.abs(rounded) * (level * step + (0.5 * step - 1.0 / 256.0))
+
+
+def slots_kernel(idx_ref, state_ref, tail_ref, edge_ref, own_ref, sums_ref, out_ref, moved, coded):
     columns = state_ref.shape[1] // 3
     at = slice(SHIFT - 1, SHIFT + 1)
     damped = own_ref[1, at, :LANES] * (1.0 / (1.0 + time_step * own_ref[2, at, :LANES]))
@@ -319,28 +333,44 @@
         moved[i, row + 1 : row + 2, :] = (
             moved[i, row + 1 : row + 2, :] + side[1:2] * tail_ref[last + i : last + i + 1, :]
         )
-    row = jnp.broadcast_to(jnp.sum(sums_ref[...], axis=0), (8, LANES))
-    n = 3 * columns
+        code = jnp.zeros((columns, LANES), f32)
+        for f in (2, 1, 0):
+            value = moved[i, f * columns : (f + 1) * columns, :]
+            sent = value.astype(bf16)
+            coded[i, f * columns : (f + 1) * columns, :] = sent
+            code = code * LEVELS[f] + residue_level(value, sent.astype(f32), LEVELS[f])
+        coded[i, 3 * columns : 4 * columns, :] = code.astype(bf16)
+    parts = jnp.concatenate(
+        pieces(jnp.sum(sums_ref[...], axis=0)) + (jnp.zeros((13, LANES), f32),), axis=0
+    ).astype(bf16)
+    n = 4 * columns
     for d in range(out_ref.shape[0]):
         for p in range(2):
-            out_ref[d, p * n : (p + 1) * n, :] = moved[idx_ref[DISTINCT + 2 * d + p]]
-        out_ref[d, 2 * n : 2 * n + 8, :] = row
+            out_ref[d, p * n : (p + 1) * n, :] = coded[idx_ref[DISTINCT + 2 * d + p]]
+        out_ref[d, 2 * n : 2 * n + 16, :] = parts
 
 
 def output_kernel(idx_ref, state_ref, out_ref, misfit_ref, *, cells):
     columns = out_ref.shape[2]
     blocks = state_ref.shape[0]
-    n = 6 * columns
+    n = 4 * columns
     me = lax.axis_index("member")
+    for p in range(2):
+        for b in range(blocks):
+            part = slice(b * LANES, (b + 1) * LANES)
+            block = state_ref[b, p * n : (p + 1) * n, :].astype(f32)
+            code = block[3 * columns :]
+            for f in range(3):
+                rounded = block[f * columns : (f + 1) * columns]
+                level = code
+                if f < 2:
+                    code = jnp.floor(code * (1.0 / LEVELS[f]) + 0.5 / LEVELS[f])
+                    level = level - code * LEVELS[f]
+                out_ref[p, f, :, part] = restored(rounded, level, LEVELS[f])
     row = jnp.zeros((1, LANES), f32)
     for b in range(blocks):
-        row = row + state_ref[b, n : n + 1, :]
-        for p in range(2):
-            for f in range(3):
-                k = p * 3 + f
-                out_ref[p, f, :, b * LANES : (b + 1) * LANES] = state_ref[
-                    b, k * columns : (k + 1) * columns, :
-                ]
+        parts = state_ref[b, 2 * n : 2 * n + 16, :].astype(f32)
+        row = row + ((parts[0:1] + parts[1:2]) + parts[2:3])
     lane = lax.broadcasted_iota(jnp.int32, (1, LANES), 1)
     for p in range(2):
         place = idx_ref[DISTINCT + 2 * me + p]
@@ -436,10 +466,13 @@
     tail = lax.ppermute(tail, "lon", eastward)
     state = call(
         slots_kernel,
-        shape((members, 6 * columns + 8, LANES), f32),
+        shape((members, 8 * columns + 16, LANES), bf16),
         [SMEM] + [VMEM] * 5,
         VMEM,
-        [pltpu.VMEM((DISTINCT, 3 * columns, LANES), f32)],
+        [
+            pltpu.VMEM((DISTINCT, 3 * columns, LANES), f32),
+            pltpu.VMEM((DISTINCT, 4 * columns, LANES), bf16),
+        ],
     )(idx, state, tail, edge, own, sums)
     state = swap(state)
     return call(

time: 108 us -> 106 us (0.981)
  blocking collectives: 46.6 us -> 44.2 us
    all_to_all x3, blocking collectives: 46.6 us -> 44.2 us  [swap(): return lax.all_to_all(x, 'member', 0, 0, tiled=True)]
where the time goes in v6:
time: 106 us; the launch traced here: 105 us
  blocking collectives  44.2 us (42%)
  starting transfers between devices  31.5 us (30%)
  waiting for transfers between devices  19.5 us (18%)
  Pallas kernels  9.1 us (9%)
    all_to_all x3, blocking collectives, swap(): return lax.all_to_all(x, 'member', 0, 0, tiled=True)  44.2 us
    all_to_all x1, starting transfers between devices, swap(): return lax.all_to_all(x, 'member', 0, 0, tiled=True)  10.2 us
    ppermute x1, starting transfers between devices, per_device(): right = lax.ppermute(head, 'lon', westward)  10 us
    all_to_all x1, starting transfers between devices, per_device(): sums = lax.all_to_all(sums, 'lon', 0, 0, tiled=True)  8.08 us
    all_to_all x1, waiting for transfers between devices, swap(): return lax.all_to_all(x, 'member', 0, 0, tiled=True)  7.63 us
    ppermute x1, waiting for transfers between devices, per_device(): tail = lax.ppermute(tail, 'lon', eastward)  5.73 us
    all_to_all x1, waiting for transfers between devices, per_device(): sums = lax.all_to_all(sums, 'lon', 0, 0, tiled=True)  4.73 us
    ppermute x1, starting transfers between devices, per_device(): tail = lax.ppermute(tail, 'lon', eastward)  3.14 us
  transfers between devices with their start and end apart: 4, of which 4 were waited for; matrix products, arithmetic and copies ran while one was open for 0% of the time, Pallas kernels for 1%

profile of v6, /device:TPU:1, one launch (start us, length us, event | category | flops | bytes accessed | tf_op | source)
XLA Modules:
  0.0 105.1 jit_solution(5647569999787028509)
XLA Ops:
  0.6 2.1 %shard_map.96 = bf16[16,112,128]{2,1,0:T(8,128)(2,1)} custom-call(bf16[2,3,16,2048]{3,2,1,0:T(8,128)(2,1)} %ens_hbm.1), custom_call_target="tpu_custom_call" | custom-call | flops 1000000 | bytes 1000000 | tf_op jit(solution)/shard_map/pallas_call | solution.py:396
  2.7 0.0 copy-start.6
  2.7 10.2 %all-to-all-start = ((bf16[16,112,128]{2,1,0:T(8,128)(2,1)}), bf16[16,112,128]{2,1,0:T(8,128)(2,1)S(1)}, u32[]{:S(2)}, u32[]{:S(2)}) async-start(bf16[16,112,128]{2,1,0:T(8,128)(2,1)} %shard_map.96), calls=%async_computation | async-start | bytes 917504 | tf_op jit(solution)/shard_map/all_to_all | solution.py:394
  13.0 0.0 copy-start.1
  13.0 0.0 copy-start.2
  13.0 0.0 copy-start.3
  13.0 0.0 copy-start.5
  13.1 1.4 %shard_map.95 = (bf16[2,128,2048]{2,1,0:T(8,128)(2,1)S(1)}, s32[64]{0:T(128)S(1)}) custom-call(s32[32]{0:T(128)S(1)} %copy-done.6, f32[128,2048]{1,0:T(8,128)S(1)} %copy-done), custom_call_target="tpu_custom_call" | custom-call | flops 1000000 | bytes 1000000 | tf_op jit(solution)/shard_map/pallas_call | solution.py:411
  14.5 7.6 %all-to-all-done.all_ref = bf16[16,112,128]{2,1,0:T(8,128)(2,1)S(1)} async-done(((bf16[16,112,128]{2,1,0:T(8,128)(2,1)}), bf16[16,112,128]{2,1,0:T(8,128)(2,1)S(1)}, u32[]{:S(2)}, u32[]{:S(2)}) %all-to-all-start) | async-done | bytes 458784 | tf_op jit(solution)/shard_map/all_to_all | solution.py:394
  22.1 0.7 shard_map.98
  22.9 10.0 %collective-permute-start = (bf16[288,128]{1,0:T(8,128)(2,1)S(1)}, bf16[288,128]{1,0:T(8,128)(2,1)S(1)}, u32[]{:S(2)}, u32[]{:S(2)}) collective-permute-start(bf16[288,128]{1,0:T(8,128)(2,1)S(1)} %get-tuple-element.29), channel_id=1, source_target_pairs={{1,0},{2,1},{3,2},{4,3},{5,4},{6,5},{7,6},{8,7},{9,8},{10,9},{11,1... | collective-permute-start | bytes 221192 | tf_op jit(solution)/shard_map/ppermute | solution.py:429
  32.9 1.4 %collective-permute-done.right_ref = bf16[288,128]{1,0:T(8,128)(2,1)S(1)} collective-permute-done((bf16[288,128]{1,0:T(8,128)(2,1)S(1)}, bf16[288,128]{1,0:T(8,128)(2,1)S(1)}, u32[]{:S(2)}, u32[]{:S(2)}) %collective-permute-start) | collective-permute-done | bytes 73760 | tf_op jit(solution)/shard_map/ppermute | solution.py:429
  34.3 0.8 shard_map.99
  35.1 14.1 %all_to_all.25.gathered_ref = bf16[16,128,128]{2,1,0:T(8,128)(2,1)S(1)} all-to-all(bf16[16,128,128]{2,1,0:T(8,128)(2,1)S(1)} %get-tuple-element.32), channel_id=1, replica_groups=mesh['member'=16,'lon'=32] {'member'}, dimensions={0} | all-to-all | bytes 1048576 | tf_op jit(solution)/shard_map/all_to_all | solution.py:394
  49.2 0.5 shard_map.100
  49.7 13.5 %all_to_all.26.gathered_ref = bf16[16,128,128]{2,1,0:T(8,128)(2,1)S(1)} all-to-all(bf16[16,128,128]{2,1,0:T(8,128)(2,1)S(1)} %get-tuple-element.36), channel_id=1, replica_groups=mesh['member'=16,'lon'=32] {'member'}, dimensions={0} | all-to-all | bytes 1048576 | tf_op jit(solution)/shard_map/all_to_all | solution.py:394
  63.2 1.2 %shard_map.101 = (f32[8,48,128]{2,1,0:T(8,128)S(1)}, f32[104,128]{1,0:T(8,128)S(1)}, f32[8,128]{1,0:T(8,128)S(1)}, f32[32,1,128]{2,1,0:T(1,128)}) custom-call(bf16[16,128,128]{2,1,0:T(8,128)(2,1)S(1)} %all_to_all.26.gathered_ref, bf16[2,128,2048]{2,1,0:T(8,128)(2,1)S(1)} %get-tuple-element.33.spread_ref, f32[8,16,128]{2,1,0:T(8,128)S(1)} %get-tuple-element.37.innov_ref, ...), custom_call_target="tpu_custom_call" | custom-call | flops 134217728 | bytes 1000000 | tf_op jit(solution)/shard_map/pallas_call | solution.py:453
  64.4 8.1 %all-to-all-start.3 = ((f32[32,1,128]{2,1,0:T(1,128)}), f32[32,1,128]{2,1,0:T(1,128)S(1)}, u32[]{:S(2)}, u32[]{:S(2)}) async-start(f32[32,1,128]{2,1,0:T(1,128)} %get-tuple-element.41), calls=%async_computation.3 | async-start | bytes 32768 | tf_op jit(solution)/shard_map/all_to_all | solution.py:465
  72.5 3.1 %collective-permute-start.1 = (f32[104,128]{1,0:T(8,128)S(1)}, f32[104,128]{1,0:T(8,128)S(1)}, u32[]{:S(2)}, u32[]{:S(2)}) collective-permute-start(f32[104,128]{1,0:T(8,128)S(1)} %get-tuple-element.39), channel_id=1, source_target_pairs={{0,1},{1,2},{2,3},{3,4},{4,5},{5,6},{6,7},{7,8},{8,9},{9,10},{10,1... | collective-permute-start | bytes 159752 | tf_op jit(solution)/shard_map/ppermute | solution.py:466
  75.6 5.7 %collective-permute-done.1.tail_ref = f32[104,128]{1,0:T(8,128)S(1)} collective-permute-done((f32[104,128]{1,0:T(8,128)S(1)}, f32[104,128]{1,0:T(8,128)S(1)}, u32[]{:S(2)}, u32[]{:S(2)}) %collective-permute-start.1) | collective-permute-done | bytes 53280 | tf_op jit(solution)/shard_map/ppermute | solution.py:466
  81.3 4.7 %all-to-all-done.3.sums_ref = f32[32,1,128]{2,1,0:T(1,128)S(1)} async-done(((f32[32,1,128]{2,1,0:T(1,128)}), f32[32,1,128]{2,1,0:T(1,128)S(1)}, u32[]{:S(2)}, u32[]{:S(2)}) %all-to-all-start.3) | async-done | bytes 16416 | tf_op jit(solution)/shard_map/all_to_all | solution.py:465
  86.1 0.7 shard_map.102
  86.8 16.6 %all_to_all.27.state_ref = bf16[16,144,128]{2,1,0:T(8,128)(2,1)S(1)} all-to-all(bf16[16,144,128]{2,1,0:T(8,128)(2,1)S(1)} %shard_map.102), channel_id=1, replica_groups=mesh['member'=16,'lon'=32] {'member'}, dimensions={0} | all-to-all | bytes 1179648 | tf_op jit(solution)/shard_map/all_to_all | solution.py:394
  103.4 1.7 %shard_map.103 = (f32[2,3,16,2048]{3,2,1,0:T(8,128)}, f32[2]{0:T(128)}) custom-call(s32[64]{0:T(128)S(1)} %get-tuple-element.22.idx_ref, bf16[16,144,128]{2,1,0:T(8,128)(2,1)S(1)} %all_to_all.27.state_ref), custom_call_target="tpu_custom_call" | custom-call | flops 1000000 | bytes 1000000 | tf_op jit(solution)/shard_map/pallas_call | solution.py:478
  (10 shorter events, 0.1 us)
Async XLA Ops:
  0.6 12.3 %copy-start = (f32[128,2048]{1,0:T(8,128)S(1)}, f32[128,2048]{1,0:T(8,128)}, u32[]{:S(2)}) copy-start(f32[128,2048]{1,0:T(8,128)} %spread_ref.1) | copy-start | bytes 3145732
  2.7 10.3 %copy-start.6 = (s32[32]{0:T(128)S(1)}, s32[32]{0:T(128)}, u32[]{:S(2)}) copy-start(s32[32]{0:T(128)} %copy_ref.1) | copy-start | bytes 388
  2.7 19.4 %all-to-all-start = ((bf16[16,112,128]{2,1,0:T(8,128)(2,1)}), bf16[16,112,128]{2,1,0:T(8,128)(2,1)S(1)}, u32[]{:S(2)}, u32[]{:S(2)}) async-start(bf16[16,112,128]{2,1,0:T(8,128)(2,1)} %shard_map.96), calls=%async_computation | async-start | bytes 917504 | tf_op jit(solution)/shard_map/all_to_all | solution.py:394
  13.0 1.4 %copy-start.1 = (f32[16,2048]{1,0:T(8,128)S(1)}, f32[16,2048]{1,0:T(8,128)}, u32[]{:S(2)}) copy-start(f32[16,2048]{1,0:T(8,128)} %depth_ref.1) | copy-start | bytes 393220
  13.0 1.4 %copy-start.2 = (s32[16,2048]{1,0:T(8,128)S(1)}, s32[16,2048]{1,0:T(8,128)}, u32[]{:S(2)}) copy-start(s32[16,2048]{1,0:T(8,128)} %mask_ref.1) | copy-start | bytes 393220
  13.0 1.4 %copy-start.3 = (f32[16,2048]{1,0:T(8,128)S(1)}, f32[16,2048]{1,0:T(8,128)}, u32[]{:S(2)}) copy-start(f32[16,2048]{1,0:T(8,128)} %fric_ref.1) | copy-start | bytes 393220
  13.0 1.4 %copy-start.4 = (f32[16,2048]{1,0:T(8,128)S(1)}, f32[16,2048]{1,0:T(8,128)}, u32[]{:S(2)}) copy-start(f32[16,2048]{1,0:T(8,128)} %obs_ref.1) | copy-start | bytes 393220
  13.0 1.4 %copy-start.5 = (f32[2048]{0:T(1024)S(1)}, f32[2048]{0:T(1024)}, u32[]{:S(2)}) copy-start(f32[2048]{0:T(1024)} %param.13) | copy-start | bytes 24580
  22.9 11.4 %collective-permute-start = (bf16[288,128]{1,0:T(8,128)(2,1)S(1)}, bf16[288,128]{1,0:T(8,128)(2,1)S(1)}, u32[]{:S(2)}, u32[]{:S(2)}) collective-permute-start(bf16[288,128]{1,0:T(8,128)(2,1)S(1)} %get-tuple-element.29), channel_id=1, source_target_pairs={{1,0},{2,1},{3,2},{4,3},{5,4},{6,5},{7,6},{8,7},{9,8},{10,9},{11,1... | collective-permute-start | bytes 221192 | tf_op jit(solution)/shard_map/ppermute | solution.py:429
  64.4 21.7 %all-to-all-start.3 = ((f32[32,1,128]{2,1,0:T(1,128)}), f32[32,1,128]{2,1,0:T(1,128)S(1)}, u32[]{:S(2)}, u32[]{:S(2)}) async-start(f32[32,1,128]{2,1,0:T(1,128)} %get-tuple-element.41), calls=%async_computation.3 | async-start | bytes 32768 | tf_op jit(solution)/shard_map/all_to_all | solution.py:465
  72.5 8.9 %collective-permute-start.1 = (f32[104,128]{1,0:T(8,128)S(1)}, f32[104,128]{1,0:T(8,128)S(1)}, u32[]{:S(2)}, u32[]{:S(2)}) collective-permute-start(f32[104,128]{1,0:T(8,128)S(1)} %get-tuple-element.39), channel_id=1, source_target_pairs={{0,1},{1,2},{2,3},{3,4},{4,5},{5,6},{6,7},{7,8},{8,9},{9,10},{10,1... | collective-permute-start | bytes 159752 | tf_op jit(solution)/shard_map/ppermute | solution.py:466

commit v7 on v6

--- a/solution.py
+++ b/solution.py
@@ -113,7 +113,7 @@
     turn_ref[...] = widened(cor_ref, me, blocks)
 
 
-def index_kernel(copy_ref, spread_ref, split_ref, idx_ref, seen):
+def index_kernel(copy_ref, spread_ref, split_ref, out_ref, idx_ref, seen):
     for p in range(32):
         seen[p] = 0
     for s in range(32):
@@ -129,27 +129,36 @@
         count = count + used
     for s in range(32):
         idx_ref[DISTINCT + s] = seen[copy_ref[s]]
+    lane = lax.broadcasted_iota(jnp.int32, out_ref.shape, 1)
+    values = jnp.zeros(out_ref.shape, jnp.int32)
+    for k in range(DISTINCT + 32):
+        values = jnp.where(lane == k, idx_ref[k], values)
+    out_ref[...] = values
     spread = spread_ref[...]
     high = spread.astype(bf16)
     split_ref[0] = high
     split_ref[1] = (spread - high.astype(f32)).astype(bf16)
 
 
-def select_kernel(idx_ref, all_ref, shead_ref, fields_ref, head_ref, rows):
-    columns = fields_ref.shape[1] // 3
+def particle_of(idx, all_ref, i, columns):
     part = 3 * columns
-    for i in range(DISTINCT):
-        particle = idx_ref[i]
-        src, p = particle // 2, particle % 2
-        main = all_ref[src, pl.ds(pl.multiple_of(p * part, 16), part), :]
-        folded = all_ref[src, 2 * part : 2 * part + columns, :].astype(f32)
-        fields_ref[i, :, :LANES] = main.astype(f32)
+    particle = idx[0, i]
+    src, p = particle // 2, particle % 2
+    main = all_ref[src, pl.ds(pl.multiple_of(p * part, 16), part), :].astype(f32)
+    folded = all_ref[src, 2 * part : 2 * part + columns, :].astype(f32)
+    halos = [jnp.where(p == 0, unfold(folded, f), unfold(folded, 3 + f)) for f in range(3)]
+    return main, halos
+
+
+def head_kernel(idx_ref, all_ref, shead_ref, head_ref, rows):
+    columns = all_ref.shape[1] // 7
+    idx = idx_ref[0:1, :]
+    for i in range(DISTINCT):
+        main, halos = particle_of(idx, all_ref, i, columns)
         for f in range(3):
-            fields_ref[i, f * columns : (f + 1) * columns, LANES:] = jnp.where(
-                p == 0, unfold(folded, f), unfold(folded, 3 + f)
-            )
             at = (i * 3 + f) * EXTRA
-            rows[at : at + EXTRA, :] = fields_ref[i, f * columns : f * columns + EXTRA, :]
+            rows[at : at + EXTRA, :LANES] = main[f * columns : f * columns + EXTRA, :]
+            rows[at : at + EXTRA, LANES:] = halos[f][:EXTRA, :]
     n = rows.shape[0]
     rows[DISTINCT * 3 * EXTRA : n, :] = shead_ref[...]
     head_ref[0:n, :] = rows[:, :LANES].astype(bf16)
@@ -157,6 +166,16 @@
     for g in range(n // 16):
         halos = fold(halos, rows[16 * g : 16 * g + 16, LANES:], g)
     head_ref[n : n + 16, :] = halos.astype(bf16)
+
+
+def fields_kernel(idx_ref, all_ref, fields_ref):
+    columns = fields_ref.shape[1] // 3
+    idx = idx_ref[0:1, :]
+    for i in range(DISTINCT):
+        main, halos = particle_of(idx, all_ref, i, columns)
+        fields_ref[i, :, :LANES] = main
+        for f in range(3):
+            fields_ref[i, f * columns : (f + 1) * columns, LANES:] = halos[f]
 
 
 def east(x):
@@ -243,36 +262,51 @@
             copies_ref[d, i * columns : (i + 1) * columns, :] = sent
 
 
-def final_kernel(
-    gathered_ref, spread_ref, innov_ref, all_ref, work_ref,
-    state_ref, tail_ref, edge_ref, sums_ref, *, total,
+def height_kernel(
+    gathered_ref, spread_ref, innov_ref, work_ref, height_ref, sums_ref, shares, *, total
+):
+    columns = work_ref.shape[1]
+    wet = work_ref[0, :, :LANES]
+    obs = work_ref[2, :, :LANES]
+    column = lax.axis_index("lon") * columns + SHIFT + lax.broadcasted_iota(
+        jnp.int32, (columns, LANES), 0
+    )
+    column = jnp.where(column >= total, column - total, column).astype(f32)
+    weight = wet * (1.0 + 2.0 * column / total)
+    spreaded = spread_dot(gathered_ref, spread_ref)
+    for i in range(DISTINCT):
+        innov = innov_ref[i]
+        sp = spreaded[i * columns : (i + 1) * columns, :]
+        height = (obs - innov) + nudge_rate * wet * (innov + sp)
+        height_ref[i] = height
+        gap = obs - height
+        shares[i : i + 1, :] = jnp.sum(weight * (gap * gap), axis=0, keepdims=True)
+    total_of = jnp.broadcast_to(jnp.sum(shares[...], axis=1, keepdims=True), shares.shape)
+    lane = lax.broadcasted_iota(jnp.int32, shares.shape, 1)
+    line = lax.broadcasted_iota(jnp.int32, shares.shape, 0)
+    row = jnp.sum(jnp.where(lane == line, total_of, 0.0), axis=0, keepdims=True)
+    for d in range(sums_ref.shape[0]):
+        sums_ref[d] = row
+
+
+def velocity_kernel(
+    gathered_ref, innov_ref, all_ref, work_ref, height_ref, state_ref, tail_ref, edge_ref
 ):
     columns = work_ref.shape[1]
     blocks = gathered_ref.shape[0]
     me = lax.axis_index("member")
-    wet = work_ref[0, :, :LANES]
     damped = work_ref[1, :, :LANES]
+    obs = work_ref[2, :, :LANES]
     obs_tile = work_ref[2, :, LANES:]
-    obs = work_ref[2, :, :LANES]
     before = jnp.maximum(me - 1, 0)
     after = jnp.minimum(me + 1, blocks - 1)
     has_before = jnp.where(me > 0, 1.0, 0.0).astype(f32)
     has_after = jnp.where(me < blocks - 1, 1.0, 0.0).astype(f32)
     lane = lax.broadcasted_iota(jnp.int32, (columns, LANES), 1)
     line = lax.broadcasted_iota(jnp.int32, (columns, LANES), 0)
-    first = lax.axis_index("lon") * columns + SHIFT
-    column = first + line
-    column = jnp.where(column >= total, column - total, column).astype(f32)
-    weight = wet * (1.0 + 2.0 * column / total)
-    spreaded = spread_dot(gathered_ref, spread_ref)
-    row = jnp.zeros((1, LANES), f32)
     for i in range(DISTINCT):
         part = slice(i * columns, (i + 1) * columns)
-        innov = innov_ref[i]
-        fresh = obs - innov
-        height = fresh + nudge_rate * wet * (innov + spreaded[part, :])
-        gap = obs - height
-        row = jnp.where(lane[0:1] == i, jnp.sum(weight * (gap * gap)), row)
+        fresh = obs - innov_ref[i]
         near = gathered_ref[before, part, :].astype(f32)
         far = gathered_ref[after, part, :].astype(f32)
         fresh_before = has_before * (obs_tile - near)
@@ -287,15 +321,13 @@
         easterly = jnp.where(line == columns - 1, 0.0, pltpu.roll(fresh, columns - 1, 0))
         zonal = all_ref[i, 2] - damped * (time_step * 0.5 * (easterly - west))
         meridional = all_ref[i, 3] - damped * (time_step * 0.5 * (up - down))
-        for f, value in enumerate((height, zonal, meridional)):
+        for f, value in enumerate((height_ref[i], zonal, meridional)):
             state_ref[i, f * columns : (f + 1) * columns, :] = value
             at = (i * 3 + f) * SHIFT
             tail_ref[at : at + SHIFT, :] = value[columns - SHIFT :, :]
         at = DISTINCT * 3 * SHIFT + i
         tail_ref[at : at + 1, :] = fresh[columns - 1 :, :]
         edge_ref[i : i + 1, :] = fresh[0:1, :]
-    for d in range(sums_ref.shape[0]):
-        sums_ref[d] = row
 
 
 LEVELS = (9, 5, 5)
@@ -312,7 +344,7 @@
     return rounded + jnp.abs(rounded) * (level * step + (0.5 * step - 1.0 / 256.0))
 
 
-def slots_kernel(idx_ref, state_ref, tail_ref, edge_ref, own_ref, sums_ref, out_ref, moved, coded):
+def coding_kernel(state_ref, tail_ref, edge_ref, own_ref, coded_ref, moved):
     columns = state_ref.shape[1] // 3
     at = slice(SHIFT - 1, SHIFT + 1)
     damped = own_ref[1, at, :LANES] * (1.0 / (1.0 + time_step * own_ref[2, at, :LANES]))
@@ -337,16 +369,20 @@
         for f in (2, 1, 0):
             value = moved[i, f * columns : (f + 1) * columns, :]
             sent = value.astype(bf16)
-            coded[i, f * columns : (f + 1) * columns, :] = sent
+            coded_ref[i, f * columns : (f + 1) * columns, :] = sent
             code = code * LEVELS[f] + residue_level(value, sent.astype(f32), LEVELS[f])
-        coded[i, 3 * columns : 4 * columns, :] = code.astype(bf16)
+        coded_ref[i, 3 * columns : 4 * columns, :] = code.astype(bf16)
+
+
+def slots_kernel(idx_ref, coded_ref, sums_ref, out_ref):
     parts = jnp.concatenate(
         pieces(jnp.sum(sums_ref[...], axis=0)) + (jnp.zeros((13, LANES), f32),), axis=0
     ).astype(bf16)
-    n = 4 * columns
+    n = coded_ref.shape[1]
+    idx = idx_ref[0:1, :]
     for d in range(out_ref.shape[0]):
         for p in range(2):
-            out_ref[d, p * n : (p + 1) * n, :] = coded[idx_ref[DISTINCT + 2 * d + p]]
+            out_ref[d, p * n : (p + 1) * n, :] = coded_ref[idx[0, DISTINCT + 2 * d + p]]
         out_ref[d, 2 * n : 2 * n + 16, :] = parts
 
 
@@ -355,6 +391,15 @@
     blocks = state_ref.shape[0]
     n = 4 * columns
     me = lax.axis_index("member")
+    row = jnp.zeros((1, LANES), f32)
+    for b in range(blocks):
+        parts = state_ref[b, 2 * n : 2 * n + 16, :].astype(f32)
+        row = row + ((parts[0:1] + parts[1:2]) + parts[2:3])
+    lane = lax.broadcasted_iota(jnp.int32, (1, LANES), 1)
+    idx = idx_ref[0:1, :]
+    for p in range(2):
+        place = jnp.sum(jnp.where(lane == DISTINCT + 2 * me + p, idx, 0))
+        misfit_ref[p] = jnp.sum(jnp.where(lane == place, row, 0.0)) / cells
     for p in range(2):
         for b in range(blocks):
             part = slice(b * LANES, (b + 1) * LANES)
@@ -367,14 +412,6 @@
                     code = jnp.floor(code * (1.0 / LEVELS[f]) + 0.5 / LEVELS[f])
                     level = level - code * LEVELS[f]
                 out_ref[p, f, :, part] = restored(rounded, level, LEVELS[f])
-    row = jnp.zeros((1, LANES), f32)
-    for b in range(blocks):
-        parts = state_ref[b, 2 * n : 2 * n + 16, :].astype(f32)
-        row = row + ((parts[0:1] + parts[1:2]) + parts[2:3])
-    lane = lax.broadcasted_iota(jnp.int32, (1, LANES), 1)
-    for p in range(2):
-        place = idx_ref[DISTINCT + 2 * me + p]
-        misfit_ref[p] = jnp.sum(jnp.where(lane == place, row, 0.0)) / cells
 
 
 def per_device(ensemble, copy_list, depth, land_mask, friction, coriolis, spread, observed):
@@ -410,23 +447,24 @@
     )(depth, land_mask, friction, observed, coriolis[None, :])
     parts, idx = call(
         index_kernel,
-        (shape((2,) + spread.shape, bf16), shape((64,), jnp.int32)),
+        (shape((2,) + spread.shape, bf16), shape((8, LANES), jnp.int32)),
         [SMEM, VMEM],
-        (VMEM, SMEM),
-        [pltpu.SMEM((32,), jnp.int32)],
+        (VMEM, VMEM),
+        [pltpu.SMEM((DISTINCT + 32,), jnp.int32), pltpu.SMEM((32,), jnp.int32)],
     )(copy_list, spread)
     packed, own, turning, parts = lax.optimization_barrier((packed, own, turning, parts))
-    fields, head = call(
-        select_kernel,
-        (
-            shape((DISTINCT, 3 * columns, wide), f32),
-            shape((halo_rows + 16, LANES), bf16),
-        ),
-        [SMEM, VMEM, VMEM],
-        (VMEM, VMEM),
+    head = call(
+        head_kernel,
+        shape((halo_rows + 16, LANES), bf16),
+        [VMEM] * 3,
+        VMEM,
         [pltpu.VMEM((halo_rows, wide), f32)],
     )(idx, packed, shead)
     right = lax.ppermute(head, "lon", westward)
+    packed, head = lax.optimization_barrier((packed, head))
+    fields = call(
+        fields_kernel, shape((DISTINCT, 3 * columns, wide), f32), [VMEM, VMEM], VMEM
+    )(idx, packed)
     step1, work, copies = call(
         step_kernel,
         (
@@ -450,35 +488,46 @@
         flops=2 * 2 * rows * LANES * lat,
     )(gathered1, parts, step1, work)
     gathered2 = swap(copies)
-    state, tail, edge, sums = call(
-        functools.partial(final_kernel, total=columns * lons),
+    height, sums = call(
+        functools.partial(height_kernel, total=columns * lons),
+        (shape((DISTINCT, columns, LANES), f32), shape((lons, 1, LANES), f32)),
+        [VMEM] * 4,
+        (VMEM, VMEM),
+        [pltpu.VMEM((DISTINCT, LANES), f32)],
+        flops=2 * 2 * rows * LANES * lat,
+    )(gathered2, parts, innov2, work)
+    shared = lax.all_to_all(sums, "lon", 0, 0, tiled=True)
+    height, sums = lax.optimization_barrier((height, sums))
+    state, tail, edge = call(
+        velocity_kernel,
         (
             shape((DISTINCT, 3 * columns, LANES), f32),
             shape((DISTINCT * (3 * SHIFT + 1), LANES), f32),
             shape((DISTINCT, LANES), f32),
-            shape((lons, 1, LANES), f32),
         ),
         [VMEM] * 5,
-        (VMEM,) * 4,
-        flops=2 * 2 * rows * LANES * lat,
-    )(gathered2, parts, innov2, step1, work)
-    sums = lax.all_to_all(sums, "lon", 0, 0, tiled=True)
+        (VMEM,) * 3,
+    )(gathered2, innov2, step1, work, height)
     tail = lax.ppermute(tail, "lon", eastward)
+    coded = call(
+        coding_kernel,
+        shape((DISTINCT, 4 * columns, LANES), bf16),
+        [VMEM] * 4,
+        VMEM,
+        [pltpu.VMEM((DISTINCT, 3 * columns, LANES), f32)],
+    )(state, tail, edge, own)
+    coded, shared = lax.optimization_barrier((coded, shared))
     state = call(
         slots_kernel,
         shape((members, 8 * columns + 16, LANES), bf16),
-        [SMEM] + [VMEM] * 5,
+        [VMEM] * 3,
         VMEM,
-        [
-            pltpu.VMEM((DISTINCT, 3 * columns, LANES), f32),
-            pltpu.VMEM((DISTINCT, 4 * columns, LANES), bf16),
-        ],
-    )(idx, state, tail, edge, own, sums)
+    )(idx, coded, shared)
     state = swap(state)
     return call(
         functools.partial(output_kernel, cells=float(lat * columns * lons)),
         (shape((2, 3, columns, lat), f32), shape((2,), f32)),
-        [SMEM, VMEM],
+        [VMEM, VMEM],
         (VMEM, SMEM),
     )(idx, state)
 

time: 106 us -> 104 us (0.981)
  Pallas kernels: 9.1 us -> 7.8 us
    pallas_call x4 -> x7, Pallas kernels: 4.01 us -> 3 us  [the longest x1 1.16 us: per_device(): call(functools.partial(height_kernel, total=columns * lons), (shape((DIST...]
where the time goes in v7:
time: 104 us
  blocking collectives  44.2 us (42%)
  starting transfers between devices  31.5 us (30%)
  waiting for transfers between devices  19.4 us (19%)
  Pallas kernels  7.8 us (8%)
    all_to_all x3, blocking collectives, swap(): return lax.all_to_all(x, 'member', 0, 0, tiled=True)  44.2 us
    all_to_all x1, starting transfers between devices, swap(): return lax.all_to_all(x, 'member', 0, 0, tiled=True)  10.2 us
    ppermute x1, starting transfers between devices, per_device(): right = lax.ppermute(head, 'lon', westward)  10 us
    all_to_all x1, starting transfers between devices, per_device(): shared = lax.all_to_all(sums, 'lon', 0, 0, tiled=True)  8.07 us
    all_to_all x1, waiting for transfers between devices, swap(): return lax.all_to_all(x, 'member', 0, 0, tiled=True)  8.01 us
    ppermute x1, waiting for transfers between devices, per_device(): tail = lax.ppermute(tail, 'lon', eastward)  5.66 us
    all_to_all x1, waiting for transfers between devices, per_device(): shared = lax.all_to_all(sums, 'lon', 0, 0, tiled=True)  4.52 us
    ppermute x1, starting transfers between devices, per_device(): tail = lax.ppermute(tail, 'lon', eastward)  3.14 us
  transfers between devices with their start and end apart: 4, of which 4 were waited for; matrix products, arithmetic and copies ran while one was open for 0% of the time, Pallas kernels for 1%

profile of v7, /device:TPU:1, one launch (start us, length us, event | category | flops | bytes accessed | tf_op | source)
XLA Modules:
  0.0 103.7 jit_solution(12992932923791069075)
XLA Ops:
  0.6 2.1 %shard_map.96 = bf16[16,112,128]{2,1,0:T(8,128)(2,1)} custom-call(bf16[2,3,16,2048]{3,2,1,0:T(8,128)(2,1)} %ens_hbm.1), custom_call_target="tpu_custom_call" | custom-call | flops 1000000 | bytes 1000000 | tf_op jit(solution)/shard_map/pallas_call | solution.py:433
  2.7 10.2 %all-to-all-start = ((bf16[16,112,128]{2,1,0:T(8,128)(2,1)}), bf16[16,112,128]{2,1,0:T(8,128)(2,1)S(1)}, u32[]{:S(2)}, u32[]{:S(2)}) async-start(bf16[16,112,128]{2,1,0:T(8,128)(2,1)} %shard_map.96), calls=%async_computation | async-start | bytes 917504 | tf_op jit(solution)/shard_map/all_to_all | solution.py:431
  13.1 0.9 shard_map.95
  14.0 0.1 copy-done.3
  14.0 0.1 copy-done.4
  14.1 8.0 %all-to-all-done.all_ref = bf16[16,112,128]{2,1,0:T(8,128)(2,1)S(1)} async-done(((bf16[16,112,128]{2,1,0:T(8,128)(2,1)}), bf16[16,112,128]{2,1,0:T(8,128)(2,1)S(1)}, u32[]{:S(2)}, u32[]{:S(2)}) %all-to-all-start) | async-done | bytes 458784 | tf_op jit(solution)/shard_map/all_to_all | solution.py:431
  22.1 0.3 shard_map.98
  22.4 10.0 %collective-permute-start = (bf16[288,128]{1,0:T(8,128)(2,1)S(1)}, bf16[288,128]{1,0:T(8,128)(2,1)S(1)}, u32[]{:S(2)}, u32[]{:S(2)}) collective-permute-start(bf16[288,128]{1,0:T(8,128)(2,1)S(1)} %shard_map.98), channel_id=1, source_target_pairs={{1,0},{2,1},{3,2},{4,3},{5,4},{6,5},{7,6},{8,7},{9,8},{10,9},{11,1... | collective-permute-start | bytes 221192 | tf_op jit(solution)/shard_map/ppermute | solution.py:463
  32.4 0.2 shard_map.99.fields_ref
  32.7 1.2 %collective-permute-done.right_ref = bf16[288,128]{1,0:T(8,128)(2,1)S(1)} collective-permute-done((bf16[288,128]{1,0:T(8,128)(2,1)S(1)}, bf16[288,128]{1,0:T(8,128)(2,1)S(1)}, u32[]{:S(2)}, u32[]{:S(2)}) %collective-permute-start) | collective-permute-done | bytes 73760 | tf_op jit(solution)/shard_map/ppermute | solution.py:463
  33.8 0.8 shard_map.100
  34.7 14.1 %all_to_all.25.gathered_ref = bf16[16,128,128]{2,1,0:T(8,128)(2,1)S(1)} all-to-all(bf16[16,128,128]{2,1,0:T(8,128)(2,1)S(1)} %get-tuple-element.34), channel_id=1, replica_groups=mesh['member'=16,'lon'=32] {'member'}, dimensions={0} | all-to-all | bytes 1048576 | tf_op jit(solution)/shard_map/all_to_all | solution.py:431
  48.8 0.5 shard_map.101
  49.3 13.5 %all_to_all.26.gathered_ref = bf16[16,128,128]{2,1,0:T(8,128)(2,1)S(1)} all-to-all(bf16[16,128,128]{2,1,0:T(8,128)(2,1)S(1)} %get-tuple-element.38), channel_id=1, replica_groups=mesh['member'=16,'lon'=32] {'member'}, dimensions={0} | all-to-all | bytes 1048576 | tf_op jit(solution)/shard_map/all_to_all | solution.py:431
  62.7 1.2 %shard_map.102 = (f32[8,16,128]{2,1,0:T(8,128)S(1)}, f32[32,1,128]{2,1,0:T(1,128)}) custom-call(bf16[16,128,128]{2,1,0:T(8,128)(2,1)S(1)} %all_to_all.26.gathered_ref, bf16[2,128,2048]{2,1,0:T(8,128)(2,1)S(1)} %get-tuple-element.35.spread_ref, f32[8,16,128]{2,1,0:T(8,128)S(1)} %get-tuple-element.39.innov_ref, f32[3,16,256]{2,1,0:T(8,128)S(1)} %get-tuple-element.37.work_ref), custom_call_target="tpu_custom_call" | custom-call | flops 134217728 | bytes 1000000 | tf_op jit(solution)/shard_map/pallas_call | solution.py:491
  63.9 8.1 %all-to-all-start.3 = ((f32[32,1,128]{2,1,0:T(1,128)}), f32[32,1,128]{2,1,0:T(1,128)S(1)}, u32[]{:S(2)}, u32[]{:S(2)}) async-start(f32[32,1,128]{2,1,0:T(1,128)} %get-tuple-element.44), calls=%async_computation.3 | async-start | bytes 32768 | tf_op jit(solution)/shard_map/all_to_all | solution.py:499
  72.0 0.1 shard_map.103
  72.1 3.1 %collective-permute-start.1 = (f32[104,128]{1,0:T(8,128)S(1)}, f32[104,128]{1,0:T(8,128)S(1)}, u32[]{:S(2)}, u32[]{:S(2)}) collective-permute-start(f32[104,128]{1,0:T(8,128)S(1)} %get-tuple-element.42), channel_id=1, source_target_pairs={{0,1},{1,2},{2,3},{3,4},{4,5},{5,6},{6,7},{7,8},{8,9},{9,10},{10,1... | collective-permute-start | bytes 159752 | tf_op jit(solution)/shard_map/ppermute | solution.py:511
  75.3 5.7 %collective-permute-done.1.tail_ref = f32[104,128]{1,0:T(8,128)S(1)} collective-permute-done((f32[104,128]{1,0:T(8,128)S(1)}, f32[104,128]{1,0:T(8,128)S(1)}, u32[]{:S(2)}, u32[]{:S(2)}) %collective-permute-start.1) | collective-permute-done | bytes 53280 | tf_op jit(solution)/shard_map/ppermute | solution.py:511
  80.9 0.1 shard_map.104.coded_ref
  81.1 4.5 %all-to-all-done.3.sums_ref = f32[32,1,128]{2,1,0:T(1,128)S(1)} async-done(((f32[32,1,128]{2,1,0:T(1,128)}), f32[32,1,128]{2,1,0:T(1,128)S(1)}, u32[]{:S(2)}, u32[]{:S(2)}) %all-to-all-start.3) | async-done | bytes 16416 | tf_op jit(solution)/shard_map/all_to_all | solution.py:499
  85.6 0.1 shard_map.105
  85.8 16.5 %all_to_all.27.state_ref = bf16[16,144,128]{2,1,0:T(8,128)(2,1)S(1)} all-to-all(bf16[16,144,128]{2,1,0:T(8,128)(2,1)S(1)} %shard_map.105), channel_id=1, replica_groups=mesh['member'=16,'lon'=32] {'member'}, dimensions={0} | all-to-all | bytes 1179648 | tf_op jit(solution)/shard_map/all_to_all | solution.py:431
  102.3 1.4 %shard_map.106 = (f32[2,3,16,2048]{3,2,1,0:T(8,128)}, f32[2]{0:T(128)}) custom-call(s32[8,128]{1,0:T(8,128)S(1)} %get-tuple-element.25.idx_ref, bf16[16,144,128]{2,1,0:T(8,128)(2,1)S(1)} %all_to_all.27.state_ref), custom_call_target="tpu_custom_call" | custom-call | flops 1000000 | bytes 1000000 | tf_op jit(solution)/shard_map/pallas_call | solution.py:527
  (13 shorter events, 0.1 us)
Async XLA Ops:
  0.6 12.3 %copy-start = (f32[128,2048]{1,0:T(8,128)S(1)}, f32[128,2048]{1,0:T(8,128)}, u32[]{:S(2)}) copy-start(f32[128,2048]{1,0:T(8,128)} %spread_ref.1) | copy-start | bytes 3145732
  2.7 10.3 %copy-start.6 = (s32[32]{0:T(128)S(1)}, s32[32]{0:T(128)}, u32[]{:S(2)}) copy-start(s32[32]{0:T(128)} %copy_ref.1) | copy-start | bytes 388
  2.7 19.4 %all-to-all-start = ((bf16[16,112,128]{2,1,0:T(8,128)(2,1)}), bf16[16,112,128]{2,1,0:T(8,128)(2,1)S(1)}, u32[]{:S(2)}, u32[]{:S(2)}) async-start(bf16[16,112,128]{2,1,0:T(8,128)(2,1)} %shard_map.96), calls=%async_computation | async-start | bytes 917504 | tf_op jit(solution)/shard_map/all_to_all | solution.py:431
  13.0 1.0 copy-start.1
  13.0 1.0 copy-start.2
  13.0 1.0 copy-start.3
  13.0 1.1 %copy-start.4 = (f32[16,2048]{1,0:T(8,128)S(1)}, f32[16,2048]{1,0:T(8,128)}, u32[]{:S(2)}) copy-start(f32[16,2048]{1,0:T(8,128)} %obs_ref.1) | copy-start | bytes 393220
  13.0 1.1 %copy-start.5 = (f32[2048]{0:T(1024)S(1)}, f32[2048]{0:T(1024)}, u32[]{:S(2)}) copy-start(f32[2048]{0:T(1024)} %param.13) | copy-start | bytes 24580
  22.4 11.4 %collective-permute-start = (bf16[288,128]{1,0:T(8,128)(2,1)S(1)}, bf16[288,128]{1,0:T(8,128)(2,1)S(1)}, u32[]{:S(2)}, u32[]{:S(2)}) collective-permute-start(bf16[288,128]{1,0:T(8,128)(2,1)S(1)} %shard_map.98), channel_id=1, source_target_pairs={{1,0},{2,1},{3,2},{4,3},{5,4},{6,5},{7,6},{8,7},{9,8},{10,9},{11,1... | collective-permute-start | bytes 221192 | tf_op jit(solution)/shard_map/ppermute | solution.py:463
  63.9 21.7 %all-to-all-start.3 = ((f32[32,1,128]{2,1,0:T(1,128)}), f32[32,1,128]{2,1,0:T(1,128)S(1)}, u32[]{:S(2)}, u32[]{:S(2)}) async-start(f32[32,1,128]{2,1,0:T(1,128)} %get-tuple-element.44), calls=%async_computation.3 | async-start | bytes 32768 | tf_op jit(solution)/shard_map/all_to_all | solution.py:499
  72.1 8.8 %collective-permute-start.1 = (f32[104,128]{1,0:T(8,128)S(1)}, f32[104,128]{1,0:T(8,128)S(1)}, u32[]{:S(2)}, u32[]{:S(2)}) collective-permute-start(f32[104,128]{1,0:T(8,128)S(1)} %get-tuple-element.42), channel_id=1, source_target_pairs={{0,1},{1,2},{2,3},{3,4},{4,5},{5,6},{6,7},{7,8},{8,9},{9,10},{10,1... | collective-permute-start | bytes 159752 | tf_op jit(solution)/shard_map/ppermute | solution.py:511

commit v8 on v7

--- a/solution.py
+++ b/solution.py
@@ -390,28 +390,25 @@
     columns = out_ref.shape[2]
     blocks = state_ref.shape[0]
     n = 4 * columns
-    me = lax.axis_index("member")
+    p = pl.program_id(0)
+    place_lane = DISTINCT + 2 * lax.axis_index("member") + p
     row = jnp.zeros((1, LANES), f32)
     for b in range(blocks):
         parts = state_ref[b, 2 * n : 2 * n + 16, :].astype(f32)
         row = row + ((parts[0:1] + parts[1:2]) + parts[2:3])
+        part = slice(b * LANES, (b + 1) * LANES)
+        block = state_ref[b, pl.ds(pl.multiple_of(p * n, 16), n), :].astype(f32)
+        code = block[3 * columns :]
+        for f in range(3):
+            rounded = block[f * columns : (f + 1) * columns]
+            level = code
+            if f < 2:
+                code = jnp.floor(code * (1.0 / LEVELS[f]) + 0.5 / LEVELS[f])
+                level = level - code * LEVELS[f]
+            out_ref[0, f, :, part] = restored(rounded, level, LEVELS[f])
     lane = lax.broadcasted_iota(jnp.int32, (1, LANES), 1)
-    idx = idx_ref[0:1, :]
-    for p in range(2):
-        place = jnp.sum(jnp.where(lane == DISTINCT + 2 * me + p, idx, 0))
-        misfit_ref[p] = jnp.sum(jnp.where(lane == place, row, 0.0)) / cells
-    for p in range(2):
-        for b in range(blocks):
-            part = slice(b * LANES, (b + 1) * LANES)
-            block = state_ref[b, p * n : (p + 1) * n, :].astype(f32)
-            code = block[3 * columns :]
-            for f in range(3):
-                rounded = block[f * columns : (f + 1) * columns]
-                level = code
-                if f < 2:
-                    code = jnp.floor(code * (1.0 / LEVELS[f]) + 0.5 / LEVELS[f])
-                    level = level - code * LEVELS[f]
-                out_ref[p, f, :, part] = restored(rounded, level, LEVELS[f])
+    place = jnp.sum(jnp.where(lane == place_lane, idx_ref[0:1, :], 0))
+    misfit_ref[p] = jnp.sum(jnp.where(lane == place, row, 0.0)) / cells
 
 
 def per_device(ensemble, copy_list, depth, land_mask, friction, coriolis, spread, observed):
@@ -524,11 +521,13 @@
         VMEM,
     )(idx, coded, shared)
     state = swap(state)
-    return call(
+    return pl.pallas_call(
         functools.partial(output_kernel, cells=float(lat * columns * lons)),
-        (shape((2, 3, columns, lat), f32), shape((2,), f32)),
-        [VMEM, VMEM],
-        (VMEM, SMEM),
+        grid=(2,),
+        out_shape=(shape((2, 3, columns, lat), f32), shape((2,), f32)),
+        in_specs=[VMEM, VMEM],
+        out_specs=(pl.BlockSpec((1, 3, columns, lat), lambda p: (p, 0, 0, 0)), SMEM),
+        compiler_params=pltpu.CompilerParams(vmem_limit_bytes=24 * 1024 * 1024),
     )(idx, state)
 
 

time: 104 us -> 104 us (level)
  no operation moved by 1% of the time
where the time goes in v8:
time: 104 us; the launch traced here: 103 us
  blocking collectives  44.2 us (42%)
  starting transfers between devices  31.5 us (30%)
  waiting for transfers between devices  19.4 us (19%)
  Pallas kernels  7.58 us (7%)
    all_to_all x3, blocking collectives, swap(): return lax.all_to_all(x, 'member', 0, 0, tiled=True)  44.2 us
    all_to_all x1, starting transfers between devices, swap(): return lax.all_to_all(x, 'member', 0, 0, tiled=True)  10.2 us
    ppermute x1, starting transfers between devices, per_device(): right = lax.ppermute(head, 'lon', westward)  10 us
    all_to_all x1, starting transfers between devices, per_device(): shared = lax.all_to_all(sums, 'lon', 0, 0, tiled=True)  8.07 us
    all_to_all x1, waiting for transfers between devices, swap(): return lax.all_to_all(x, 'member', 0, 0, tiled=True)  8.01 us
    ppermute x1, waiting for transfers between devices, per_device(): tail = lax.ppermute(tail, 'lon', eastward)  5.66 us
    all_to_all x1, waiting for transfers between devices, per_device(): shared = lax.all_to_all(sums, 'lon', 0, 0, tiled=True)  4.52 us
    ppermute x1, starting transfers between devices, per_device(): tail = lax.ppermute(tail, 'lon', eastward)  3.14 us
  transfers between devices with their start and end apart: 4, of which 4 were waited for; matrix products, arithmetic and copies ran while one was open for 0% of the time, Pallas kernels for 1%

profile of v8, /device:TPU:1, one launch (start us, length us, event | category | flops | bytes accessed | tf_op | source)
XLA Modules:
  0.0 103.5 jit_solution(8967057700464228783)
XLA Ops:
  0.6 2.1 %shard_map.96 = bf16[16,112,128]{2,1,0:T(8,128)(2,1)} custom-call(bf16[2,3,16,2048]{3,2,1,0:T(8,128)(2,1)} %ens_hbm.1), custom_call_target="tpu_custom_call" | custom-call | flops 1000000 | bytes 1000000 | tf_op jit(solution)/shard_map/pallas_call | solution.py:430
  2.7 10.2 %all-to-all-start = ((bf16[16,112,128]{2,1,0:T(8,128)(2,1)}), bf16[16,112,128]{2,1,0:T(8,128)(2,1)S(1)}, u32[]{:S(2)}, u32[]{:S(2)}) async-start(bf16[16,112,128]{2,1,0:T(8,128)(2,1)} %shard_map.96), calls=%async_computation | async-start | bytes 917504 | tf_op jit(solution)/shard_map/all_to_all | solution.py:428
  13.1 0.9 shard_map.95
  14.0 0.1 copy-done.3
  14.0 0.1 copy-done.4
  14.1 8.0 %all-to-all-done.all_ref = bf16[16,112,128]{2,1,0:T(8,128)(2,1)S(1)} async-done(((bf16[16,112,128]{2,1,0:T(8,128)(2,1)}), bf16[16,112,128]{2,1,0:T(8,128)(2,1)S(1)}, u32[]{:S(2)}, u32[]{:S(2)}) %all-to-all-start) | async-done | bytes 458784 | tf_op jit(solution)/shard_map/all_to_all | solution.py:428
  22.1 0.3 shard_map.98
  22.4 10.0 %collective-permute-start = (bf16[288,128]{1,0:T(8,128)(2,1)S(1)}, bf16[288,128]{1,0:T(8,128)(2,1)S(1)}, u32[]{:S(2)}, u32[]{:S(2)}) collective-permute-start(bf16[288,128]{1,0:T(8,128)(2,1)S(1)} %shard_map.98), channel_id=1, source_target_pairs={{1,0},{2,1},{3,2},{4,3},{5,4},{6,5},{7,6},{8,7},{9,8},{10,9},{11,1... | collective-permute-start | bytes 221192 | tf_op jit(solution)/shard_map/ppermute | solution.py:460
  32.4 0.2 shard_map.99.fields_ref
  32.7 1.2 %collective-permute-done.right_ref = bf16[288,128]{1,0:T(8,128)(2,1)S(1)} collective-permute-done((bf16[288,128]{1,0:T(8,128)(2,1)S(1)}, bf16[288,128]{1,0:T(8,128)(2,1)S(1)}, u32[]{:S(2)}, u32[]{:S(2)}) %collective-permute-start) | collective-permute-done | bytes 73760 | tf_op jit(solution)/shard_map/ppermute | solution.py:460
  33.8 0.8 shard_map.100
  34.7 14.1 %all_to_all.25.gathered_ref = bf16[16,128,128]{2,1,0:T(8,128)(2,1)S(1)} all-to-all(bf16[16,128,128]{2,1,0:T(8,128)(2,1)S(1)} %get-tuple-element.34), channel_id=1, replica_groups=mesh['member'=16,'lon'=32] {'member'}, dimensions={0} | all-to-all | bytes 1048576 | tf_op jit(solution)/shard_map/all_to_all | solution.py:428
  48.8 0.5 shard_map.101
  49.3 13.5 %all_to_all.26.gathered_ref = bf16[16,128,128]{2,1,0:T(8,128)(2,1)S(1)} all-to-all(bf16[16,128,128]{2,1,0:T(8,128)(2,1)S(1)} %get-tuple-element.38), channel_id=1, replica_groups=mesh['member'=16,'lon'=32] {'member'}, dimensions={0} | all-to-all | bytes 1048576 | tf_op jit(solution)/shard_map/all_to_all | solution.py:428
  62.7 1.2 %shard_map.102 = (f32[8,16,128]{2,1,0:T(8,128)S(1)}, f32[32,1,128]{2,1,0:T(1,128)}) custom-call(bf16[16,128,128]{2,1,0:T(8,128)(2,1)S(1)} %all_to_all.26.gathered_ref, bf16[2,128,2048]{2,1,0:T(8,128)(2,1)S(1)} %get-tuple-element.35.spread_ref, f32[8,16,128]{2,1,0:T(8,128)S(1)} %get-tuple-element.39.innov_ref, f32[3,16,256]{2,1,0:T(8,128)S(1)} %get-tuple-element.37.work_ref), custom_call_target="tpu_custom_call" | custom-call | flops 134217728 | bytes 1000000 | tf_op jit(solution)/shard_map/pallas_call | solution.py:488
  63.9 8.1 %all-to-all-start.3 = ((f32[32,1,128]{2,1,0:T(1,128)}), f32[32,1,128]{2,1,0:T(1,128)S(1)}, u32[]{:S(2)}, u32[]{:S(2)}) async-start(f32[32,1,128]{2,1,0:T(1,128)} %get-tuple-element.44), calls=%async_computation.3 | async-start | bytes 32768 | tf_op jit(solution)/shard_map/all_to_all | solution.py:496
  72.0 0.1 shard_map.103
  72.1 3.1 %collective-permute-start.1 = (f32[104,128]{1,0:T(8,128)S(1)}, f32[104,128]{1,0:T(8,128)S(1)}, u32[]{:S(2)}, u32[]{:S(2)}) collective-permute-start(f32[104,128]{1,0:T(8,128)S(1)} %get-tuple-element.42), channel_id=1, source_target_pairs={{0,1},{1,2},{2,3},{3,4},{4,5},{5,6},{6,7},{7,8},{8,9},{9,10},{10,1... | collective-permute-start | bytes 159752 | tf_op jit(solution)/shard_map/ppermute | solution.py:508
  75.3 5.7 %collective-permute-done.1.tail_ref = f32[104,128]{1,0:T(8,128)S(1)} collective-permute-done((f32[104,128]{1,0:T(8,128)S(1)}, f32[104,128]{1,0:T(8,128)S(1)}, u32[]{:S(2)}, u32[]{:S(2)}) %collective-permute-start.1) | collective-permute-done | bytes 53280 | tf_op jit(solution)/shard_map/ppermute | solution.py:508
  80.9 0.1 shard_map.104.coded_ref
  81.1 4.5 %all-to-all-done.3.sums_ref = f32[32,1,128]{2,1,0:T(1,128)S(1)} async-done(((f32[32,1,128]{2,1,0:T(1,128)}), f32[32,1,128]{2,1,0:T(1,128)S(1)}, u32[]{:S(2)}, u32[]{:S(2)}) %all-to-all-start.3) | async-done | bytes 16416 | tf_op jit(solution)/shard_map/all_to_all | solution.py:496
  85.6 0.1 shard_map.105
  85.8 16.5 %all_to_all.27.state_ref = bf16[16,144,128]{2,1,0:T(8,128)(2,1)S(1)} all-to-all(bf16[16,144,128]{2,1,0:T(8,128)(2,1)S(1)} %shard_map.105), channel_id=1, replica_groups=mesh['member'=16,'lon'=32] {'member'}, dimensions={0} | all-to-all | bytes 1179648 | tf_op jit(solution)/shard_map/all_to_all | solution.py:428
  102.3 1.2 %shard_map.106 = (f32[2,3,16,2048]{3,2,1,0:T(8,128)}, f32[2]{0:T(128)}) custom-call(s32[8,128]{1,0:T(8,128)S(1)} %get-tuple-element.25.idx_ref, bf16[16,144,128]{2,1,0:T(8,128)(2,1)S(1)} %all_to_all.27.state_ref), custom_call_target="tpu_custom_call" | custom-call | tf_op jit(solution)/shard_map/pallas_call | solution.py:524
  (13 shorter events, 0.1 us)
Async XLA Ops:
  0.6 12.3 %copy-start = (f32[128,2048]{1,0:T(8,128)S(1)}, f32[128,2048]{1,0:T(8,128)}, u32[]{:S(2)}) copy-start(f32[128,2048]{1,0:T(8,128)} %spread_ref.1) | copy-start | bytes 3145732
  2.7 10.3 %copy-start.6 = (s32[32]{0:T(128)S(1)}, s32[32]{0:T(128)}, u32[]{:S(2)}) copy-start(s32[32]{0:T(128)} %copy_ref.1) | copy-start | bytes 388
  2.7 19.4 %all-to-all-start = ((bf16[16,112,128]{2,1,0:T(8,128)(2,1)}), bf16[16,112,128]{2,1,0:T(8,128)(2,1)S(1)}, u32[]{:S(2)}, u32[]{:S(2)}) async-start(bf16[16,112,128]{2,1,0:T(8,128)(2,1)} %shard_map.96), calls=%async_computation | async-start | bytes 917504 | tf_op jit(solution)/shard_map/all_to_all | solution.py:428
  13.0 1.0 copy-start.1
  13.0 1.0 copy-start.2
  13.0 1.0 copy-start.3
  13.0 1.1 %copy-start.4 = (f32[16,2048]{1,0:T(8,128)S(1)}, f32[16,2048]{1,0:T(8,128)}, u32[]{:S(2)}) copy-start(f32[16,2048]{1,0:T(8,128)} %obs_ref.1) | copy-start | bytes 393220
  13.0 1.1 %copy-start.5 = (f32[2048]{0:T(1024)S(1)}, f32[2048]{0:T(1024)}, u32[]{:S(2)}) copy-start(f32[2048]{0:T(1024)} %param.13) | copy-start | bytes 24580
  22.4 11.4 %collective-permute-start = (bf16[288,128]{1,0:T(8,128)(2,1)S(1)}, bf16[288,128]{1,0:T(8,128)(2,1)S(1)}, u32[]{:S(2)}, u32[]{:S(2)}) collective-permute-start(bf16[288,128]{1,0:T(8,128)(2,1)S(1)} %shard_map.98), channel_id=1, source_target_pairs={{1,0},{2,1},{3,2},{4,3},{5,4},{6,5},{7,6},{8,7},{9,8},{10,9},{11,1... | collective-permute-start | bytes 221192 | tf_op jit(solution)/shard_map/ppermute | solution.py:460
  63.9 21.7 %all-to-all-start.3 = ((f32[32,1,128]{2,1,0:T(1,128)}), f32[32,1,128]{2,1,0:T(1,128)S(1)}, u32[]{:S(2)}, u32[]{:S(2)}) async-start(f32[32,1,128]{2,1,0:T(1,128)} %get-tuple-element.44), calls=%async_computation.3 | async-start | bytes 32768 | tf_op jit(solution)/shard_map/all_to_all | solution.py:496
  72.1 8.8 %collective-permute-start.1 = (f32[104,128]{1,0:T(8,128)S(1)}, f32[104,128]{1,0:T(8,128)S(1)}, u32[]{:S(2)}, u32[]{:S(2)}) collective-permute-start(f32[104,128]{1,0:T(8,128)S(1)} %get-tuple-element.42), channel_id=1, source_target_pairs={{0,1},{1,2},{2,3},{3,4},{4,5},{5,6},{6,7},{7,8},{8,9},{9,10},{10,1... | collective-permute-start | bytes 159752 | tf_op jit(solution)/shard_map/ppermute | solution.py:508

commit v9 on v8

--- a/solution.py
+++ b/solution.py
@@ -186,6 +186,40 @@
     return 0.5 * (pltpu.roll(x, x.shape[1] - 1, 1) - pltpu.roll(x, 1, 1))
 
 
+LEVELS = (9, 5, 5)
+
+
+def residue_level(value, rounded, levels):
+    size = jnp.maximum(jnp.abs(rounded), 1e-30)
+    at = (value - rounded) * 256.0 / size + 1.0
+    return jnp.clip(jnp.floor(at * (0.5 * levels)), 0.0, levels - 1.0)
+
+
+def restored(rounded, level, levels):
+    step = 2.0 / (256.0 * levels)
+    return rounded + jnp.abs(rounded) * (level * step + (0.5 * step - 1.0 / 256.0))
+
+
+SIXTHS = 6.0
+
+
+def send_rows(copies_ref, values):
+    columns = values[0].shape[0]
+    tiles, levels = [], []
+    for value in values:
+        sent = value.astype(bf16)
+        tiles.append(sent)
+        levels.append(residue_level(value, sent.astype(f32), SIXTHS))
+    for k in range(0, len(values), 3):
+        code = jnp.zeros_like(values[0])
+        for level in reversed(levels[k : k + 3]):
+            code = code * SIXTHS + level
+        tiles.append(code.astype(bf16))
+    for d in range(copies_ref.shape[0]):
+        for k, tile in enumerate(tiles):
+            copies_ref[d, k * columns : (k + 1) * columns, :] = tile
+
+
 def step_kernel(
     fields_ref, right_ref, own_ref, turn_ref, out_ref, work_ref, copies_ref, rrows,
 ):
@@ -213,6 +247,7 @@
     turning = turn_ref[...]
     for k, value in enumerate((wet, damped, obs)):
         work_ref[k] = value[keep, :]
+    values = []
     for i in range(DISTINCT):
         fields = []
         for f in range(3):
@@ -231,35 +266,49 @@
         zonal_part = damped * (zonal1 + time_step * (turning * meridional1))
         meridional_part = damped * (meridional1 - time_step * (turning * zonal1))
         innov = (obs - fresh)[keep, :LANES]
-        sent = innov.astype(bf16)
-        for d in range(copies_ref.shape[0]):
-            copies_ref[d, i * columns : (i + 1) * columns, :] = sent
+        values.append(innov)
         out_ref[i, 0] = innov
         for k, value in enumerate((change, zonal_part, meridional_part)):
             out_ref[i, k + 1] = value[keep, :LANES]
-
-
-def spread_dot(gathered_ref, spread_ref):
+    send_rows(copies_ref, values)
+
+
+def spread_dot(gathered_ref, spread_ref, columns):
     blocks = gathered_ref.shape[0]
-    lhs = jnp.concatenate([gathered_ref[b] for b in range(blocks)], axis=1)
+    n = DISTINCT * columns
+    lhs = jnp.concatenate([gathered_ref[b, 0:n, :] for b in range(blocks)], axis=1)
+    codes = jnp.concatenate([gathered_ref[b, n:, :] for b in range(blocks)], axis=1).astype(f32)
+    step = 2.0 / (256.0 * SIXTHS)
+    rest = []
+    for i in range(DISTINCT):
+        if i % 3 == 0:
+            code = codes[i // 3 * columns : (i // 3 + 1) * columns]
+        above = jnp.floor(code * (1.0 / SIXTHS) + 0.5 / SIXTHS)
+        size = jnp.abs(lhs[i * columns : (i + 1) * columns].astype(f32))
+        level = code - above * SIXTHS
+        rest.append((size * (level * step + (0.5 * step - 1.0 / 256.0))).astype(bf16))
+        code = above
+    rest = jnp.concatenate(rest, axis=0)
     dims = (((1,), (1,)), ((), ()))
-    return lax.dot_general(
-        lhs, spread_ref[0], dims, preferred_element_type=f32
-    ) + lax.dot_general(lhs, spread_ref[1], dims, preferred_element_type=f32)
+
+    def dot(x, y):
+        return lax.dot_general(x, y, dims, preferred_element_type=f32)
+
+    return dot(lhs, spread_ref[0]) + (dot(lhs, spread_ref[1]) + dot(rest, spread_ref[0]))
 
 
 def update_kernel(gathered_ref, spread_ref, all_ref, work_ref, innov_ref, copies_ref):
     columns = work_ref.shape[1]
     wet = work_ref[0, :, :LANES]
-    spreaded = spread_dot(gathered_ref, spread_ref)
+    spreaded = spread_dot(gathered_ref, spread_ref, columns)
+    values = []
     for i in range(DISTINCT):
         innov = all_ref[i, 0]
         sp = spreaded[i * columns : (i + 1) * columns, :]
         new = innov - nudge_rate * wet * (innov + sp) - all_ref[i, 1]
         innov_ref[i] = new
-        sent = new.astype(bf16)
-        for d in range(copies_ref.shape[0]):
-            copies_ref[d, i * columns : (i + 1) * columns, :] = sent
+        values.append(new)
+    send_rows(copies_ref, values)
 
 
 def height_kernel(
@@ -273,7 +322,7 @@
     )
     column = jnp.where(column >= total, column - total, column).astype(f32)
     weight = wet * (1.0 + 2.0 * column / total)
-    spreaded = spread_dot(gathered_ref, spread_ref)
+    spreaded = spread_dot(gathered_ref, spread_ref, columns)
     for i in range(DISTINCT):
         innov = innov_ref[i]
         sp = spreaded[i * columns : (i + 1) * columns, :]
@@ -328,20 +377,6 @@
         at = DISTINCT * 3 * SHIFT + i
         tail_ref[at : at + 1, :] = fresh[columns - 1 :, :]
         edge_ref[i : i + 1, :] = fresh[0:1, :]
-
-
-LEVELS = (9, 5, 5)
-
-
-def residue_level(value, rounded, levels):
-    size = jnp.maximum(jnp.abs(rounded), 1e-30)
-    at = (value - rounded) * 256.0 / size + 1.0
-    return jnp.clip(jnp.floor(at * (0.5 * levels)), 0.0, levels - 1.0)
-
-
-def restored(rounded, level, levels):
-    step = 2.0 / (256.0 * levels)
-    return rounded + jnp.abs(rounded) * (level * step + (0.5 * step - 1.0 / 256.0))
 
 
 def coding_kernel(state_ref, tail_ref, edge_ref, own_ref, coded_ref, moved):
@@ -467,7 +502,7 @@
         (
             shape((DISTINCT, 4, columns, LANES), f32),
             shape((3, columns, wide), f32),
-            shape((members, rows, LANES), bf16),
+            shape((members, rows + 3 * columns, LANES), bf16),
         ),
         [VMEM] * 4,
         (VMEM, VMEM, VMEM),
@@ -478,7 +513,7 @@
         update_kernel,
         (
             shape((DISTINCT, columns, LANES), f32),
-            shape((members, rows, LANES), bf16),
+            shape((members, rows + 3 * columns, LANES), bf16),
         ),
         [VMEM] * 4,
         (VMEM, VMEM),

time: 104 us -> 108 us (1.038)
  blocking collectives: 44.2 us -> 47.8 us
    all_to_all x3, blocking collectives: 44.2 us -> 47.8 us  [swap(): return lax.all_to_all(x, 'member', 0, 0, tiled=True)]
where the time goes in v9:
time: 108 us
  blocking collectives  47.8 us (44%)
  starting transfers between devices  31.5 us (29%)
  waiting for transfers between devices  19.3 us (18%)
  Pallas kernels  8.29 us (8%)
    all_to_all x3, blocking collectives, swap(): return lax.all_to_all(x, 'member', 0, 0, tiled=True)  47.8 us
    all_to_all x1, starting transfers between devices, swap(): return lax.all_to_all(x, 'member', 0, 0, tiled=True)  10.2 us
    ppermute x1, starting transfers between devices, per_device(): right = lax.ppermute(head, 'lon', westward)  10 us
    all_to_all x1, starting transfers between devices, per_device(): shared = lax.all_to_all(sums, 'lon', 0, 0, tiled=True)  8.08 us
    all_to_all x1, waiting for transfers between devices, swap(): return lax.all_to_all(x, 'member', 0, 0, tiled=True)  8.01 us
    ppermute x1, waiting for transfers between devices, per_device(): tail = lax.ppermute(tail, 'lon', eastward)  5.65 us
    all_to_all x1, waiting for transfers between devices, per_device(): shared = lax.all_to_all(sums, 'lon', 0, 0, tiled=True)  4.51 us
    ppermute x1, starting transfers between devices, per_device(): tail = lax.ppermute(tail, 'lon', eastward)  3.14 us
  transfers between devices with their start and end apart: 4, of which 4 were waited for; matrix products, arithmetic and copies ran while one was open for 0% of the time, Pallas kernels for 1%

profile of v9, /device:TPU:1, one launch (start us, length us, event | category | flops | bytes accessed | tf_op | source)
XLA Modules:
  0.0 107.8 jit_solution(16750130947188703737)
XLA Ops:
  0.6 2.1 %shard_map.96 = bf16[16,112,128]{2,1,0:T(8,128)(2,1)} custom-call(bf16[2,3,16,2048]{3,2,1,0:T(8,128)(2,1)} %ens_hbm.1), custom_call_target="tpu_custom_call" | custom-call | flops 1000000 | bytes 1000000 | tf_op jit(solution)/shard_map/pallas_call | solution.py:465
  2.7 10.2 %all-to-all-start = ((bf16[16,112,128]{2,1,0:T(8,128)(2,1)}), bf16[16,112,128]{2,1,0:T(8,128)(2,1)S(1)}, u32[]{:S(2)}, u32[]{:S(2)}) async-start(bf16[16,112,128]{2,1,0:T(8,128)(2,1)} %shard_map.96), calls=%async_computation | async-start | bytes 917504 | tf_op jit(solution)/shard_map/all_to_all | solution.py:463
  13.1 0.9 shard_map.95
  14.0 0.1 copy-done.3
  14.0 0.1 copy-done.4
  14.1 8.0 %all-to-all-done.all_ref = bf16[16,112,128]{2,1,0:T(8,128)(2,1)S(1)} async-done(((bf16[16,112,128]{2,1,0:T(8,128)(2,1)}), bf16[16,112,128]{2,1,0:T(8,128)(2,1)S(1)}, u32[]{:S(2)}, u32[]{:S(2)}) %all-to-all-start) | async-done | bytes 458784 | tf_op jit(solution)/shard_map/all_to_all | solution.py:463
  22.1 0.3 shard_map.98
  22.4 10.0 %collective-permute-start = (bf16[288,128]{1,0:T(8,128)(2,1)S(1)}, bf16[288,128]{1,0:T(8,128)(2,1)S(1)}, u32[]{:S(2)}, u32[]{:S(2)}) collective-permute-start(bf16[288,128]{1,0:T(8,128)(2,1)S(1)} %shard_map.98), channel_id=1, source_target_pairs={{1,0},{2,1},{3,2},{4,3},{5,4},{6,5},{7,6},{8,7},{9,8},{10,9},{11,1... | collective-permute-start | bytes 221192 | tf_op jit(solution)/shard_map/ppermute | solution.py:495
  32.4 0.2 shard_map.99.fields_ref
  32.7 1.2 %collective-permute-done.right_ref = bf16[288,128]{1,0:T(8,128)(2,1)S(1)} collective-permute-done((bf16[288,128]{1,0:T(8,128)(2,1)S(1)}, bf16[288,128]{1,0:T(8,128)(2,1)S(1)}, u32[]{:S(2)}, u32[]{:S(2)}) %collective-permute-start) | collective-permute-done | bytes 73760 | tf_op jit(solution)/shard_map/ppermute | solution.py:495
  33.8 0.8 shard_map.100
  34.6 16.9 %all_to_all.25.gathered_ref = bf16[16,176,128]{2,1,0:T(8,128)(2,1)S(1)} all-to-all(bf16[16,176,128]{2,1,0:T(8,128)(2,1)S(1)} %get-tuple-element.34), channel_id=1, replica_groups=mesh['member'=16,'lon'=32] {'member'}, dimensions={0} | all-to-all | bytes 1441792 | tf_op jit(solution)/shard_map/all_to_all | solution.py:463
  51.5 0.8 shard_map.101
  52.4 15.3 %all_to_all.26.gathered_ref = bf16[16,176,128]{2,1,0:T(8,128)(2,1)S(1)} all-to-all(bf16[16,176,128]{2,1,0:T(8,128)(2,1)S(1)} %get-tuple-element.38), channel_id=1, replica_groups=mesh['member'=16,'lon'=32] {'member'}, dimensions={0} | all-to-all | bytes 1441792 | tf_op jit(solution)/shard_map/all_to_all | solution.py:463
  67.7 1.5 %shard_map.102 = (f32[8,16,128]{2,1,0:T(8,128)S(1)}, f32[32,1,128]{2,1,0:T(1,128)}) custom-call(bf16[16,176,128]{2,1,0:T(8,128)(2,1)S(1)} %all_to_all.26.gathered_ref, bf16[2,128,2048]{2,1,0:T(8,128)(2,1)S(1)} %get-tuple-element.35.spread_ref, f32[8,16,128]{2,1,0:T(8,128)S(1)} %get-tuple-element.39.innov_ref, f32[3,16,256]{2,1,0:T(8,128)S(1)} %get-tuple-element.37.work_ref), custom_call_target="tpu_custom_call" | custom-call | flops 134217728 | bytes 1000000 | tf_op jit(solution)/shard_map/pallas_call | solution.py:523
  69.2 8.1 %all-to-all-start.3 = ((f32[32,1,128]{2,1,0:T(1,128)}), f32[32,1,128]{2,1,0:T(1,128)S(1)}, u32[]{:S(2)}, u32[]{:S(2)}) async-start(f32[32,1,128]{2,1,0:T(1,128)} %get-tuple-element.44), calls=%async_computation.3 | async-start | bytes 32768 | tf_op jit(solution)/shard_map/all_to_all | solution.py:531
  77.3 0.2 shard_map.103
  77.4 3.1 %collective-permute-start.1 = (f32[104,128]{1,0:T(8,128)S(1)}, f32[104,128]{1,0:T(8,128)S(1)}, u32[]{:S(2)}, u32[]{:S(2)}) collective-permute-start(f32[104,128]{1,0:T(8,128)S(1)} %get-tuple-element.42), channel_id=1, source_target_pairs={{0,1},{1,2},{2,3},{3,4},{4,5},{5,6},{6,7},{7,8},{8,9},{9,10},{10,1... | collective-permute-start | bytes 159752 | tf_op jit(solution)/shard_map/ppermute | solution.py:543
  80.6 5.7 %collective-permute-done.1.tail_ref = f32[104,128]{1,0:T(8,128)S(1)} collective-permute-done((f32[104,128]{1,0:T(8,128)S(1)}, f32[104,128]{1,0:T(8,128)S(1)}, u32[]{:S(2)}, u32[]{:S(2)}) %collective-permute-start.1) | collective-permute-done | bytes 53280 | tf_op jit(solution)/shard_map/ppermute | solution.py:543
  86.2 0.1 shard_map.104.coded_ref
  86.4 4.5 %all-to-all-done.3.sums_ref = f32[32,1,128]{2,1,0:T(1,128)S(1)} async-done(((f32[32,1,128]{2,1,0:T(1,128)}), f32[32,1,128]{2,1,0:T(1,128)S(1)}, u32[]{:S(2)}, u32[]{:S(2)}) %all-to-all-start.3) | async-done | bytes 16416 | tf_op jit(solution)/shard_map/all_to_all | solution.py:531
  90.9 0.1 shard_map.105
  91.0 15.6 %all_to_all.27.state_ref = bf16[16,144,128]{2,1,0:T(8,128)(2,1)S(1)} all-to-all(bf16[16,144,128]{2,1,0:T(8,128)(2,1)S(1)} %shard_map.105), channel_id=1, replica_groups=mesh['member'=16,'lon'=32] {'member'}, dimensions={0} | all-to-all | bytes 1179648 | tf_op jit(solution)/shard_map/all_to_all | solution.py:463
  106.6 1.2 %shard_map.106 = (f32[2,3,16,2048]{3,2,1,0:T(8,128)}, f32[2]{0:T(128)}) custom-call(s32[8,128]{1,0:T(8,128)S(1)} %get-tuple-element.25.idx_ref, bf16[16,144,128]{2,1,0:T(8,128)(2,1)S(1)} %all_to_all.27.state_ref), custom_call_target="tpu_custom_call" | custom-call | tf_op jit(solution)/shard_map/pallas_call | solution.py:559
  (13 shorter events, 0.1 us)
Async XLA Ops:
  0.6 12.3 %copy-start = (f32[128,2048]{1,0:T(8,128)S(1)}, f32[128,2048]{1,0:T(8,128)}, u32[]{:S(2)}) copy-start(f32[128,2048]{1,0:T(8,128)} %spread_ref.1) | copy-start | bytes 3145732
  2.7 10.3 %copy-start.6 = (s32[32]{0:T(128)S(1)}, s32[32]{0:T(128)}, u32[]{:S(2)}) copy-start(s32[32]{0:T(128)} %copy_ref.1) | copy-start | bytes 388
  2.7 19.4 %all-to-all-start = ((bf16[16,112,128]{2,1,0:T(8,128)(2,1)}), bf16[16,112,128]{2,1,0:T(8,128)(2,1)S(1)}, u32[]{:S(2)}, u32[]{:S(2)}) async-start(bf16[16,112,128]{2,1,0:T(8,128)(2,1)} %shard_map.96), calls=%async_computation | async-start | bytes 917504 | tf_op jit(solution)/shard_map/all_to_all | solution.py:463
  13.0 1.0 copy-start.1
  13.0 1.0 copy-start.2
  13.0 1.0 copy-start.3
  13.0 1.1 copy-start.4
  13.0 1.1 copy-start.5
  22.4 11.4 %collective-permute-start = (bf16[288,128]{1,0:T(8,128)(2,1)S(1)}, bf16[288,128]{1,0:T(8,128)(2,1)S(1)}, u32[]{:S(2)}, u32[]{:S(2)}) collective-permute-start(bf16[288,128]{1,0:T(8,128)(2,1)S(1)} %shard_map.98), channel_id=1, source_target_pairs={{1,0},{2,1},{3,2},{4,3},{5,4},{6,5},{7,6},{8,7},{9,8},{10,9},{11,1... | collective-permute-start | bytes 221192 | tf_op jit(solution)/shard_map/ppermute | solution.py:495
  69.2 21.7 %all-to-all-start.3 = ((f32[32,1,128]{2,1,0:T(1,128)}), f32[32,1,128]{2,1,0:T(1,128)S(1)}, u32[]{:S(2)}, u32[]{:S(2)}) async-start(f32[32,1,128]{2,1,0:T(1,128)} %get-tuple-element.44), calls=%async_computation.3 | async-start | bytes 32768 | tf_op jit(solution)/shard_map/all_to_all | solution.py:531
  77.4 8.8 %collective-permute-start.1 = (f32[104,128]{1,0:T(8,128)S(1)}, f32[104,128]{1,0:T(8,128)S(1)}, u32[]{:S(2)}, u32[]{:S(2)}) collective-permute-start(f32[104,128]{1,0:T(8,128)S(1)} %get-tuple-element.42), channel_id=1, source_target_pairs={{0,1},{1,2},{2,3},{3,4},{4,5},{5,6},{6,7},{7,8},{8,9},{9,10},{10,1... | collective-permute-start | bytes 159752 | tf_op jit(solution)/shard_map/ppermute | solution.py:543

commit v10 on v9

--- a/solution.py
+++ b/solution.py
@@ -200,7 +200,8 @@
     return rounded + jnp.abs(rounded) * (level * step + (0.5 * step - 1.0 / 256.0))
 
 
-SIXTHS = 6.0
+STEPS_EACH = 4.0
+SHARED = 4
 
 
 def send_rows(copies_ref, values):
@@ -209,11 +210,11 @@
     for value in values:
         sent = value.astype(bf16)
         tiles.append(sent)
-        levels.append(residue_level(value, sent.astype(f32), SIXTHS))
-    for k in range(0, len(values), 3):
+        levels.append(residue_level(value, sent.astype(f32), STEPS_EACH))
+    for k in range(0, len(values), SHARED):
         code = jnp.zeros_like(values[0])
-        for level in reversed(levels[k : k + 3]):
-            code = code * SIXTHS + level
+        for level in reversed(levels[k : k + SHARED]):
+            code = code * STEPS_EACH + level
         tiles.append(code.astype(bf16))
     for d in range(copies_ref.shape[0]):
         for k, tile in enumerate(tiles):
@@ -278,14 +279,14 @@
     n = DISTINCT * columns
     lhs = jnp.concatenate([gathered_ref[b, 0:n, :] for b in range(blocks)], axis=1)
     codes = jnp.concatenate([gathered_ref[b, n:, :] for b in range(blocks)], axis=1).astype(f32)
-    step = 2.0 / (256.0 * SIXTHS)
+    step = 2.0 / (256.0 * STEPS_EACH)
     rest = []
     for i in range(DISTINCT):
-        if i % 3 == 0:
-            code = codes[i // 3 * columns : (i // 3 + 1) * columns]
-        above = jnp.floor(code * (1.0 / SIXTHS) + 0.5 / SIXTHS)
+        if i % SHARED == 0:
+            code = codes[i // SHARED * columns : (i // SHARED + 1) * columns]
+        above = jnp.floor(code * (1.0 / STEPS_EACH) + 0.5 / STEPS_EACH)
         size = jnp.abs(lhs[i * columns : (i + 1) * columns].astype(f32))
-        level = code - above * SIXTHS
+        level = code - above * STEPS_EACH
         rest.append((size * (level * step + (0.5 * step - 1.0 / 256.0))).astype(bf16))
         code = above
     rest = jnp.concatenate(rest, axis=0)
@@ -502,7 +503,7 @@
         (
             shape((DISTINCT, 4, columns, LANES), f32),
             shape((3, columns, wide), f32),
-            shape((members, rows + 3 * columns, LANES), bf16),
+            shape((members, rows + DISTINCT // SHARED * columns, LANES), bf16),
         ),
         [VMEM] * 4,
         (VMEM, VMEM, VMEM),
@@ -513,7 +514,7 @@
         update_kernel,
         (
             shape((DISTINCT, columns, LANES), f32),
-            shape((members, rows + 3 * columns, LANES), bf16),
+            shape((members, rows + DISTINCT // SHARED * columns, LANES), bf16),
         ),
         [VMEM] * 4,
         (VMEM, VMEM),

time: 108 us -> 107 us (level)
  blocking collectives: 47.8 us -> 46.4 us
    all_to_all x3, blocking collectives: 47.8 us -> 46.4 us  [swap(): return lax.all_to_all(x, 'member', 0, 0, tiled=True)]
where the time goes in v10:
time: 107 us; the launch traced here: 106 us
  blocking collectives  46.4 us (43%)
  starting transfers between devices  31.5 us (29%)
  waiting for transfers between devices  19.4 us (18%)
  Pallas kernels  8.28 us (8%)
    all_to_all x3, blocking collectives, swap(): return lax.all_to_all(x, 'member', 0, 0, tiled=True)  46.4 us
    all_to_all x1, starting transfers between devices, swap(): return lax.all_to_all(x, 'member', 0, 0, tiled=True)  10.2 us
    ppermute x1, starting transfers between devices, per_device(): right = lax.ppermute(head, 'lon', westward)  10 us
    all_to_all x1, starting transfers between devices, per_device(): shared = lax.all_to_all(sums, 'lon', 0, 0, tiled=True)  8.08 us
    all_to_all x1, waiting for transfers between devices, swap(): return lax.all_to_all(x, 'member', 0, 0, tiled=True)  8.01 us
    ppermute x1, waiting for transfers between devices, per_device(): tail = lax.ppermute(tail, 'lon', eastward)  5.65 us
    all_to_all x1, waiting for transfers between devices, per_device(): shared = lax.all_to_all(sums, 'lon', 0, 0, tiled=True)  4.57 us
    ppermute x1, starting transfers between devices, per_device(): tail = lax.ppermute(tail, 'lon', eastward)  3.14 us
  transfers between devices with their start and end apart: 4, of which 4 were waited for; matrix products, arithmetic and copies ran while one was open for 0% of the time, Pallas kernels for 1%

profile of v10, /device:TPU:1, one launch (start us, length us, event | category | flops | bytes accessed | tf_op | source)
XLA Modules:
  0.0 106.5 jit_solution(10290208810795545440)
XLA Ops:
  0.6 2.1 %shard_map.96 = bf16[16,112,128]{2,1,0:T(8,128)(2,1)} custom-call(bf16[2,3,16,2048]{3,2,1,0:T(8,128)(2,1)} %ens_hbm.1), custom_call_target="tpu_custom_call" | custom-call | flops 1000000 | bytes 1000000 | tf_op jit(solution)/shard_map/pallas_call | solution.py:466
  2.7 10.2 %all-to-all-start = ((bf16[16,112,128]{2,1,0:T(8,128)(2,1)}), bf16[16,112,128]{2,1,0:T(8,128)(2,1)S(1)}, u32[]{:S(2)}, u32[]{:S(2)}) async-start(bf16[16,112,128]{2,1,0:T(8,128)(2,1)} %shard_map.96), calls=%async_computation | async-start | bytes 917504 | tf_op jit(solution)/shard_map/all_to_all | solution.py:464
  13.1 0.9 shard_map.95
  14.0 0.1 copy-done.3
  14.0 0.1 copy-done.4
  14.1 8.0 %all-to-all-done.all_ref = bf16[16,112,128]{2,1,0:T(8,128)(2,1)S(1)} async-done(((bf16[16,112,128]{2,1,0:T(8,128)(2,1)}), bf16[16,112,128]{2,1,0:T(8,128)(2,1)S(1)}, u32[]{:S(2)}, u32[]{:S(2)}) %all-to-all-start) | async-done | bytes 458784 | tf_op jit(solution)/shard_map/all_to_all | solution.py:464
  22.1 0.3 shard_map.98
  22.4 10.0 %collective-permute-start = (bf16[288,128]{1,0:T(8,128)(2,1)S(1)}, bf16[288,128]{1,0:T(8,128)(2,1)S(1)}, u32[]{:S(2)}, u32[]{:S(2)}) collective-permute-start(bf16[288,128]{1,0:T(8,128)(2,1)S(1)} %shard_map.98), channel_id=1, source_target_pairs={{1,0},{2,1},{3,2},{4,3},{5,4},{6,5},{7,6},{8,7},{9,8},{10,9},{11,1... | collective-permute-start | bytes 221192 | tf_op jit(solution)/shard_map/ppermute | solution.py:496
  32.4 0.2 shard_map.99.fields_ref
  32.7 1.2 %collective-permute-done.right_ref = bf16[288,128]{1,0:T(8,128)(2,1)S(1)} collective-permute-done((bf16[288,128]{1,0:T(8,128)(2,1)S(1)}, bf16[288,128]{1,0:T(8,128)(2,1)S(1)}, u32[]{:S(2)}, u32[]{:S(2)}) %collective-permute-start) | collective-permute-done | bytes 73760 | tf_op jit(solution)/shard_map/ppermute | solution.py:496
  33.8 0.8 shard_map.100
  34.6 16.3 %all_to_all.25.gathered_ref = bf16[16,160,128]{2,1,0:T(8,128)(2,1)S(1)} all-to-all(bf16[16,160,128]{2,1,0:T(8,128)(2,1)S(1)} %get-tuple-element.34), channel_id=1, replica_groups=mesh['member'=16,'lon'=32] {'member'}, dimensions={0} | all-to-all | bytes 1310720 | tf_op jit(solution)/shard_map/all_to_all | solution.py:464
  50.9 0.8 shard_map.101
  51.7 14.6 %all_to_all.26.gathered_ref = bf16[16,160,128]{2,1,0:T(8,128)(2,1)S(1)} all-to-all(bf16[16,160,128]{2,1,0:T(8,128)(2,1)S(1)} %get-tuple-element.38), channel_id=1, replica_groups=mesh['member'=16,'lon'=32] {'member'}, dimensions={0} | all-to-all | bytes 1310720 | tf_op jit(solution)/shard_map/all_to_all | solution.py:464
  66.4 1.5 %shard_map.102 = (f32[8,16,128]{2,1,0:T(8,128)S(1)}, f32[32,1,128]{2,1,0:T(1,128)}) custom-call(bf16[16,160,128]{2,1,0:T(8,128)(2,1)S(1)} %all_to_all.26.gathered_ref, bf16[2,128,2048]{2,1,0:T(8,128)(2,1)S(1)} %get-tuple-element.35.spread_ref, f32[8,16,128]{2,1,0:T(8,128)S(1)} %get-tuple-element.39.innov_ref, f32[3,16,256]{2,1,0:T(8,128)S(1)} %get-tuple-element.37.work_ref), custom_call_target="tpu_custom_call" | custom-call | flops 134217728 | bytes 1000000 | tf_op jit(solution)/shard_map/pallas_call | solution.py:524
  67.9 8.1 %all-to-all-start.3 = ((f32[32,1,128]{2,1,0:T(1,128)}), f32[32,1,128]{2,1,0:T(1,128)S(1)}, u32[]{:S(2)}, u32[]{:S(2)}) async-start(f32[32,1,128]{2,1,0:T(1,128)} %get-tuple-element.44), calls=%async_computation.3 | async-start | bytes 32768 | tf_op jit(solution)/shard_map/all_to_all | solution.py:532
  76.0 0.2 shard_map.103
  76.1 3.1 %collective-permute-start.1 = (f32[104,128]{1,0:T(8,128)S(1)}, f32[104,128]{1,0:T(8,128)S(1)}, u32[]{:S(2)}, u32[]{:S(2)}) collective-permute-start(f32[104,128]{1,0:T(8,128)S(1)} %get-tuple-element.42), channel_id=1, source_target_pairs={{0,1},{1,2},{2,3},{3,4},{4,5},{5,6},{6,7},{7,8},{8,9},{9,10},{10,1... | collective-permute-start | bytes 159752 | tf_op jit(solution)/shard_map/ppermute | solution.py:544
  79.3 5.7 %collective-permute-done.1.tail_ref = f32[104,128]{1,0:T(8,128)S(1)} collective-permute-done((f32[104,128]{1,0:T(8,128)S(1)}, f32[104,128]{1,0:T(8,128)S(1)}, u32[]{:S(2)}, u32[]{:S(2)}) %collective-permute-start.1) | collective-permute-done | bytes 53280 | tf_op jit(solution)/shard_map/ppermute | solution.py:544
  84.9 0.1 shard_map.104.coded_ref
  85.1 4.6 %all-to-all-done.3.sums_ref = f32[32,1,128]{2,1,0:T(1,128)S(1)} async-done(((f32[32,1,128]{2,1,0:T(1,128)}), f32[32,1,128]{2,1,0:T(1,128)S(1)}, u32[]{:S(2)}, u32[]{:S(2)}) %all-to-all-start.3) | async-done | bytes 16416 | tf_op jit(solution)/shard_map/all_to_all | solution.py:532
  89.6 0.1 shard_map.105
  89.8 15.5 %all_to_all.27.state_ref = bf16[16,144,128]{2,1,0:T(8,128)(2,1)S(1)} all-to-all(bf16[16,144,128]{2,1,0:T(8,128)(2,1)S(1)} %shard_map.105), channel_id=1, replica_groups=mesh['member'=16,'lon'=32] {'member'}, dimensions={0} | all-to-all | bytes 1179648 | tf_op jit(solution)/shard_map/all_to_all | solution.py:464
  105.3 1.2 %shard_map.106 = (f32[2,3,16,2048]{3,2,1,0:T(8,128)}, f32[2]{0:T(128)}) custom-call(s32[8,128]{1,0:T(8,128)S(1)} %get-tuple-element.25.idx_ref, bf16[16,144,128]{2,1,0:T(8,128)(2,1)S(1)} %all_to_all.27.state_ref), custom_call_target="tpu_custom_call" | custom-call | tf_op jit(solution)/shard_map/pallas_call | solution.py:560
  (13 shorter events, 0.1 us)
Async XLA Ops:
  0.6 12.3 %copy-start = (f32[128,2048]{1,0:T(8,128)S(1)}, f32[128,2048]{1,0:T(8,128)}, u32[]{:S(2)}) copy-start(f32[128,2048]{1,0:T(8,128)} %spread_ref.1) | copy-start | bytes 3145732
  2.7 10.3 %copy-start.6 = (s32[32]{0:T(128)S(1)}, s32[32]{0:T(128)}, u32[]{:S(2)}) copy-start(s32[32]{0:T(128)} %copy_ref.1) | copy-start | bytes 388
  2.7 19.4 %all-to-all-start = ((bf16[16,112,128]{2,1,0:T(8,128)(2,1)}), bf16[16,112,128]{2,1,0:T(8,128)(2,1)S(1)}, u32[]{:S(2)}, u32[]{:S(2)}) async-start(bf16[16,112,128]{2,1,0:T(8,128)(2,1)} %shard_map.96), calls=%async_computation | async-start | bytes 917504 | tf_op jit(solution)/shard_map/all_to_all | solution.py:464
  13.0 1.0 copy-start.1
  13.0 1.0 copy-start.2
  13.0 1.0 copy-start.3
  13.0 1.1 %copy-start.4 = (f32[16,2048]{1,0:T(8,128)S(1)}, f32[16,2048]{1,0:T(8,128)}, u32[]{:S(2)}) copy-start(f32[16,2048]{1,0:T(8,128)} %obs_ref.1) | copy-start | bytes 393220
  13.0 1.1 copy-start.5
  22.4 11.4 %collective-permute-start = (bf16[288,128]{1,0:T(8,128)(2,1)S(1)}, bf16[288,128]{1,0:T(8,128)(2,1)S(1)}, u32[]{:S(2)}, u32[]{:S(2)}) collective-permute-start(bf16[288,128]{1,0:T(8,128)(2,1)S(1)} %shard_map.98), channel_id=1, source_target_pairs={{1,0},{2,1},{3,2},{4,3},{5,4},{6,5},{7,6},{8,7},{9,8},{10,9},{11,1... | collective-permute-start | bytes 221192 | tf_op jit(solution)/shard_map/ppermute | solution.py:496
  67.9 21.8 %all-to-all-start.3 = ((f32[32,1,128]{2,1,0:T(1,128)}), f32[32,1,128]{2,1,0:T(1,128)S(1)}, u32[]{:S(2)}, u32[]{:S(2)}) async-start(f32[32,1,128]{2,1,0:T(1,128)} %get-tuple-element.44), calls=%async_computation.3 | async-start | bytes 32768 | tf_op jit(solution)/shard_map/all_to_all | solution.py:532
  76.1 8.8 %collective-permute-start.1 = (f32[104,128]{1,0:T(8,128)S(1)}, f32[104,128]{1,0:T(8,128)S(1)}, u32[]{:S(2)}, u32[]{:S(2)}) collective-permute-start(f32[104,128]{1,0:T(8,128)S(1)} %get-tuple-element.42), channel_id=1, source_target_pairs={{0,1},{1,2},{2,3},{3,4},{4,5},{5,6},{6,7},{7,8},{8,9},{9,10},{10,1... | collective-permute-start | bytes 159752 | tf_op jit(solution)/shard_map/ppermute | solution.py:544
